TPU v7x, 32 devices: a whole 2x2x4 slice. The times are simulated.
32 devices in a mesh: parts: 2 (over y), term: 16 (over z, x, core).
Axes of the slice: x: 2, y: 2, z: 4, core: 2. Of those that a mesh axis runs over, the one named last changes fastest.
Arguments:
- wavefunction: bfloat16 [4096, 1024], P(('parts', 'term')), parts along dimension 0, may hold values from -6 to 6
- left_ops: bfloat16 [320, 512, 512], P(('parts', 'term')), parts along dimension 0, may hold values from -0.0390625 to 0.0390625
- right_ops: bfloat16 [320, 512, 512], P(('parts', 'term')), parts along dimension 0, may hold values from -0.25 to 0.25
- src_sector: int32 [320], P(('parts', 'term')), parts along dimension 0, may hold values from 0 to 3
- dst_sector: int32 [320], P(('parts', 'term')), parts along dimension 0, may hold values from 0 to 3
- live_terms: int32 [32], P(('parts', 'term')), parts along dimension 0, may hold values from 1 to 10, 96 in all
Outputs:
- sigma_pair: float32 [4096, 1024], P(('parts', 'term')), parts along dimension 0
There are 2 independent parts, one for each index of `parts`. A program takes and returns all parts, laid end to end along the dimension named above; each array names one. Nothing has to cross between parts.
Inputs may be any that keep to these rules, and one draw needn't show every extreme that they name: Slots 0 to live_terms[g] - 1 of group g are live; the counts of one part sum to 96 and one group has all 10 live.
All inputs are finite; a program needn't handle non-finite values.
Results may differ from a plain program's by a relative error of at most 0.0029.
Values may be sent and summed in bfloat16 or wider, within the bound.
No kernel may reach another device: no remote copies, remote signals or barrier semaphores. Data moves between devices by JAX's collectives and lax.ppermute only.
A program may use at most 128 MiB of HBM per device.

v0:
```python
import functools

import jax
import jax.numpy as jnp
from jax import lax
from jax.experimental import pallas as pl
from jax.experimental.pallas import tpu as pltpu
from jax.sharding import PartitionSpec as P

F32, BF16 = jnp.float32, jnp.bfloat16
CORES = 2
TILE = 256
VMEM = 16 * 1024 * 1024
ANY = pl.BlockSpec(memory_space=pl.ANY)
SMEM = pl.BlockSpec(memory_space=pltpu.SMEM)
WHOLE = pl.BlockSpec(memory_space=pltpu.VMEM)


def list_slots(own, sib, field, sector, slots, found):
    count = jnp.int32(0)
    for core, meta in enumerate((own, sib)):
        live = meta[2 * slots]
        for t in range(slots):
            found[count] = core * slots + t
            hit = jnp.logical_and(t < live, meta[field * slots + t] == sector)
            count = count + hit.astype(jnp.int32)
    return count


def in_pairs(count, depth, fetch, wait, work):
    for i in range(depth - 2):
        @pl.when(i < count)
        def _():
            fetch(i, i)

    def pair(p, carry):
        i = 2 * p
        for ahead in (i + depth - 2, i + depth - 1):
            @pl.when(ahead < count)
            def _():
                fetch(ahead, lax.rem(ahead, depth))
        spots = [lax.rem(i, depth), lax.rem(i, depth) + 1]
        for k in spots:
            wait(k)
        work((i, i + 1), spots)
        return carry

    lax.fori_loop(0, count // 2, pair, 0)

    @pl.when(count % 2 == 1)
    def _():
        k = lax.rem(count - 1, depth)
        wait(k)
        work((count - 1,), (k,))


def start_fetch(term, slots, own_hbm, sib_hbm, target, sem):
    @pl.when(term < slots)
    def _():
        pltpu.make_async_copy(own_hbm.at[term], target, sem).start()

    @pl.when(term >= slots)
    def _():
        pltpu.make_async_copy(sib_hbm.at[term - slots], target, sem).start()


def left_kernel(phase, *refs):
    (own, sib, where, here, others, left, left_sib), refs = refs[:7], refs[7:]
    mixed, token, found, source, lbuf, obuf, lsem, osem = refs[-8:]
    token[...] = jnp.zeros_like(token)
    slots, depth, outs = left.shape[0], lbuf.shape[0], obuf.shape[0]
    half = here.shape[1]
    bands = others.shape[0] + 1
    sector, band, core = where[phase], where[where.shape[0] - 2], where[where.shape[0] - 1]
    count = list_slots(own, sib, 0, sector, slots, found)

    def fetch(i, k):
        start_fetch(found[i], slots, left, left_sib, lbuf.at[k], lsem.at[k])

    def wait(k):
        pltpu.make_async_copy(left.at[0], lbuf.at[k], lsem.at[k]).wait()

    def out_copy(i, o):
        return pltpu.make_async_copy(obuf.at[o], mixed.at[found[i]], osem.at[o])

    def work(items, spots):
        for i, k in zip(items, spots):
            o = lax.rem(i, outs)

            @pl.when(i >= outs)
            def _():
                out_copy(i - outs, o).wait()

            for n in range(0, source.shape[1], TILE):
                for m in range(0, source.shape[0], TILE):
                    obuf[o, m : m + TILE, n : n + TILE] = jnp.dot(
                        lbuf[k, m : m + TILE, :], source[:, n : n + TILE], preferred_element_type=F32
                    ).astype(BF16)
            out_copy(i, o).start()

    for j in range(bands):
        b = lax.rem(band + j, bands)
        for i in range(CORES):
            c = core if i == 0 else 1 - core
            row = pl.multiple_of((b * CORES + c) * half, half)
            source[pl.ds(row, half)] = here[i] if j == 0 else others[j - 1, i]
    in_pairs(count, depth, fetch, wait, work)
    for back in range(outs, 0, -1):
        @pl.when(count >= back)
        def _():
            out_copy(count - back, lax.rem(count - back, outs)).wait()


def right_kernel(phase, own, sib, where, mixed, right, right_sib, keep, send, found, acc, rbuf, rsem):
    slots, depth = right.shape[0], rbuf.shape[0]
    half = keep.shape[1]
    bands = send.shape[0] + 1
    sector, band, core = where[phase], where[where.shape[0] - 2], where[where.shape[0] - 1]
    count = list_slots(own, sib, 1, sector, slots, found)

    def fetch(i, k):
        start_fetch(found[i], slots, right, right_sib, rbuf.at[k], rsem.at[k])

    def wait(k):
        pltpu.make_async_copy(right.at[0], rbuf.at[k], rsem.at[k]).wait()

    def work(items, spots):
        for n in range(0, acc.shape[1], TILE):
            acc[:, n : n + TILE] += sum(
                lax.dot_general(
                    mixed[found[i]], rbuf[k, n : n + TILE, :], (((1,), (1,)), ((), ())), preferred_element_type=F32
                )
                for i, k in zip(items, spots)
            )

    acc[...] = jnp.zeros_like(acc)
    in_pairs(count, depth, fetch, wait, work)
    for j in range(bands):
        b = lax.rem(band + j, bands)
        for i in range(CORES):
            c = core if i == 0 else 1 - core
            rows = acc[pl.ds(pl.multiple_of((b * CORES + c) * half, half), half)]
            if j == 0:
                keep[i] = rows
            else:
                send[j - 1, i] = rows.astype(BF16)


def local(devices, wavefunction, left, right, src, dst, live):
    slots, width = left.shape[0], left.shape[1]
    half = wavefunction.shape[0]
    sectors = half * devices // width
    bands = devices // (sectors * CORES)
    assert sectors == 4
    me = lax.axis_index("term")
    core, band, plane = me % CORES, (me // CORES) % bands, me // (CORES * bands)

    def move(value, to_plane=lambda a: a, band_step=0, flip=False):
        pairs = []
        for i in range(devices):
            c, b, a = i % CORES, (i // CORES) % bands, i // (CORES * bands)
            c = 1 - c if flip else c
            pairs.append((i, (to_plane(a) * bands + (b + band_step) % bands) * CORES + c))
        return lax.ppermute(value, "term", pairs)

    def beside(a):
        return a ^ 1

    def mirror(a):
        return 3 - a

    def bands_of(block):
        return jnp.stack([move(block, band_step=-j) for j in range(1, bands)])

    own_meta = jnp.concatenate([src, dst, live])
    sib_meta = move(own_meta, flip=True)
    mine = lax.dynamic_slice_in_dim(wavefunction, core * width, width, 1)
    theirs = lax.dynamic_slice_in_dim(wavefunction, (1 - core) * width, width, 1)
    from_sib = move(theirs, flip=True)
    left_sib, from_sib, sib_meta = lax.optimization_barrier((left, from_sib, sib_meta))
    left_sib = move(left_sib, flip=True)
    own_block = jnp.stack([mine, from_sib])
    mirror_block = move(own_block, mirror)
    beside_block, own_bands = lax.optimization_barrier((move(own_block, beside), bands_of(own_block)))
    beside_bands = bands_of(beside_block)
    blocks = [(own_block, own_bands), None, None, None]
    partner = plane ^ 1
    where_src = jnp.stack([plane, partner, 3 - plane, 3 - partner, band, core]).astype(jnp.int32)
    where_dst = jnp.stack([3 - partner, 3 - plane, partner, plane, band, core]).astype(jnp.int32)

    params = pltpu.CompilerParams(vmem_limit_bytes=VMEM)
    left_cost = pl.CostEstimate(flops=10**6, bytes_accessed=width, transcendentals=0)
    cost = pl.CostEstimate(flops=3 * 10**9, bytes_accessed=7 * width * width * 2, transcendentals=0)
    depth = 8
    mixed = None
    for phase in range(sectors):
        if phase == 1:
            mirror_block, right_sib, beside_bands, token = lax.optimization_barrier(
                (mirror_block, right, beside_bands, token)
            )
            right_sib = move(right_sib, flip=True)
            blocks[1] = (beside_block, beside_bands)
            blocks[2] = (mirror_block, bands_of(mirror_block))
            far_block = move(mirror_block, beside)
        if phase == 2:
            far_block, token = lax.optimization_barrier((far_block, token))
            blocks[3] = (far_block, bands_of(far_block))
        operands = [own_meta, sib_meta, where_src, *blocks[phase], left, left_sib]
        if mixed is not None:
            operands += [mixed, token]
        mixed, token = pl.pallas_call(
            functools.partial(left_kernel, phase),
            out_shape=(
                jax.ShapeDtypeStruct((CORES * slots, width, width), BF16),
                jax.ShapeDtypeStruct((8, 128), F32),
            ),
            in_specs=[SMEM] * 3 + [WHOLE] * 2 + [ANY] * (len(operands) - 5),
            out_specs=(ANY, WHOLE),
            scratch_shapes=[
                pltpu.SMEM((CORES * slots + 1,), jnp.int32),
                pltpu.VMEM((width, width), BF16),
                pltpu.VMEM((depth, width, width), BF16),
                pltpu.VMEM((4, width, width), BF16),
                pltpu.SemaphoreType.DMA((depth,)),
                pltpu.SemaphoreType.DMA((4,)),
            ],
            input_output_aliases={} if mixed is None else {7: 0},
            compiler_params=params,
            cost_estimate=left_cost,
            name="left_mix",
        )(*operands)

    def right_mix(phase, meta):
        keep, send = pl.pallas_call(
            functools.partial(right_kernel, phase),
            out_shape=(
                jax.ShapeDtypeStruct((CORES, half, width), F32),
                jax.ShapeDtypeStruct((bands - 1, CORES, half, width), BF16),
            ),
            in_specs=[SMEM] * 3 + [WHOLE] + [ANY] * 2,
            out_specs=(WHOLE, WHOLE),
            scratch_shapes=[
                pltpu.SMEM((CORES * slots + 1,), jnp.int32),
                pltpu.VMEM((width, width), F32),
                pltpu.VMEM((depth, width, width), BF16),
                pltpu.SemaphoreType.DMA((depth,)),
            ],
            compiler_params=params,
            cost_estimate=cost,
            name="right_mix",
        )(meta, sib_meta, where_dst, mixed, right, right_sib)
        for j in range(1, bands):
            keep = keep + move(send[j - 1], band_step=j).astype(F32)
        return keep

    beside_far = right_mix(0, own_meta).astype(BF16)
    mirrored = right_mix(1, own_meta)
    meta, beside_far = lax.optimization_barrier((own_meta, beside_far))
    mirrored = (mirrored + move(beside_far, beside).astype(F32)).astype(BF16)
    beside_near = right_mix(2, meta).astype(BF16)
    total = right_mix(3, meta) + move(mirrored, mirror).astype(F32) + move(beside_near, beside).astype(F32)
    same, cross = total[0], move(total[1], flip=True)
    first = core == 0
    return jnp.concatenate([jnp.where(first, same, cross), jnp.where(first, cross, same)], axis=1)


def solution(mesh):
    spec = P(("parts", "term"))
    return jax.shard_map(
        functools.partial(local, mesh.shape["term"]),
        mesh=mesh,
        in_specs=(spec,) * 6,
        out_specs=spec,
        check_vma=False,
    )
```

profile of v0, /device:TPU:0, one launch (start us, length us, event | category | flops | bytes accessed | tf_op | source)
XLA Modules:
  0.0 99.3 jit_solution(15429761311661787624)
XLA Ops:
  0.0 1.0 dynamic-slice_bitcast_fusion
  1.0 0.5 collective-permute-start
  2.2 0.7 pad_add_fusion.refs_0_.own
  2.9 0.1 collective-permute-start.1
  3.0 1.1 %collective-permute-done.1.refs_1_.sib = s32[21]{0:T(128)S(1)} collective-permute-done((s32[21]{0:T(128)S(1)}, s32[21]{0:T(128)S(1)}, u32[]{:S(2)}, u32[]{:S(2)}) %collective-permute-start.1) | collective-permute-done | bytes 116 | tf_op jit(solution)/shard_map/ppermute | solution.py:164
  4.0 0.0 collective-permute-done
  4.0 0.2 collective-permute-start.6
  4.3 2.9 %collective-permute-start.4 = (bf16[2,128,512]{2,1,0:T(8,128)(2,1)S(1)}, bf16[2,128,512]{2,1,0:T(8,128)(2,1)S(1)}, u32[]{:S(2)}, u32[]{:S(2)}) collective-permute-start(bf16[2,128,512]{2,1,0:T(8,128)(2,1)S(1)} %pad_maximum_fusion.1.refs_3_), channel_id=1, source_target_pairs={{0,2},{1,3},{2,0},{3,1},{4,6},{5,7},{6,4},{7,5},{8,10},{9,11},{10,... | collective-permute-start | bytes 786440 | tf_op jit(solution)/shard_map/ppermute | solution.py:164
  7.1 1.6 %collective-permute-start.3 = (bf16[2,128,512]{2,1,0:T(8,128)(2,1)S(1)}, bf16[2,128,512]{2,1,0:T(8,128)(2,1)S(1)}, u32[]{:S(2)}, u32[]{:S(2)}) collective-permute-start(bf16[2,128,512]{2,1,0:T(8,128)(2,1)S(1)} %pad_maximum_fusion.1.refs_3_), channel_id=1, source_target_pairs={{0,4},{1,5},{2,6},{3,7},{4,0},{5,1},{6,2},{7,3},{8,12},{9,13},{10,... | collective-permute-start | bytes 786440 | tf_op jit(solution)/shard_map/ppermute | solution.py:164
  8.7 2.5 %collective-permute-start.2 = (bf16[2,128,512]{2,1,0:T(8,128)(2,1)S(1)}, bf16[2,128,512]{2,1,0:T(8,128)(2,1)S(1)}, u32[]{:S(2)}, u32[]{:S(2)}) collective-permute-start(bf16[2,128,512]{2,1,0:T(8,128)(2,1)S(1)} %pad_maximum_fusion.1.refs_3_), channel_id=1, source_target_pairs={{0,12},{1,13},{2,14},{3,15},{4,8},{5,9},{6,10},{7,11},{8,4},{9,5},... | collective-permute-start | bytes 786440 | tf_op jit(solution)/shard_map/ppermute | solution.py:164
  11.2 2.6 %collective-permute-done.4 = bf16[2,128,512]{2,1,0:T(8,128)(2,1)S(1)} collective-permute-done((bf16[2,128,512]{2,1,0:T(8,128)(2,1)S(1)}, bf16[2,128,512]{2,1,0:T(8,128)(2,1)S(1)}, u32[]{:S(2)}, u32[]{:S(2)}) %collective-permute-start.4) | collective-permute-done | bytes 262176 | tf_op jit(solution)/shard_map/ppermute | solution.py:164
  13.8 1.6 %collective-permute-done.3.refs_3_ = bf16[2,128,512]{2,1,0:T(8,128)(2,1)S(1)} collective-permute-done((bf16[2,128,512]{2,1,0:T(8,128)(2,1)S(1)}, bf16[2,128,512]{2,1,0:T(8,128)(2,1)S(1)}, u32[]{:S(2)}, u32[]{:S(2)}) %collective-permute-start.3) | collective-permute-done | bytes 262176 | tf_op jit(solution)/shard_map/ppermute | solution.py:164
  15.4 0.5 collective-permute-start.5
  15.9 0.1 stack.58.refs_2_
  16.0 0.0 collective-permute-done.6.refs_6_
  16.0 0.0 copy-start.4
  16.0 2.5 %copy-done.4 = bf16[10,512,512]{2,1,0:T(8,128)(2,1)S(1)} copy-done((bf16[10,512,512]{2,1,0:T(8,128)(2,1)S(1)}, bf16[10,512,512]{2,1,0:T(8,128)(2,1)}, u32[]{:S(2)}) %copy-start.4) | copy-done | bytes 5242904
  18.5 2.9 %left_mix.4 = (bf16[20,512,512]{2,1,0:T(8,128)(2,1)S(1)}, f32[8,128]{1,0:T(8,128)S(1)}) custom-call(s32[21]{0:T(128)S(1)} %pad_add_fusion.refs_0_.own, s32[21]{0:T(128)S(1)} %collective-permute-done.1.refs_1_.sib, s32[6]{0:T(128)S(1)} %stack.58.refs_2_, bf16[2,128,512]{2,1,0:T(8,128)(2,1)S(1)} %pad_maximum_fusion.1.refs_3_, ...), custom_call_target="tpu_custom_call" | custom-call | flops 1000000 | bytes 512 | tf_op jit(solution)/shard_map/left_mix/pallas_call | solution.py:211
  21.5 1.6 %collective-permute-done.2.refs_3_ = bf16[2,128,512]{2,1,0:T(8,128)(2,1)S(1)} collective-permute-done((bf16[2,128,512]{2,1,0:T(8,128)(2,1)S(1)}, bf16[2,128,512]{2,1,0:T(8,128)(2,1)S(1)}, u32[]{:S(2)}, u32[]{:S(2)}) %collective-permute-start.2) | collective-permute-done | bytes 262176 | tf_op jit(solution)/shard_map/ppermute | solution.py:164
  23.0 0.0 collective-permute-done.5
  23.0 0.0 collective-permute-start.10
  23.0 1.2 %collective-permute-start.7 = (bf16[2,128,512]{2,1,0:T(8,128)(2,1)S(1)}, bf16[2,128,512]{2,1,0:T(8,128)(2,1)S(1)}, u32[]{:S(2)}, u32[]{:S(2)}) collective-permute-start(bf16[2,128,512]{2,1,0:T(8,128)(2,1)S(1)} %collective-permute-done.2.refs_3_), channel_id=1, source_target_pairs={{0,4},{1,5},{2,6},{3,7},{4,0},{5,1},{6,2},{7,3},{8,12},{9,13},{10,... | collective-permute-start | bytes 786440 | tf_op jit(solution)/shard_map/ppermute | solution.py:164
  24.3 0.7 collective-permute-start.9
  25.0 2.4 %left_mix.5 = (bf16[20,512,512]{2,1,0:T(8,128)(2,1)S(1)}, f32[8,128]{1,0:T(8,128)S(1)}) custom-call(s32[21]{0:T(128)S(1)} %pad_add_fusion.refs_0_.own, s32[21]{0:T(128)S(1)} %collective-permute-done.1.refs_1_.sib, s32[6]{0:T(128)S(1)} %stack.58.refs_2_, bf16[2,128,512]{2,1,0:T(8,128)(2,1)S(1)} %collective-permute-done.3.refs_3_, ...), custom_call_target="tpu_custom_call", output_to_operand_aliasing={{0}: (7, {})} | custom-call | flops 1000000 | bytes 512 | tf_op jit(solution)/shard_map/left_mix/pallas_call | solution.py:211
  27.3 0.0 copy-start
  27.4 4.0 %copy-done = bf16[20,512,512]{2,1,0:T(8,128)(2,1)} copy-done((bf16[20,512,512]{2,1,0:T(8,128)(2,1)}, bf16[20,512,512]{2,1,0:T(8,128)(2,1)S(1)}, u32[]{:S(2)}) %copy-start) | copy-done | bytes 10485784
  31.4 0.4 collective-permute-done.7.refs_3_
  31.7 3.5 %collective-permute-start.8 = (bf16[2,128,512]{2,1,0:T(8,128)(2,1)S(1)}, bf16[2,128,512]{2,1,0:T(8,128)(2,1)S(1)}, u32[]{:S(2)}, u32[]{:S(2)}) collective-permute-start(bf16[2,128,512]{2,1,0:T(8,128)(2,1)S(1)} %collective-permute-done.7.refs_3_), channel_id=1, source_target_pairs={{0,2},{1,3},{2,0},{3,1},{4,6},{5,7},{6,4},{7,5},{8,10},{9,11},{10,... | collective-permute-start | bytes 786440 | tf_op jit(solution)/shard_map/ppermute | solution.py:164
  35.2 0.1 stack.57.where
  35.3 0.0 collective-permute-done.9
  35.3 4.0 %copy-done.1 = bf16[20,512,512]{2,1,0:T(8,128)(2,1)S(1)} copy-done((bf16[20,512,512]{2,1,0:T(8,128)(2,1)S(1)}, bf16[20,512,512]{2,1,0:T(8,128)(2,1)}, u32[]{:S(2)}) %copy-start.1) | copy-done | bytes 10485784
  39.3 2.5 %copy-done.5 = bf16[10,512,512]{2,1,0:T(8,128)(2,1)S(1)} copy-done((bf16[10,512,512]{2,1,0:T(8,128)(2,1)S(1)}, bf16[10,512,512]{2,1,0:T(8,128)(2,1)}, u32[]{:S(2)}) %copy-start.5) | copy-done | bytes 5242904
  41.8 0.8 left_mix.6
  42.6 0.0 collective-permute-done.8
  42.6 4.0 %left_mix.7 = (bf16[20,512,512]{2,1,0:T(8,128)(2,1)S(1)}, f32[8,128]{1,0:T(8,128)}) custom-call(s32[21]{0:T(128)S(1)} %pad_add_fusion.refs_0_.own, s32[21]{0:T(128)S(1)} %collective-permute-done.1.refs_1_.sib, s32[6]{0:T(128)S(1)} %stack.58.refs_2_, bf16[2,128,512]{2,1,0:T(8,128)(2,1)S(1)} %collective-permute-done.7.refs_3_, ...), custom_call_target="tpu_custom_call", output_to_operand_aliasing={{0}: (7, {})} | custom-call | flops 1000000 | bytes 512 | tf_op jit(solution)/shard_map/left_mix/pallas_call | solution.py:211
  46.6 0.0 copy-start.2
  46.6 4.0 %copy-done.2 = bf16[20,512,512]{2,1,0:T(8,128)(2,1)} copy-done((bf16[20,512,512]{2,1,0:T(8,128)(2,1)}, bf16[20,512,512]{2,1,0:T(8,128)(2,1)S(1)}, u32[]{:S(2)}) %copy-start.2) | copy-done | bytes 10485784
  50.6 0.0 collective-permute-done.10.right_sib
  50.6 4.0 %copy-done.3 = bf16[20,512,512]{2,1,0:T(8,128)(2,1)S(1)} copy-done((bf16[20,512,512]{2,1,0:T(8,128)(2,1)S(1)}, bf16[20,512,512]{2,1,0:T(8,128)(2,1)}, u32[]{:S(2)}) %copy-start.3) | copy-done | bytes 10485784
  54.6 3.2 %right_mix.4 = (f32[2,128,512]{2,1,0:T(8,128)S(1)}, bf16[1,2,128,512]{3,2,1,0:T(8,128)(2,1)S(1)}) custom-call(s32[21]{0:T(128)S(1)} %pad_add_fusion.refs_0_.own, s32[21]{0:T(128)S(1)} %collective-permute-done.1.refs_1_.sib, s32[6]{0:T(128)S(1)} %stack.57.where, bf16[20,512,512]{2,1,0:T(8,128)(2,1)S(1)} %copy-done.3, bf16[10,512,512]{2,1,0:T(8,128)(2,1)} %right.7, ...), custom_call_target="tpu_custom_call" | custom-call | flops 3000000000 | bytes 3670016 | tf_op jit(solution)/shard_map/right_mix/pallas_call | solution.py:234
  57.7 0.5 collective-permute-start.11
  58.2 3.2 %right_mix.6 = (f32[2,128,512]{2,1,0:T(8,128)S(1)}, bf16[1,2,128,512]{3,2,1,0:T(8,128)(2,1)S(1)}) custom-call(s32[21]{0:T(128)S(1)} %pad_add_fusion.refs_0_.own, s32[21]{0:T(128)S(1)} %collective-permute-done.1.refs_1_.sib, s32[6]{0:T(128)S(1)} %stack.57.where, bf16[20,512,512]{2,1,0:T(8,128)(2,1)S(1)} %copy-done.3, bf16[10,512,512]{2,1,0:T(8,128)(2,1)} %right.7, ...), custom_call_target="tpu_custom_call" | custom-call | flops 3000000000 | bytes 3670016 | tf_op jit(solution)/shard_map/right_mix/pallas_call | solution.py:234
  61.4 1.2 %collective-permute-start.13 = (bf16[2,128,512]{2,1,0:T(8,128)(2,1)S(1)}, bf16[2,128,512]{2,1,0:T(8,128)(2,1)S(1)}, u32[]{:S(2)}, u32[]{:S(2)}) collective-permute-start(bf16[2,128,512]{2,1,0:T(8,128)(2,1)S(1)} %bitcast.30), channel_id=1, source_target_pairs={{0,2},{1,3},{2,0},{3,1},{4,6},{5,7},{6,4},{7,5},{8,10},{9,11},{10,... | collective-permute-start | bytes 786440 | tf_op jit(solution)/shard_map/ppermute | solution.py:164
  62.6 4.5 %collective-permute-done.11 = bf16[2,128,512]{2,1,0:T(8,128)(2,1)S(1)} collective-permute-done((bf16[2,128,512]{2,1,0:T(8,128)(2,1)S(1)}, bf16[2,128,512]{2,1,0:T(8,128)(2,1)S(1)}, u32[]{:S(2)}, u32[]{:S(2)}) %collective-permute-start.11) | collective-permute-done | bytes 262176 | tf_op jit(solution)/shard_map/ppermute | solution.py:164
  67.0 0.1 add_convert_fusion.2
  67.1 2.6 %collective-permute-start.14 = (bf16[2,128,512]{2,1,0:T(8,128)(2,1)S(1)}, bf16[2,128,512]{2,1,0:T(8,128)(2,1)S(1)}, u32[]{:S(2)}, u32[]{:S(2)}) collective-permute-start(bf16[2,128,512]{2,1,0:T(8,128)(2,1)S(1)} %add_convert_fusion.2), channel_id=1, source_target_pairs={{0,4},{1,5},{2,6},{3,7},{4,0},{5,1},{6,2},{7,3},{8,12},{9,13},{10,... | collective-permute-start | bytes 786440 | tf_op jit(solution)/shard_map/ppermute | solution.py:164
  69.8 3.2 %right_mix.7 = (f32[2,128,512]{2,1,0:T(8,128)S(1)}, bf16[1,2,128,512]{3,2,1,0:T(8,128)(2,1)S(1)}) custom-call(s32[21]{0:T(128)S(1)} %pad_add_fusion.refs_0_.own, s32[21]{0:T(128)S(1)} %collective-permute-done.1.refs_1_.sib, s32[6]{0:T(128)S(1)} %stack.57.where, bf16[20,512,512]{2,1,0:T(8,128)(2,1)S(1)} %copy-done.3, bf16[10,512,512]{2,1,0:T(8,128)(2,1)} %right.7, ...), custom_call_target="tpu_custom_call" | custom-call | flops 3000000000 | bytes 3670016 | tf_op jit(solution)/shard_map/right_mix/pallas_call | solution.py:234
  72.9 2.0 %collective-permute-start.16 = (bf16[2,128,512]{2,1,0:T(8,128)(2,1)S(1)}, bf16[2,128,512]{2,1,0:T(8,128)(2,1)S(1)}, u32[]{:S(2)}, u32[]{:S(2)}) collective-permute-start(bf16[2,128,512]{2,1,0:T(8,128)(2,1)S(1)} %bitcast.31), channel_id=1, source_target_pairs={{0,2},{1,3},{2,0},{3,1},{4,6},{5,7},{6,4},{7,5},{8,10},{9,11},{10,... | collective-permute-start | bytes 786440 | tf_op jit(solution)/shard_map/ppermute | solution.py:164
  74.9 2.3 %right_mix.5 = (f32[2,128,512]{2,1,0:T(8,128)S(1)}, bf16[1,2,128,512]{3,2,1,0:T(8,128)(2,1)S(1)}) custom-call(s32[21]{0:T(128)S(1)} %pad_add_fusion.refs_0_.own, s32[21]{0:T(128)S(1)} %collective-permute-done.1.refs_1_.sib, s32[6]{0:T(128)S(1)} %stack.57.where, bf16[20,512,512]{2,1,0:T(8,128)(2,1)S(1)} %copy-done.3, bf16[10,512,512]{2,1,0:T(8,128)(2,1)} %right.7, ...), custom_call_target="tpu_custom_call" | custom-call | flops 3000000000 | bytes 3670016 | tf_op jit(solution)/shard_map/right_mix/pallas_call | solution.py:234
  77.2 1.8 %collective-permute-start.12 = (bf16[2,128,512]{2,1,0:T(8,128)(2,1)S(1)}, bf16[2,128,512]{2,1,0:T(8,128)(2,1)S(1)}, u32[]{:S(2)}, u32[]{:S(2)}) collective-permute-start(bf16[2,128,512]{2,1,0:T(8,128)(2,1)S(1)} %bitcast.29), channel_id=1, source_target_pairs={{0,2},{1,3},{2,0},{3,1},{4,6},{5,7},{6,4},{7,5},{8,10},{9,11},{10,... | collective-permute-start | bytes 786440 | tf_op jit(solution)/shard_map/ppermute | solution.py:164
  79.0 0.0 collective-permute-done.13
  79.0 0.0 collective-permute-done.14
  79.0 0.1 add_convert_fusion.1
  79.1 9.3 %collective-permute-start.15 = (bf16[2,128,512]{2,1,0:T(8,128)(2,1)S(1)}, bf16[2,128,512]{2,1,0:T(8,128)(2,1)S(1)}, u32[]{:S(2)}, u32[]{:S(2)}) collective-permute-start(bf16[2,128,512]{2,1,0:T(8,128)(2,1)S(1)} %add_convert_fusion.1), channel_id=1, source_target_pairs={{0,12},{1,13},{2,14},{3,15},{4,8},{5,9},{6,10},{7,11},{8,4},{9,5},... | collective-permute-start | bytes 786440 | tf_op jit(solution)/shard_map/ppermute | solution.py:164
  88.4 0.0 collective-permute-done.16
  88.4 0.1 add_convert_fusion
  88.4 0.1 collective-permute-start.17
  88.5 0.0 collective-permute-done.12
  88.5 5.4 %collective-permute-done.15 = bf16[2,128,512]{2,1,0:T(8,128)(2,1)S(1)} collective-permute-done((bf16[2,128,512]{2,1,0:T(8,128)(2,1)S(1)}, bf16[2,128,512]{2,1,0:T(8,128)(2,1)S(1)}, u32[]{:S(2)}, u32[]{:S(2)}) %collective-permute-start.15) | collective-permute-done | bytes 262176 | tf_op jit(solution)/shard_map/ppermute | solution.py:164
  93.9 2.7 %collective-permute-done.17 = bf16[2,128,512]{2,1,0:T(8,128)(2,1)S(1)} collective-permute-done((bf16[2,128,512]{2,1,0:T(8,128)(2,1)S(1)}, bf16[2,128,512]{2,1,0:T(8,128)(2,1)S(1)}, u32[]{:S(2)}, u32[]{:S(2)}) %collective-permute-start.17) | collective-permute-done | bytes 262176 | tf_op jit(solution)/shard_map/ppermute | solution.py:164
  96.7 0.1 convert_add_fusion
  96.8 0.1 collective-permute-start.18
  96.9 1.5 %collective-permute-done.18 = f32[128,512]{1,0:T(8,128)S(1)} collective-permute-done((f32[128,512]{1,0:T(8,128)S(1)}, f32[128,512]{1,0:T(8,128)S(1)}, u32[]{:S(2)}, u32[]{:S(2)}) %collective-permute-start.18) | collective-permute-done | bytes 262176 | tf_op jit(solution)/shard_map/ppermute | solution.py:164
  98.5 0.8 pad_maximum_fusion
  (6 shorter events, 0.1 us)
Async XLA Ops:
  1.0 3.0 %collective-permute-start = (bf16[128,512]{1,0:T(8,128)(2,1)S(1)}, bf16[128,512]{1,0:T(8,128)(2,1)S(1)}, u32[]{:S(2)}, u32[]{:S(2)}) collective-permute-start(bf16[128,512]{1,0:T(8,128)(2,1)S(1)} %get-tuple-element.64), channel_id=1, source_target_pairs={{0,1},{1,0},{2,3},{3,2},{4,5},{5,4},{6,7},{7,6},{8,9},{9,8},{10,11... | collective-permute-start | bytes 393224 | tf_op jit(solution)/shard_map/ppermute | solution.py:164
  2.9 1.1 %collective-permute-start.1 = (s32[21]{0:T(128)S(1)}, s32[21]{0:T(128)S(1)}, u32[]{:S(2)}, u32[]{:S(2)}) collective-permute-start(s32[21]{0:T(128)S(1)} %pad_add_fusion.refs_0_.own), channel_id=1, source_target_pairs={{0,1},{1,0},{2,3},{3,2},{4,5},{5,4},{6,7},{7,6},{8,9},{9,8},{10,11... | collective-permute-start | bytes 260 | tf_op jit(solution)/shard_map/ppermute | solution.py:164
  4.0 12.0 %collective-permute-start.6 = (bf16[10,512,512]{2,1,0:T(8,128)(2,1)}, bf16[10,512,512]{2,1,0:T(8,128)(2,1)}, u32[]{:S(2)}, u32[]{:S(2)}) collective-permute-start(bf16[10,512,512]{2,1,0:T(8,128)(2,1)} %refs_5_.7), channel_id=1, source_target_pairs={{0,1},{1,0},{2,3},{3,2},{4,5},{5,4},{6,7},{7,6},{8,9},{9,8},{10,11... | collective-permute-start | bytes 15728648 | tf_op jit(solution)/shard_map/ppermute | solution.py:164
  4.3 9.5 %collective-permute-start.4 = (bf16[2,128,512]{2,1,0:T(8,128)(2,1)S(1)}, bf16[2,128,512]{2,1,0:T(8,128)(2,1)S(1)}, u32[]{:S(2)}, u32[]{:S(2)}) collective-permute-start(bf16[2,128,512]{2,1,0:T(8,128)(2,1)S(1)} %pad_maximum_fusion.1.refs_3_), channel_id=1, source_target_pairs={{0,2},{1,3},{2,0},{3,1},{4,6},{5,7},{6,4},{7,5},{8,10},{9,11},{10,... | collective-permute-start | bytes 786440 | tf_op jit(solution)/shard_map/ppermute | solution.py:164
  7.1 8.3 %collective-permute-start.3 = (bf16[2,128,512]{2,1,0:T(8,128)(2,1)S(1)}, bf16[2,128,512]{2,1,0:T(8,128)(2,1)S(1)}, u32[]{:S(2)}, u32[]{:S(2)}) collective-permute-start(bf16[2,128,512]{2,1,0:T(8,128)(2,1)S(1)} %pad_maximum_fusion.1.refs_3_), channel_id=1, source_target_pairs={{0,4},{1,5},{2,6},{3,7},{4,0},{5,1},{6,2},{7,3},{8,12},{9,13},{10,... | collective-permute-start | bytes 786440 | tf_op jit(solution)/shard_map/ppermute | solution.py:164
  8.7 14.3 %collective-permute-start.2 = (bf16[2,128,512]{2,1,0:T(8,128)(2,1)S(1)}, bf16[2,128,512]{2,1,0:T(8,128)(2,1)S(1)}, u32[]{:S(2)}, u32[]{:S(2)}) collective-permute-start(bf16[2,128,512]{2,1,0:T(8,128)(2,1)S(1)} %pad_maximum_fusion.1.refs_3_), channel_id=1, source_target_pairs={{0,12},{1,13},{2,14},{3,15},{4,8},{5,9},{6,10},{7,11},{8,4},{9,5},... | collective-permute-start | bytes 786440 | tf_op jit(solution)/shard_map/ppermute | solution.py:164
  15.4 7.6 %collective-permute-start.5 = (bf16[2,128,512]{2,1,0:T(8,128)(2,1)S(1)}, bf16[2,128,512]{2,1,0:T(8,128)(2,1)S(1)}, u32[]{:S(2)}, u32[]{:S(2)}) collective-permute-start(bf16[2,128,512]{2,1,0:T(8,128)(2,1)S(1)} %collective-permute-done.3.refs_3_), channel_id=1, source_target_pairs={{0,2},{1,3},{2,0},{3,1},{4,6},{5,7},{6,4},{7,5},{8,10},{9,11},{10,... | collective-permute-start | bytes 786440 | tf_op jit(solution)/shard_map/ppermute | solution.py:164
  16.0 2.5 %copy-start.4 = (bf16[10,512,512]{2,1,0:T(8,128)(2,1)S(1)}, bf16[10,512,512]{2,1,0:T(8,128)(2,1)}, u32[]{:S(2)}) copy-start(bf16[10,512,512]{2,1,0:T(8,128)(2,1)} %refs_5_.7) | copy-start | bytes 15728644
  23.0 27.6 %collective-permute-start.10 = (bf16[10,512,512]{2,1,0:T(8,128)(2,1)}, bf16[10,512,512]{2,1,0:T(8,128)(2,1)}, u32[]{:S(2)}, u32[]{:S(2)}) collective-permute-start(bf16[10,512,512]{2,1,0:T(8,128)(2,1)} %right.7), channel_id=1, source_target_pairs={{0,1},{1,0},{2,3},{3,2},{4,5},{5,4},{6,7},{7,6},{8,9},{9,8},{10,11... | collective-permute-start | bytes 15728648 | tf_op jit(solution)/shard_map/ppermute | solution.py:164
  23.0 8.7 %collective-permute-start.7 = (bf16[2,128,512]{2,1,0:T(8,128)(2,1)S(1)}, bf16[2,128,512]{2,1,0:T(8,128)(2,1)S(1)}, u32[]{:S(2)}, u32[]{:S(2)}) collective-permute-start(bf16[2,128,512]{2,1,0:T(8,128)(2,1)S(1)} %collective-permute-done.2.refs_3_), channel_id=1, source_target_pairs={{0,4},{1,5},{2,6},{3,7},{4,0},{5,1},{6,2},{7,3},{8,12},{9,13},{10,... | collective-permute-start | bytes 786440 | tf_op jit(solution)/shard_map/ppermute | solution.py:164
  24.3 11.0 %collective-permute-start.9 = (bf16[2,128,512]{2,1,0:T(8,128)(2,1)S(1)}, bf16[2,128,512]{2,1,0:T(8,128)(2,1)S(1)}, u32[]{:S(2)}, u32[]{:S(2)}) collective-permute-start(bf16[2,128,512]{2,1,0:T(8,128)(2,1)S(1)} %collective-permute-done.2.refs_3_), channel_id=1, source_target_pairs={{0,2},{1,3},{2,0},{3,1},{4,6},{5,7},{6,4},{7,5},{8,10},{9,11},{10,... | collective-permute-start | bytes 786440 | tf_op jit(solution)/shard_map/ppermute | solution.py:164
  27.3 4.0 %copy-start = (bf16[20,512,512]{2,1,0:T(8,128)(2,1)}, bf16[20,512,512]{2,1,0:T(8,128)(2,1)S(1)}, u32[]{:S(2)}) copy-start(bf16[20,512,512]{2,1,0:T(8,128)(2,1)S(1)} %get-tuple-element.45.refs_7_) | copy-start | bytes 31457284
  31.7 10.8 %collective-permute-start.8 = (bf16[2,128,512]{2,1,0:T(8,128)(2,1)S(1)}, bf16[2,128,512]{2,1,0:T(8,128)(2,1)S(1)}, u32[]{:S(2)}, u32[]{:S(2)}) collective-permute-start(bf16[2,128,512]{2,1,0:T(8,128)(2,1)S(1)} %collective-permute-done.7.refs_3_), channel_id=1, source_target_pairs={{0,2},{1,3},{2,0},{3,1},{4,6},{5,7},{6,4},{7,5},{8,10},{9,11},{10,... | collective-permute-start | bytes 786440 | tf_op jit(solution)/shard_map/ppermute | solution.py:164
  35.3 4.0 %copy-start.1 = (bf16[20,512,512]{2,1,0:T(8,128)(2,1)S(1)}, bf16[20,512,512]{2,1,0:T(8,128)(2,1)}, u32[]{:S(2)}) copy-start(bf16[20,512,512]{2,1,0:T(8,128)(2,1)} %copy-done) | copy-start | bytes 31457284
  39.3 2.5 %copy-start.5 = (bf16[10,512,512]{2,1,0:T(8,128)(2,1)S(1)}, bf16[10,512,512]{2,1,0:T(8,128)(2,1)}, u32[]{:S(2)}) copy-start(bf16[10,512,512]{2,1,0:T(8,128)(2,1)} %refs_5_.7) | copy-start | bytes 15728644
  46.6 4.0 %copy-start.2 = (bf16[20,512,512]{2,1,0:T(8,128)(2,1)}, bf16[20,512,512]{2,1,0:T(8,128)(2,1)S(1)}, u32[]{:S(2)}) copy-start(bf16[20,512,512]{2,1,0:T(8,128)(2,1)S(1)} %get-tuple-element.49.mixed) | copy-start | bytes 31457284
  50.6 4.0 %copy-start.3 = (bf16[20,512,512]{2,1,0:T(8,128)(2,1)S(1)}, bf16[20,512,512]{2,1,0:T(8,128)(2,1)}, u32[]{:S(2)}) copy-start(bf16[20,512,512]{2,1,0:T(8,128)(2,1)} %copy-done.2) | copy-start | bytes 31457284
  57.7 9.3 %collective-permute-start.11 = (bf16[2,128,512]{2,1,0:T(8,128)(2,1)S(1)}, bf16[2,128,512]{2,1,0:T(8,128)(2,1)S(1)}, u32[]{:S(2)}, u32[]{:S(2)}) collective-permute-start(bf16[2,128,512]{2,1,0:T(8,128)(2,1)S(1)} %bitcast.32), channel_id=1, source_target_pairs={{0,2},{1,3},{2,0},{3,1},{4,6},{5,7},{6,4},{7,5},{8,10},{9,11},{10,... | collective-permute-start | bytes 786440 | tf_op jit(solution)/shard_map/ppermute | solution.py:164
  61.4 17.6 %collective-permute-start.13 = (bf16[2,128,512]{2,1,0:T(8,128)(2,1)S(1)}, bf16[2,128,512]{2,1,0:T(8,128)(2,1)S(1)}, u32[]{:S(2)}, u32[]{:S(2)}) collective-permute-start(bf16[2,128,512]{2,1,0:T(8,128)(2,1)S(1)} %bitcast.30), channel_id=1, source_target_pairs={{0,2},{1,3},{2,0},{3,1},{4,6},{5,7},{6,4},{7,5},{8,10},{9,11},{10,... | collective-permute-start | bytes 786440 | tf_op jit(solution)/shard_map/ppermute | solution.py:164
  67.1 11.9 %collective-permute-start.14 = (bf16[2,128,512]{2,1,0:T(8,128)(2,1)S(1)}, bf16[2,128,512]{2,1,0:T(8,128)(2,1)S(1)}, u32[]{:S(2)}, u32[]{:S(2)}) collective-permute-start(bf16[2,128,512]{2,1,0:T(8,128)(2,1)S(1)} %add_convert_fusion.2), channel_id=1, source_target_pairs={{0,4},{1,5},{2,6},{3,7},{4,0},{5,1},{6,2},{7,3},{8,12},{9,13},{10,... | collective-permute-start | bytes 786440 | tf_op jit(solution)/shard_map/ppermute | solution.py:164
  72.9 15.5 %collective-permute-start.16 = (bf16[2,128,512]{2,1,0:T(8,128)(2,1)S(1)}, bf16[2,128,512]{2,1,0:T(8,128)(2,1)S(1)}, u32[]{:S(2)}, u32[]{:S(2)}) collective-permute-start(bf16[2,128,512]{2,1,0:T(8,128)(2,1)S(1)} %bitcast.31), channel_id=1, source_target_pairs={{0,2},{1,3},{2,0},{3,1},{4,6},{5,7},{6,4},{7,5},{8,10},{9,11},{10,... | collective-permute-start | bytes 786440 | tf_op jit(solution)/shard_map/ppermute | solution.py:164
  77.2 11.4 %collective-permute-start.12 = (bf16[2,128,512]{2,1,0:T(8,128)(2,1)S(1)}, bf16[2,128,512]{2,1,0:T(8,128)(2,1)S(1)}, u32[]{:S(2)}, u32[]{:S(2)}) collective-permute-start(bf16[2,128,512]{2,1,0:T(8,128)(2,1)S(1)} %bitcast.29), channel_id=1, source_target_pairs={{0,2},{1,3},{2,0},{3,1},{4,6},{5,7},{6,4},{7,5},{8,10},{9,11},{10,... | collective-permute-start | bytes 786440 | tf_op jit(solution)/shard_map/ppermute | solution.py:164
  79.1 14.8 %collective-permute-start.15 = (bf16[2,128,512]{2,1,0:T(8,128)(2,1)S(1)}, bf16[2,128,512]{2,1,0:T(8,128)(2,1)S(1)}, u32[]{:S(2)}, u32[]{:S(2)}) collective-permute-start(bf16[2,128,512]{2,1,0:T(8,128)(2,1)S(1)} %add_convert_fusion.1), channel_id=1, source_target_pairs={{0,12},{1,13},{2,14},{3,15},{4,8},{5,9},{6,10},{7,11},{8,4},{9,5},... | collective-permute-start | bytes 786440 | tf_op jit(solution)/shard_map/ppermute | solution.py:164
  88.4 8.2 %collective-permute-start.17 = (bf16[2,128,512]{2,1,0:T(8,128)(2,1)S(1)}, bf16[2,128,512]{2,1,0:T(8,128)(2,1)S(1)}, u32[]{:S(2)}, u32[]{:S(2)}) collective-permute-start(bf16[2,128,512]{2,1,0:T(8,128)(2,1)S(1)} %add_convert_fusion), channel_id=1, source_target_pairs={{0,4},{1,5},{2,6},{3,7},{4,0},{5,1},{6,2},{7,3},{8,12},{9,13},{10,... | collective-permute-start | bytes 786440 | tf_op jit(solution)/shard_map/ppermute | solution.py:164
  96.8 1.6 %collective-permute-start.18 = (f32[128,512]{1,0:T(8,128)S(1)}, f32[128,512]{1,0:T(8,128)S(1)}, u32[]{:S(2)}, u32[]{:S(2)}) collective-permute-start(f32[128,512]{1,0:T(8,128)S(1)} %slice_bitcast_fusion), channel_id=1, source_target_pairs={{0,1},{1,0},{2,3},{3,2},{4,5},{5,4},{6,7},{7,6},{8,9},{9,8},{10,11... | collective-permute-start | bytes 786440 | tf_op jit(solution)/shard_map/ppermute | solution.py:164
where the time goes:
time: 99.9 us; the launch traced here: 99.3 us
  starting transfers between devices  31.1 us (31%)
  local copies, waits for them, and re-layouts  22.1 us (22%)
  Pallas kernels  21.8 us (22%)
  waiting for transfers between devices  21.4 us (21%)
  other arithmetic  2.03 us (2%)
    ppermute x19, starting transfers between devices, move(): return lax.ppermute(value, 'term', pairs)  31.1 us
    ppermute x19, waiting for transfers between devices, move(): return lax.ppermute(value, 'term', pairs)  21.4 us
    unnamed x12, local copies, waits for them, and re-layouts  21 us
    pallas_call x4, Pallas kernels, right_mix(): pl.pallas_call(functools.partial(right_kernel, phase), out_shape=(jax.Sha...  11.7 us
    pallas_call x4, Pallas kernels, local(): pl.pallas_call(functools.partial(left_kernel, phase), out_shape=(jax.Shap...  10.1 us
  transfers between devices with their start and end apart: 19, of which 9 were waited for; matrix products, arithmetic and copies ran while one was open for 1% of the time, Pallas kernels for 19%

commit v1 on v0

--- a/solution.py
+++ b/solution.py
@@ -10,7 +10,7 @@
 F32, BF16 = jnp.float32, jnp.bfloat16
 CORES = 2
 TILE = 256
-VMEM = 16 * 1024 * 1024
+VMEM = 48 * 1024 * 1024
 ANY = pl.BlockSpec(memory_space=pl.ANY)
 SMEM = pl.BlockSpec(memory_space=pltpu.SMEM)
 WHOLE = pl.BlockSpec(memory_space=pltpu.VMEM)

time: 99.9 us -> 100 us (level)
  the two profiles are of different devices: /device:TPU:0 before, /device:TPU:13 now
where the time goes in v1:
time: 100 us; the launch traced here: 99 us
  Pallas kernels  41.3 us (41%)
  starting transfers between devices  30.4 us (30%)
  waiting for transfers between devices  18.4 us (18%)
  local copies, waits for them, and re-layouts  6.15 us (6%)
  other arithmetic  2.03 us (2%)
    ppermute x19, starting transfers between devices, move(): return lax.ppermute(value, 'term', pairs)  30.4 us
    pallas_call x4, Pallas kernels, right_mix(): pl.pallas_call(functools.partial(right_kernel, phase), out_shape=(jax.Sha...  25.5 us
    ppermute x19, waiting for transfers between devices, move(): return lax.ppermute(value, 'term', pairs)  18.4 us
    pallas_call x4, Pallas kernels, local(): pl.pallas_call(functools.partial(left_kernel, phase), out_shape=(jax.Shap...  15.8 us
    unnamed x4, local copies, waits for them, and re-layouts  4.98 us
  transfers between devices with their start and end apart: 19, of which 7 were waited for; matrix products, arithmetic and copies ran while one was open for 1% of the time, Pallas kernels for 35%

profile of v1, /device:TPU:13, one launch (start us, length us, event | category | flops | bytes accessed | tf_op | source)
XLA Modules:
  0.0 99.0 jit_solution(1978599544284740407)
XLA Ops:
  0.0 1.0 dynamic-slice_bitcast_fusion
  1.0 0.7 collective-permute-start
  2.4 0.7 pad_add_fusion.refs_0_.own
  3.1 0.0 collective-permute-start.1
  3.1 1.1 %collective-permute-done.1.refs_1_.sib = s32[21]{0:T(128)S(1)} collective-permute-done((s32[21]{0:T(128)S(1)}, s32[21]{0:T(128)S(1)}, u32[]{:S(2)}, u32[]{:S(2)}) %collective-permute-start.1) | collective-permute-done | bytes 116 | tf_op jit(solution)/shard_map/ppermute | solution.py:164
  4.3 0.0 collective-permute-done
  4.3 0.2 collective-permute-start.6
  4.5 1.3 %collective-permute-start.4 = (bf16[2,128,512]{2,1,0:T(8,128)(2,1)S(1)}, bf16[2,128,512]{2,1,0:T(8,128)(2,1)S(1)}, u32[]{:S(2)}, u32[]{:S(2)}) collective-permute-start(bf16[2,128,512]{2,1,0:T(8,128)(2,1)S(1)} %pad_maximum_fusion.1.refs_3_), channel_id=1, source_target_pairs={{0,2},{1,3},{2,0},{3,1},{4,6},{5,7},{6,4},{7,5},{8,10},{9,11},{10,... | collective-permute-start | bytes 786440 | tf_op jit(solution)/shard_map/ppermute | solution.py:164
  5.8 0.2 collective-permute-start.3
  5.9 2.4 %collective-permute-start.2 = (bf16[2,128,512]{2,1,0:T(8,128)(2,1)S(1)}, bf16[2,128,512]{2,1,0:T(8,128)(2,1)S(1)}, u32[]{:S(2)}, u32[]{:S(2)}) collective-permute-start(bf16[2,128,512]{2,1,0:T(8,128)(2,1)S(1)} %pad_maximum_fusion.1.refs_3_), channel_id=1, source_target_pairs={{0,12},{1,13},{2,14},{3,15},{4,8},{5,9},{6,10},{7,11},{8,4},{9,5},... | collective-permute-start | bytes 786440 | tf_op jit(solution)/shard_map/ppermute | solution.py:164
  8.4 3.8 %collective-permute-done.4 = bf16[2,128,512]{2,1,0:T(8,128)(2,1)S(1)} collective-permute-done((bf16[2,128,512]{2,1,0:T(8,128)(2,1)S(1)}, bf16[2,128,512]{2,1,0:T(8,128)(2,1)S(1)}, u32[]{:S(2)}, u32[]{:S(2)}) %collective-permute-start.4) | collective-permute-done | bytes 262176 | tf_op jit(solution)/shard_map/ppermute | solution.py:164
  12.2 0.9 collective-permute-done.3.refs_3_
  13.0 0.3 collective-permute-start.5
  13.4 0.1 stack.58.refs_2_
  13.5 0.0 collective-permute-done.6.refs_6_
  13.5 0.0 copy-start
  13.5 2.5 %copy-done = bf16[10,512,512]{2,1,0:T(8,128)(2,1)S(1)} copy-done((bf16[10,512,512]{2,1,0:T(8,128)(2,1)S(1)}, bf16[10,512,512]{2,1,0:T(8,128)(2,1)}, u32[]{:S(2)}) %copy-start) | copy-done | bytes 5242904
  15.9 4.0 %left_mix.4 = (bf16[20,512,512]{2,1,0:T(8,128)(2,1)}, f32[8,128]{1,0:T(8,128)S(1)}) custom-call(s32[21]{0:T(128)S(1)} %pad_add_fusion.refs_0_.own, s32[21]{0:T(128)S(1)} %collective-permute-done.1.refs_1_.sib, s32[6]{0:T(128)S(1)} %stack.58.refs_2_, bf16[2,128,512]{2,1,0:T(8,128)(2,1)S(1)} %pad_maximum_fusion.1.refs_3_, ...), custom_call_target="tpu_custom_call" | custom-call | flops 1000000 | bytes 512 | tf_op jit(solution)/shard_map/left_mix/pallas_call | solution.py:211
  20.0 0.0 collective-permute-done.2.refs_3_
  20.0 0.0 collective-permute-done.5
  20.0 1.9 %collective-permute-start.10 = (bf16[10,512,512]{2,1,0:T(8,128)(2,1)}, bf16[10,512,512]{2,1,0:T(8,128)(2,1)}, u32[]{:S(2)}, u32[]{:S(2)}) collective-permute-start(bf16[10,512,512]{2,1,0:T(8,128)(2,1)} %right.7), channel_id=1, source_target_pairs={{0,1},{1,0},{2,3},{3,2},{4,5},{5,4},{6,7},{7,6},{8,9},{9,8},{10,11... | collective-permute-start | bytes 15728648 | tf_op jit(solution)/shard_map/ppermute | solution.py:164
  21.9 0.5 collective-permute-start.7
  22.4 1.6 %collective-permute-start.9 = (bf16[2,128,512]{2,1,0:T(8,128)(2,1)S(1)}, bf16[2,128,512]{2,1,0:T(8,128)(2,1)S(1)}, u32[]{:S(2)}, u32[]{:S(2)}) collective-permute-start(bf16[2,128,512]{2,1,0:T(8,128)(2,1)S(1)} %collective-permute-done.2.refs_3_), channel_id=1, source_target_pairs={{0,2},{1,3},{2,0},{3,1},{4,6},{5,7},{6,4},{7,5},{8,10},{9,11},{10,... | collective-permute-start | bytes 786440 | tf_op jit(solution)/shard_map/ppermute | solution.py:164
  24.0 4.0 %left_mix.5 = (bf16[20,512,512]{2,1,0:T(8,128)(2,1)}, f32[8,128]{1,0:T(8,128)S(1)}) custom-call(s32[21]{0:T(128)S(1)} %pad_add_fusion.refs_0_.own, s32[21]{0:T(128)S(1)} %collective-permute-done.1.refs_1_.sib, s32[6]{0:T(128)S(1)} %stack.58.refs_2_, bf16[2,128,512]{2,1,0:T(8,128)(2,1)S(1)} %collective-permute-done.3.refs_3_, ...), custom_call_target="tpu_custom_call", output_to_operand_aliasing={{0}: (7, {})} | custom-call | flops 1000000 | bytes 512 | tf_op jit(solution)/shard_map/left_mix/pallas_call | solution.py:211
  28.0 1.8 %collective-permute-done.7.refs_3_ = bf16[2,128,512]{2,1,0:T(8,128)(2,1)S(1)} collective-permute-done((bf16[2,128,512]{2,1,0:T(8,128)(2,1)S(1)}, bf16[2,128,512]{2,1,0:T(8,128)(2,1)S(1)}, u32[]{:S(2)}, u32[]{:S(2)}) %collective-permute-start.7) | collective-permute-done | bytes 262176 | tf_op jit(solution)/shard_map/ppermute | solution.py:164
  29.8 2.1 %collective-permute-start.8 = (bf16[2,128,512]{2,1,0:T(8,128)(2,1)S(1)}, bf16[2,128,512]{2,1,0:T(8,128)(2,1)S(1)}, u32[]{:S(2)}, u32[]{:S(2)}) collective-permute-start(bf16[2,128,512]{2,1,0:T(8,128)(2,1)S(1)} %collective-permute-done.7.refs_3_), channel_id=1, source_target_pairs={{0,2},{1,3},{2,0},{3,1},{4,6},{5,7},{6,4},{7,5},{8,10},{9,11},{10,... | collective-permute-start | bytes 786440 | tf_op jit(solution)/shard_map/ppermute | solution.py:164
  31.9 0.1 stack.57.where
  32.0 0.0 collective-permute-done.9
  32.0 0.0 copy-start.1
  32.0 2.5 %copy-done.1 = bf16[10,512,512]{2,1,0:T(8,128)(2,1)S(1)} copy-done((bf16[10,512,512]{2,1,0:T(8,128)(2,1)S(1)}, bf16[10,512,512]{2,1,0:T(8,128)(2,1)}, u32[]{:S(2)}) %copy-start.1) | copy-done | bytes 5242904
  34.5 3.7 %left_mix.6 = (bf16[20,512,512]{2,1,0:T(8,128)(2,1)}, f32[8,128]{1,0:T(8,128)S(1)}) custom-call(s32[21]{0:T(128)S(1)} %pad_add_fusion.refs_0_.own, s32[21]{0:T(128)S(1)} %collective-permute-done.1.refs_1_.sib, s32[6]{0:T(128)S(1)} %stack.58.refs_2_, bf16[2,128,512]{2,1,0:T(8,128)(2,1)S(1)} %collective-permute-done.2.refs_3_, ...), custom_call_target="tpu_custom_call", output_to_operand_aliasing={{0}: (7, {})} | custom-call | flops 1000000 | bytes 512 | tf_op jit(solution)/shard_map/left_mix/pallas_call | solution.py:211
  38.2 0.0 collective-permute-done.8
  38.2 4.1 %left_mix.7 = (bf16[20,512,512]{2,1,0:T(8,128)(2,1)}, f32[8,128]{1,0:T(8,128)}) custom-call(s32[21]{0:T(128)S(1)} %pad_add_fusion.refs_0_.own, s32[21]{0:T(128)S(1)} %collective-permute-done.1.refs_1_.sib, s32[6]{0:T(128)S(1)} %stack.58.refs_2_, bf16[2,128,512]{2,1,0:T(8,128)(2,1)S(1)} %collective-permute-done.7.refs_3_, ...), custom_call_target="tpu_custom_call", output_to_operand_aliasing={{0}: (7, {})} | custom-call | flops 1000000 | bytes 512 | tf_op jit(solution)/shard_map/left_mix/pallas_call | solution.py:211
  42.3 0.0 collective-permute-done.10.right_sib
  42.3 6.1 %right_mix.4 = (f32[2,128,512]{2,1,0:T(8,128)S(1)}, bf16[1,2,128,512]{3,2,1,0:T(8,128)(2,1)S(1)}) custom-call(s32[21]{0:T(128)S(1)} %pad_add_fusion.refs_0_.own, s32[21]{0:T(128)S(1)} %collective-permute-done.1.refs_1_.sib, s32[6]{0:T(128)S(1)} %stack.57.where, bf16[20,512,512]{2,1,0:T(8,128)(2,1)} %get-tuple-element.49.mixed, bf16[10,512,512]{2,1,0:T(8,128)(2,1)} %right.7, ...), custom_call_target="tpu_custom_call" | custom-call | flops 3000000000 | bytes 3670016 | tf_op jit(solution)/shard_map/right_mix/pallas_call | solution.py:234
  48.5 0.1 collective-permute-start.11
  48.5 6.1 %right_mix.6 = (f32[2,128,512]{2,1,0:T(8,128)S(1)}, bf16[1,2,128,512]{3,2,1,0:T(8,128)(2,1)S(1)}) custom-call(s32[21]{0:T(128)S(1)} %pad_add_fusion.refs_0_.own, s32[21]{0:T(128)S(1)} %collective-permute-done.1.refs_1_.sib, s32[6]{0:T(128)S(1)} %stack.57.where, bf16[20,512,512]{2,1,0:T(8,128)(2,1)} %get-tuple-element.49.mixed, bf16[10,512,512]{2,1,0:T(8,128)(2,1)} %right.7, ...), custom_call_target="tpu_custom_call" | custom-call | flops 3000000000 | bytes 3670016 | tf_op jit(solution)/shard_map/right_mix/pallas_call | solution.py:234
  54.7 2.0 %collective-permute-start.13 = (bf16[2,128,512]{2,1,0:T(8,128)(2,1)S(1)}, bf16[2,128,512]{2,1,0:T(8,128)(2,1)S(1)}, u32[]{:S(2)}, u32[]{:S(2)}) collective-permute-start(bf16[2,128,512]{2,1,0:T(8,128)(2,1)S(1)} %bitcast.30), channel_id=1, source_target_pairs={{0,2},{1,3},{2,0},{3,1},{4,6},{5,7},{6,4},{7,5},{8,10},{9,11},{10,... | collective-permute-start | bytes 786440 | tf_op jit(solution)/shard_map/ppermute | solution.py:164
  56.7 0.0 collective-permute-done.11
  56.7 0.1 add_convert_fusion.2
  56.7 0.1 collective-permute-start.14
  56.8 6.6 %right_mix.7 = (f32[2,128,512]{2,1,0:T(8,128)S(1)}, bf16[1,2,128,512]{3,2,1,0:T(8,128)(2,1)S(1)}) custom-call(s32[21]{0:T(128)S(1)} %pad_add_fusion.refs_0_.own, s32[21]{0:T(128)S(1)} %collective-permute-done.1.refs_1_.sib, s32[6]{0:T(128)S(1)} %stack.57.where, bf16[20,512,512]{2,1,0:T(8,128)(2,1)} %get-tuple-element.49.mixed, bf16[10,512,512]{2,1,0:T(8,128)(2,1)} %right.7, ...), custom_call_target="tpu_custom_call" | custom-call | flops 3000000000 | bytes 3670016 | tf_op jit(solution)/shard_map/right_mix/pallas_call | solution.py:234
  63.4 0.4 collective-permute-start.16
  63.8 6.6 %right_mix.5 = (f32[2,128,512]{2,1,0:T(8,128)S(1)}, bf16[1,2,128,512]{3,2,1,0:T(8,128)(2,1)S(1)}) custom-call(s32[21]{0:T(128)S(1)} %pad_add_fusion.refs_0_.own, s32[21]{0:T(128)S(1)} %collective-permute-done.1.refs_1_.sib, s32[6]{0:T(128)S(1)} %stack.57.where, bf16[20,512,512]{2,1,0:T(8,128)(2,1)} %get-tuple-element.49.mixed, bf16[10,512,512]{2,1,0:T(8,128)(2,1)} %right.7, ...), custom_call_target="tpu_custom_call" | custom-call | flops 3000000000 | bytes 3670016 | tf_op jit(solution)/shard_map/right_mix/pallas_call | solution.py:234
  70.4 1.2 %collective-permute-start.12 = (bf16[2,128,512]{2,1,0:T(8,128)(2,1)S(1)}, bf16[2,128,512]{2,1,0:T(8,128)(2,1)S(1)}, u32[]{:S(2)}, u32[]{:S(2)}) collective-permute-start(bf16[2,128,512]{2,1,0:T(8,128)(2,1)S(1)} %bitcast.29), channel_id=1, source_target_pairs={{0,2},{1,3},{2,0},{3,1},{4,6},{5,7},{6,4},{7,5},{8,10},{9,11},{10,... | collective-permute-start | bytes 786440 | tf_op jit(solution)/shard_map/ppermute | solution.py:164
  71.6 0.0 collective-permute-done.13
  71.6 0.0 collective-permute-done.14
  71.6 0.1 add_convert_fusion.1
  71.8 9.3 %collective-permute-start.15 = (bf16[2,128,512]{2,1,0:T(8,128)(2,1)S(1)}, bf16[2,128,512]{2,1,0:T(8,128)(2,1)S(1)}, u32[]{:S(2)}, u32[]{:S(2)}) collective-permute-start(bf16[2,128,512]{2,1,0:T(8,128)(2,1)S(1)} %add_convert_fusion.1), channel_id=1, source_target_pairs={{0,12},{1,13},{2,14},{3,15},{4,8},{5,9},{6,10},{7,11},{8,4},{9,5},... | collective-permute-start | bytes 786440 | tf_op jit(solution)/shard_map/ppermute | solution.py:164
  81.0 0.0 collective-permute-done.16
  81.0 0.1 add_convert_fusion
  81.1 2.9 %collective-permute-start.17 = (bf16[2,128,512]{2,1,0:T(8,128)(2,1)S(1)}, bf16[2,128,512]{2,1,0:T(8,128)(2,1)S(1)}, u32[]{:S(2)}, u32[]{:S(2)}) collective-permute-start(bf16[2,128,512]{2,1,0:T(8,128)(2,1)S(1)} %add_convert_fusion), channel_id=1, source_target_pairs={{0,4},{1,5},{2,6},{3,7},{4,0},{5,1},{6,2},{7,3},{8,12},{9,13},{10,... | collective-permute-start | bytes 786440 | tf_op jit(solution)/shard_map/ppermute | solution.py:164
  84.0 0.0 collective-permute-done.12
  84.0 7.4 %collective-permute-done.15 = bf16[2,128,512]{2,1,0:T(8,128)(2,1)S(1)} collective-permute-done((bf16[2,128,512]{2,1,0:T(8,128)(2,1)S(1)}, bf16[2,128,512]{2,1,0:T(8,128)(2,1)S(1)}, u32[]{:S(2)}, u32[]{:S(2)}) %collective-permute-start.15) | collective-permute-done | bytes 262176 | tf_op jit(solution)/shard_map/ppermute | solution.py:164
  91.4 2.1 %collective-permute-done.17 = bf16[2,128,512]{2,1,0:T(8,128)(2,1)S(1)} collective-permute-done((bf16[2,128,512]{2,1,0:T(8,128)(2,1)S(1)}, bf16[2,128,512]{2,1,0:T(8,128)(2,1)S(1)}, u32[]{:S(2)}, u32[]{:S(2)}) %collective-permute-start.17) | collective-permute-done | bytes 262176 | tf_op jit(solution)/shard_map/ppermute | solution.py:164
  93.6 0.1 convert_add_fusion
  93.7 3.3 %collective-permute-start.18 = (f32[128,512]{1,0:T(8,128)S(1)}, f32[128,512]{1,0:T(8,128)S(1)}, u32[]{:S(2)}, u32[]{:S(2)}) collective-permute-start(f32[128,512]{1,0:T(8,128)S(1)} %slice_bitcast_fusion), channel_id=1, source_target_pairs={{0,1},{1,0},{2,3},{3,2},{4,5},{5,4},{6,7},{7,6},{8,9},{9,8},{10,11... | collective-permute-start | bytes 786440 | tf_op jit(solution)/shard_map/ppermute | solution.py:164
  97.0 1.2 %collective-permute-done.18 = f32[128,512]{1,0:T(8,128)S(1)} collective-permute-done((f32[128,512]{1,0:T(8,128)S(1)}, f32[128,512]{1,0:T(8,128)S(1)}, u32[]{:S(2)}, u32[]{:S(2)}) %collective-permute-start.18) | collective-permute-done | bytes 262176 | tf_op jit(solution)/shard_map/ppermute | solution.py:164
  98.2 0.8 pad_maximum_fusion
  (3 shorter events, 0.1 us)
Async XLA Ops:
  1.0 3.3 %collective-permute-start = (bf16[128,512]{1,0:T(8,128)(2,1)S(1)}, bf16[128,512]{1,0:T(8,128)(2,1)S(1)}, u32[]{:S(2)}, u32[]{:S(2)}) collective-permute-start(bf16[128,512]{1,0:T(8,128)(2,1)S(1)} %get-tuple-element.64), channel_id=1, source_target_pairs={{0,1},{1,0},{2,3},{3,2},{4,5},{5,4},{6,7},{7,6},{8,9},{9,8},{10,11... | collective-permute-start | bytes 393224 | tf_op jit(solution)/shard_map/ppermute | solution.py:164
  3.1 1.1 %collective-permute-start.1 = (s32[21]{0:T(128)S(1)}, s32[21]{0:T(128)S(1)}, u32[]{:S(2)}, u32[]{:S(2)}) collective-permute-start(s32[21]{0:T(128)S(1)} %pad_add_fusion.refs_0_.own), channel_id=1, source_target_pairs={{0,1},{1,0},{2,3},{3,2},{4,5},{5,4},{6,7},{7,6},{8,9},{9,8},{10,11... | collective-permute-start | bytes 260 | tf_op jit(solution)/shard_map/ppermute | solution.py:164
  4.3 9.2 %collective-permute-start.6 = (bf16[10,512,512]{2,1,0:T(8,128)(2,1)}, bf16[10,512,512]{2,1,0:T(8,128)(2,1)}, u32[]{:S(2)}, u32[]{:S(2)}) collective-permute-start(bf16[10,512,512]{2,1,0:T(8,128)(2,1)} %refs_5_.7), channel_id=1, source_target_pairs={{0,1},{1,0},{2,3},{3,2},{4,5},{5,4},{6,7},{7,6},{8,9},{9,8},{10,11... | collective-permute-start | bytes 15728648 | tf_op jit(solution)/shard_map/ppermute | solution.py:164
  4.5 7.7 %collective-permute-start.4 = (bf16[2,128,512]{2,1,0:T(8,128)(2,1)S(1)}, bf16[2,128,512]{2,1,0:T(8,128)(2,1)S(1)}, u32[]{:S(2)}, u32[]{:S(2)}) collective-permute-start(bf16[2,128,512]{2,1,0:T(8,128)(2,1)S(1)} %pad_maximum_fusion.1.refs_3_), channel_id=1, source_target_pairs={{0,2},{1,3},{2,0},{3,1},{4,6},{5,7},{6,4},{7,5},{8,10},{9,11},{10,... | collective-permute-start | bytes 786440 | tf_op jit(solution)/shard_map/ppermute | solution.py:164
  5.8 7.3 %collective-permute-start.3 = (bf16[2,128,512]{2,1,0:T(8,128)(2,1)S(1)}, bf16[2,128,512]{2,1,0:T(8,128)(2,1)S(1)}, u32[]{:S(2)}, u32[]{:S(2)}) collective-permute-start(bf16[2,128,512]{2,1,0:T(8,128)(2,1)S(1)} %pad_maximum_fusion.1.refs_3_), channel_id=1, source_target_pairs={{0,4},{1,5},{2,6},{3,7},{4,0},{5,1},{6,2},{7,3},{8,12},{9,13},{10,... | collective-permute-start | bytes 786440 | tf_op jit(solution)/shard_map/ppermute | solution.py:164
  5.9 14.1 %collective-permute-start.2 = (bf16[2,128,512]{2,1,0:T(8,128)(2,1)S(1)}, bf16[2,128,512]{2,1,0:T(8,128)(2,1)S(1)}, u32[]{:S(2)}, u32[]{:S(2)}) collective-permute-start(bf16[2,128,512]{2,1,0:T(8,128)(2,1)S(1)} %pad_maximum_fusion.1.refs_3_), channel_id=1, source_target_pairs={{0,12},{1,13},{2,14},{3,15},{4,8},{5,9},{6,10},{7,11},{8,4},{9,5},... | collective-permute-start | bytes 786440 | tf_op jit(solution)/shard_map/ppermute | solution.py:164
  13.0 7.0 %collective-permute-start.5 = (bf16[2,128,512]{2,1,0:T(8,128)(2,1)S(1)}, bf16[2,128,512]{2,1,0:T(8,128)(2,1)S(1)}, u32[]{:S(2)}, u32[]{:S(2)}) collective-permute-start(bf16[2,128,512]{2,1,0:T(8,128)(2,1)S(1)} %collective-permute-done.3.refs_3_), channel_id=1, source_target_pairs={{0,2},{1,3},{2,0},{3,1},{4,6},{5,7},{6,4},{7,5},{8,10},{9,11},{10,... | collective-permute-start | bytes 786440 | tf_op jit(solution)/shard_map/ppermute | solution.py:164
  13.5 2.5 %copy-start = (bf16[10,512,512]{2,1,0:T(8,128)(2,1)S(1)}, bf16[10,512,512]{2,1,0:T(8,128)(2,1)}, u32[]{:S(2)}) copy-start(bf16[10,512,512]{2,1,0:T(8,128)(2,1)} %refs_5_.7) | copy-start | bytes 15728644
  20.0 22.3 %collective-permute-start.10 = (bf16[10,512,512]{2,1,0:T(8,128)(2,1)}, bf16[10,512,512]{2,1,0:T(8,128)(2,1)}, u32[]{:S(2)}, u32[]{:S(2)}) collective-permute-start(bf16[10,512,512]{2,1,0:T(8,128)(2,1)} %right.7), channel_id=1, source_target_pairs={{0,1},{1,0},{2,3},{3,2},{4,5},{5,4},{6,7},{7,6},{8,9},{9,8},{10,11... | collective-permute-start | bytes 15728648 | tf_op jit(solution)/shard_map/ppermute | solution.py:164
  21.9 7.9 %collective-permute-start.7 = (bf16[2,128,512]{2,1,0:T(8,128)(2,1)S(1)}, bf16[2,128,512]{2,1,0:T(8,128)(2,1)S(1)}, u32[]{:S(2)}, u32[]{:S(2)}) collective-permute-start(bf16[2,128,512]{2,1,0:T(8,128)(2,1)S(1)} %collective-permute-done.2.refs_3_), channel_id=1, source_target_pairs={{0,4},{1,5},{2,6},{3,7},{4,0},{5,1},{6,2},{7,3},{8,12},{9,13},{10,... | collective-permute-start | bytes 786440 | tf_op jit(solution)/shard_map/ppermute | solution.py:164
  22.4 9.6 %collective-permute-start.9 = (bf16[2,128,512]{2,1,0:T(8,128)(2,1)S(1)}, bf16[2,128,512]{2,1,0:T(8,128)(2,1)S(1)}, u32[]{:S(2)}, u32[]{:S(2)}) collective-permute-start(bf16[2,128,512]{2,1,0:T(8,128)(2,1)S(1)} %collective-permute-done.2.refs_3_), channel_id=1, source_target_pairs={{0,2},{1,3},{2,0},{3,1},{4,6},{5,7},{6,4},{7,5},{8,10},{9,11},{10,... | collective-permute-start | bytes 786440 | tf_op jit(solution)/shard_map/ppermute | solution.py:164
  29.8 8.4 %collective-permute-start.8 = (bf16[2,128,512]{2,1,0:T(8,128)(2,1)S(1)}, bf16[2,128,512]{2,1,0:T(8,128)(2,1)S(1)}, u32[]{:S(2)}, u32[]{:S(2)}) collective-permute-start(bf16[2,128,512]{2,1,0:T(8,128)(2,1)S(1)} %collective-permute-done.7.refs_3_), channel_id=1, source_target_pairs={{0,2},{1,3},{2,0},{3,1},{4,6},{5,7},{6,4},{7,5},{8,10},{9,11},{10,... | collective-permute-start | bytes 786440 | tf_op jit(solution)/shard_map/ppermute | solution.py:164
  32.0 2.5 %copy-start.1 = (bf16[10,512,512]{2,1,0:T(8,128)(2,1)S(1)}, bf16[10,512,512]{2,1,0:T(8,128)(2,1)}, u32[]{:S(2)}) copy-start(bf16[10,512,512]{2,1,0:T(8,128)(2,1)} %refs_5_.7) | copy-start | bytes 15728644
  48.5 8.2 %collective-permute-start.11 = (bf16[2,128,512]{2,1,0:T(8,128)(2,1)S(1)}, bf16[2,128,512]{2,1,0:T(8,128)(2,1)S(1)}, u32[]{:S(2)}, u32[]{:S(2)}) collective-permute-start(bf16[2,128,512]{2,1,0:T(8,128)(2,1)S(1)} %bitcast.32), channel_id=1, source_target_pairs={{0,2},{1,3},{2,0},{3,1},{4,6},{5,7},{6,4},{7,5},{8,10},{9,11},{10,... | collective-permute-start | bytes 786440 | tf_op jit(solution)/shard_map/ppermute | solution.py:164
  54.7 17.0 %collective-permute-start.13 = (bf16[2,128,512]{2,1,0:T(8,128)(2,1)S(1)}, bf16[2,128,512]{2,1,0:T(8,128)(2,1)S(1)}, u32[]{:S(2)}, u32[]{:S(2)}) collective-permute-start(bf16[2,128,512]{2,1,0:T(8,128)(2,1)S(1)} %bitcast.30), channel_id=1, source_target_pairs={{0,2},{1,3},{2,0},{3,1},{4,6},{5,7},{6,4},{7,5},{8,10},{9,11},{10,... | collective-permute-start | bytes 786440 | tf_op jit(solution)/shard_map/ppermute | solution.py:164
  56.7 14.9 %collective-permute-start.14 = (bf16[2,128,512]{2,1,0:T(8,128)(2,1)S(1)}, bf16[2,128,512]{2,1,0:T(8,128)(2,1)S(1)}, u32[]{:S(2)}, u32[]{:S(2)}) collective-permute-start(bf16[2,128,512]{2,1,0:T(8,128)(2,1)S(1)} %add_convert_fusion.2), channel_id=1, source_target_pairs={{0,4},{1,5},{2,6},{3,7},{4,0},{5,1},{6,2},{7,3},{8,12},{9,13},{10,... | collective-permute-start | bytes 786440 | tf_op jit(solution)/shard_map/ppermute | solution.py:164
  63.4 17.6 %collective-permute-start.16 = (bf16[2,128,512]{2,1,0:T(8,128)(2,1)S(1)}, bf16[2,128,512]{2,1,0:T(8,128)(2,1)S(1)}, u32[]{:S(2)}, u32[]{:S(2)}) collective-permute-start(bf16[2,128,512]{2,1,0:T(8,128)(2,1)S(1)} %bitcast.31), channel_id=1, source_target_pairs={{0,2},{1,3},{2,0},{3,1},{4,6},{5,7},{6,4},{7,5},{8,10},{9,11},{10,... | collective-permute-start | bytes 786440 | tf_op jit(solution)/shard_map/ppermute | solution.py:164
  70.4 13.6 %collective-permute-start.12 = (bf16[2,128,512]{2,1,0:T(8,128)(2,1)S(1)}, bf16[2,128,512]{2,1,0:T(8,128)(2,1)S(1)}, u32[]{:S(2)}, u32[]{:S(2)}) collective-permute-start(bf16[2,128,512]{2,1,0:T(8,128)(2,1)S(1)} %bitcast.29), channel_id=1, source_target_pairs={{0,2},{1,3},{2,0},{3,1},{4,6},{5,7},{6,4},{7,5},{8,10},{9,11},{10,... | collective-permute-start | bytes 786440 | tf_op jit(solution)/shard_map/ppermute | solution.py:164
  71.8 19.7 %collective-permute-start.15 = (bf16[2,128,512]{2,1,0:T(8,128)(2,1)S(1)}, bf16[2,128,512]{2,1,0:T(8,128)(2,1)S(1)}, u32[]{:S(2)}, u32[]{:S(2)}) collective-permute-start(bf16[2,128,512]{2,1,0:T(8,128)(2,1)S(1)} %add_convert_fusion.1), channel_id=1, source_target_pairs={{0,12},{1,13},{2,14},{3,15},{4,8},{5,9},{6,10},{7,11},{8,4},{9,5},... | collective-permute-start | bytes 786440 | tf_op jit(solution)/shard_map/ppermute | solution.py:164
  81.1 12.4 %collective-permute-start.17 = (bf16[2,128,512]{2,1,0:T(8,128)(2,1)S(1)}, bf16[2,128,512]{2,1,0:T(8,128)(2,1)S(1)}, u32[]{:S(2)}, u32[]{:S(2)}) collective-permute-start(bf16[2,128,512]{2,1,0:T(8,128)(2,1)S(1)} %add_convert_fusion), channel_id=1, source_target_pairs={{0,4},{1,5},{2,6},{3,7},{4,0},{5,1},{6,2},{7,3},{8,12},{9,13},{10,... | collective-permute-start | bytes 786440 | tf_op jit(solution)/shard_map/ppermute | solution.py:164
  93.7 4.4 %collective-permute-start.18 = (f32[128,512]{1,0:T(8,128)S(1)}, f32[128,512]{1,0:T(8,128)S(1)}, u32[]{:S(2)}, u32[]{:S(2)}) collective-permute-start(f32[128,512]{1,0:T(8,128)S(1)} %slice_bitcast_fusion), channel_id=1, source_target_pairs={{0,1},{1,0},{2,3},{3,2},{4,5},{5,4},{6,7},{7,6},{8,9},{9,8},{10,11... | collective-permute-start | bytes 786440 | tf_op jit(solution)/shard_map/ppermute | solution.py:164

commit v2 on v1

--- a/solution.py
+++ b/solution.py
@@ -9,7 +9,6 @@
 
 F32, BF16 = jnp.float32, jnp.bfloat16
 CORES = 2
-TILE = 256
 VMEM = 48 * 1024 * 1024
 ANY = pl.BlockSpec(memory_space=pl.ANY)
 SMEM = pl.BlockSpec(memory_space=pltpu.SMEM)
@@ -91,11 +90,7 @@
             def _():
                 out_copy(i - outs, o).wait()
 
-            for n in range(0, source.shape[1], TILE):
-                for m in range(0, source.shape[0], TILE):
-                    obuf[o, m : m + TILE, n : n + TILE] = jnp.dot(
-                        lbuf[k, m : m + TILE, :], source[:, n : n + TILE], preferred_element_type=F32
-                    ).astype(BF16)
+            obuf[o] = jnp.dot(lbuf[k], source[...], preferred_element_type=F32).astype(BF16)
             out_copy(i, o).start()
 
     for j in range(bands):
@@ -111,7 +106,8 @@
             out_copy(count - back, lax.rem(count - back, outs)).wait()
 
 
-def right_kernel(phase, own, sib, where, mixed, right, right_sib, keep, send, found, acc, rbuf, rsem):
+def right_kernel(phase, *refs):
+    own, sib, where, mixed, right, right_sib, keep, send, found, acc, mbuf, rbuf, msem, rsem = refs
     slots, depth = right.shape[0], rbuf.shape[0]
     half = keep.shape[1]
     bands = send.shape[0] + 1
@@ -119,19 +115,17 @@
     count = list_slots(own, sib, 1, sector, slots, found)
 
     def fetch(i, k):
+        pltpu.make_async_copy(mixed.at[found[i]], mbuf.at[k], msem.at[k]).start()
         start_fetch(found[i], slots, right, right_sib, rbuf.at[k], rsem.at[k])
 
     def wait(k):
+        pltpu.make_async_copy(mixed.at[0], mbuf.at[k], msem.at[k]).wait()
         pltpu.make_async_copy(right.at[0], rbuf.at[k], rsem.at[k]).wait()
 
     def work(items, spots):
-        for n in range(0, acc.shape[1], TILE):
-            acc[:, n : n + TILE] += sum(
-                lax.dot_general(
-                    mixed[found[i]], rbuf[k, n : n + TILE, :], (((1,), (1,)), ((), ())), preferred_element_type=F32
-                )
-                for i, k in zip(items, spots)
-            )
+        acc[...] += sum(
+            lax.dot_general(mbuf[k], rbuf[k], (((1,), (1,)), ((), ())), preferred_element_type=F32) for k in spots
+        )
 
     acc[...] = jnp.zeros_like(acc)
     in_pairs(count, depth, fetch, wait, work)
@@ -237,12 +231,14 @@
                 jax.ShapeDtypeStruct((CORES, half, width), F32),
                 jax.ShapeDtypeStruct((bands - 1, CORES, half, width), BF16),
             ),
-            in_specs=[SMEM] * 3 + [WHOLE] + [ANY] * 2,
+            in_specs=[SMEM] * 3 + [ANY] * 3,
             out_specs=(WHOLE, WHOLE),
             scratch_shapes=[
                 pltpu.SMEM((CORES * slots + 1,), jnp.int32),
                 pltpu.VMEM((width, width), F32),
                 pltpu.VMEM((depth, width, width), BF16),
+                pltpu.VMEM((depth, width, width), BF16),
+                pltpu.SemaphoreType.DMA((depth,)),
                 pltpu.SemaphoreType.DMA((depth,)),
             ],
             compiler_params=params,

time: 100 us -> 88.4 us (0.88)
  Pallas kernels: 41.3 us -> 27 us
  waiting for transfers between devices: 18.4 us -> 20.4 us
  starting transfers between devices: 30.4 us -> 31.5 us
    pallas_call x4, Pallas kernels: 25.5 us -> 14 us  [right_mix(): pl.pallas_call(functools.partial(right_kernel, phase), out_shape=(jax.Sha...]
    pallas_call x4, Pallas kernels: 15.8 us -> 13 us  [local(): pl.pallas_call(functools.partial(left_kernel, phase), out_shape=(jax.Shap...]
    ppermute x19, waiting for transfers between devices: 18.4 us -> 20.4 us  [move(): return lax.ppermute(value, 'term', pairs)]
    ppermute x19, starting transfers between devices: 30.4 us -> 31.5 us  [move(): return lax.ppermute(value, 'term', pairs)]
  transfers between devices with their start and end apart: 19 -> 19, of which waited for: 7 -> 9; matrix products, arithmetic and copies ran while one was open for 1% -> 1% of each run, Pallas kernels for 35% -> 27%
where the time goes in v2:
time: 88.4 us; the launch traced here: 87.9 us
  starting transfers between devices  31.5 us (36%)
  Pallas kernels  27 us (31%)
  waiting for transfers between devices  20.4 us (23%)
  local copies, waits for them, and re-layouts  6.15 us (7%)
  other arithmetic  2.03 us (2%)
    ppermute x19, starting transfers between devices, move(): return lax.ppermute(value, 'term', pairs)  31.5 us
    ppermute x19, waiting for transfers between devices, move(): return lax.ppermute(value, 'term', pairs)  20.4 us
    pallas_call x4, Pallas kernels, right_mix(): pl.pallas_call(functools.partial(right_kernel, phase), out_shape=(jax.Sha...  14 us
    pallas_call x4, Pallas kernels, local(): pl.pallas_call(functools.partial(left_kernel, phase), out_shape=(jax.Shap...  13 us
    unnamed x4, local copies, waits for them, and re-layouts  4.98 us
  transfers between devices with their start and end apart: 19, of which 9 were waited for; matrix products, arithmetic and copies ran while one was open for 1% of the time, Pallas kernels for 27%

profile of v2, /device:TPU:13, one launch (start us, length us, event | category | flops | bytes accessed | tf_op | source)
XLA Modules:
  0.0 87.9 jit_solution(1124051136019933188)
XLA Ops:
  0.0 1.0 %dynamic-slice_bitcast_fusion = (bf16[1,128,512]{2,1,0:T(8,128)(2,1)S(1)}, bf16[128,512]{1,0:T(8,128)(2,1)S(1)}) fusion(bf16[128,1024]{1,0:T(8,128)(2,1)} %param.6, s32[]{:T(128)S(6)} %select_n.42, s32[]{:T(128)S(6)} %select_n.38), kind=kLoop, calls=%fused_computation.10 | loop fusion | bytes 524296 | tf_op jit(solution)/shard_map/stack | solution.py:176
  1.0 0.7 collective-permute-start
  2.4 0.7 pad_add_fusion.refs_0_
  3.1 0.0 collective-permute-start.1
  3.1 1.1 %collective-permute-done.1.refs_1_ = s32[21]{0:T(128)S(1)} collective-permute-done((s32[21]{0:T(128)S(1)}, s32[21]{0:T(128)S(1)}, u32[]{:S(2)}, u32[]{:S(2)}) %collective-permute-start.1) | collective-permute-done | bytes 116 | tf_op jit(solution)/shard_map/ppermute | solution.py:158
  4.3 0.0 collective-permute-done
  4.3 0.2 collective-permute-start.6
  4.5 1.3 %collective-permute-start.4 = (bf16[2,128,512]{2,1,0:T(8,128)(2,1)S(1)}, bf16[2,128,512]{2,1,0:T(8,128)(2,1)S(1)}, u32[]{:S(2)}, u32[]{:S(2)}) collective-permute-start(bf16[2,128,512]{2,1,0:T(8,128)(2,1)S(1)} %pad_maximum_fusion.1.refs_3_), channel_id=1, source_target_pairs={{0,2},{1,3},{2,0},{3,1},{4,6},{5,7},{6,4},{7,5},{8,10},{9,11},{10,... | collective-permute-start | bytes 786440 | tf_op jit(solution)/shard_map/ppermute | solution.py:158
  5.8 0.2 collective-permute-start.3
  5.9 2.4 %collective-permute-start.2 = (bf16[2,128,512]{2,1,0:T(8,128)(2,1)S(1)}, bf16[2,128,512]{2,1,0:T(8,128)(2,1)S(1)}, u32[]{:S(2)}, u32[]{:S(2)}) collective-permute-start(bf16[2,128,512]{2,1,0:T(8,128)(2,1)S(1)} %pad_maximum_fusion.1.refs_3_), channel_id=1, source_target_pairs={{0,12},{1,13},{2,14},{3,15},{4,8},{5,9},{6,10},{7,11},{8,4},{9,5},... | collective-permute-start | bytes 786440 | tf_op jit(solution)/shard_map/ppermute | solution.py:158
  8.4 3.8 %collective-permute-done.4 = bf16[2,128,512]{2,1,0:T(8,128)(2,1)S(1)} collective-permute-done((bf16[2,128,512]{2,1,0:T(8,128)(2,1)S(1)}, bf16[2,128,512]{2,1,0:T(8,128)(2,1)S(1)}, u32[]{:S(2)}, u32[]{:S(2)}) %collective-permute-start.4) | collective-permute-done | bytes 262176 | tf_op jit(solution)/shard_map/ppermute | solution.py:158
  12.2 0.9 %collective-permute-done.3.refs_3_ = bf16[2,128,512]{2,1,0:T(8,128)(2,1)S(1)} collective-permute-done((bf16[2,128,512]{2,1,0:T(8,128)(2,1)S(1)}, bf16[2,128,512]{2,1,0:T(8,128)(2,1)S(1)}, u32[]{:S(2)}, u32[]{:S(2)}) %collective-permute-start.3) | collective-permute-done | bytes 262176 | tf_op jit(solution)/shard_map/ppermute | solution.py:158
  13.0 0.3 collective-permute-start.5
  13.4 0.1 stack.58.refs_2_
  13.5 0.0 collective-permute-done.6.refs_6_
  13.5 0.0 copy-start
  13.5 2.5 %copy-done = bf16[10,512,512]{2,1,0:T(8,128)(2,1)S(1)} copy-done((bf16[10,512,512]{2,1,0:T(8,128)(2,1)S(1)}, bf16[10,512,512]{2,1,0:T(8,128)(2,1)}, u32[]{:S(2)}) %copy-start) | copy-done | bytes 5242904
  15.9 2.1 %left_mix.4 = (bf16[20,512,512]{2,1,0:T(8,128)(2,1)}, f32[8,128]{1,0:T(8,128)S(1)}) custom-call(s32[21]{0:T(128)S(1)} %pad_add_fusion.refs_0_, s32[21]{0:T(128)S(1)} %collective-permute-done.1.refs_1_, s32[6]{0:T(128)S(1)} %stack.58.refs_2_, bf16[2,128,512]{2,1,0:T(8,128)(2,1)S(1)} %pad_maximum_fusion.1.refs_3_, bf16[1,2,128,512]{3,2,1,0:T(8,128)(2,1)S(1)} %bitcast.28, ...), custom_call_target="tpu_custom_call" | custom-call | flops 1000000 | bytes 512 | tf_op jit(solution)/shard_map/left_mix/pallas_call | solution.py:205
  18.0 0.0 collective-permute-done.2.refs_3_
  18.0 0.5 collective-permute-done.5
  18.6 3.4 %collective-permute-start.10 = (bf16[10,512,512]{2,1,0:T(8,128)(2,1)}, bf16[10,512,512]{2,1,0:T(8,128)(2,1)}, u32[]{:S(2)}, u32[]{:S(2)}) collective-permute-start(bf16[10,512,512]{2,1,0:T(8,128)(2,1)} %refs_4_.7), channel_id=1, source_target_pairs={{0,1},{1,0},{2,3},{3,2},{4,5},{5,4},{6,7},{7,6},{8,9},{9,8},{10,11... | collective-permute-start | bytes 15728648 | tf_op jit(solution)/shard_map/ppermute | solution.py:158
  21.9 0.5 collective-permute-start.7
  22.4 0.7 collective-permute-start.9
  23.1 3.7 %left_mix.5 = (bf16[20,512,512]{2,1,0:T(8,128)(2,1)}, f32[8,128]{1,0:T(8,128)S(1)}) custom-call(s32[21]{0:T(128)S(1)} %pad_add_fusion.refs_0_, s32[21]{0:T(128)S(1)} %collective-permute-done.1.refs_1_, s32[6]{0:T(128)S(1)} %stack.58.refs_2_, bf16[2,128,512]{2,1,0:T(8,128)(2,1)S(1)} %collective-permute-done.3.refs_3_, ...), custom_call_target="tpu_custom_call", output_to_operand_aliasing={{0}: (7, {})} | custom-call | flops 1000000 | bytes 512 | tf_op jit(solution)/shard_map/left_mix/pallas_call | solution.py:205
  26.8 3.0 %collective-permute-done.7.refs_3_ = bf16[2,128,512]{2,1,0:T(8,128)(2,1)S(1)} collective-permute-done((bf16[2,128,512]{2,1,0:T(8,128)(2,1)S(1)}, bf16[2,128,512]{2,1,0:T(8,128)(2,1)S(1)}, u32[]{:S(2)}, u32[]{:S(2)}) %collective-permute-start.7) | collective-permute-done | bytes 262176 | tf_op jit(solution)/shard_map/ppermute | solution.py:158
  29.9 1.1 %collective-permute-start.8 = (bf16[2,128,512]{2,1,0:T(8,128)(2,1)S(1)}, bf16[2,128,512]{2,1,0:T(8,128)(2,1)S(1)}, u32[]{:S(2)}, u32[]{:S(2)}) collective-permute-start(bf16[2,128,512]{2,1,0:T(8,128)(2,1)S(1)} %collective-permute-done.7.refs_3_), channel_id=1, source_target_pairs={{0,2},{1,3},{2,0},{3,1},{4,6},{5,7},{6,4},{7,5},{8,10},{9,11},{10,... | collective-permute-start | bytes 786440 | tf_op jit(solution)/shard_map/ppermute | solution.py:158
  31.0 0.1 stack.57.refs_2_
  31.1 0.0 collective-permute-done.9
  31.1 0.0 copy-start.1
  31.1 2.5 %copy-done.1 = bf16[10,512,512]{2,1,0:T(8,128)(2,1)S(1)} copy-done((bf16[10,512,512]{2,1,0:T(8,128)(2,1)S(1)}, bf16[10,512,512]{2,1,0:T(8,128)(2,1)}, u32[]{:S(2)}) %copy-start.1) | copy-done | bytes 5242904
  33.6 4.0 %left_mix.6 = (bf16[20,512,512]{2,1,0:T(8,128)(2,1)}, f32[8,128]{1,0:T(8,128)S(1)}) custom-call(s32[21]{0:T(128)S(1)} %pad_add_fusion.refs_0_, s32[21]{0:T(128)S(1)} %collective-permute-done.1.refs_1_, s32[6]{0:T(128)S(1)} %stack.58.refs_2_, bf16[2,128,512]{2,1,0:T(8,128)(2,1)S(1)} %collective-permute-done.2.refs_3_, ...), custom_call_target="tpu_custom_call", output_to_operand_aliasing={{0}: (7, {})} | custom-call | flops 1000000 | bytes 512 | tf_op jit(solution)/shard_map/left_mix/pallas_call | solution.py:205
  37.6 0.0 collective-permute-done.8
  37.6 3.2 %left_mix.7 = (bf16[20,512,512]{2,1,0:T(8,128)(2,1)}, f32[8,128]{1,0:T(8,128)}) custom-call(s32[21]{0:T(128)S(1)} %pad_add_fusion.refs_0_, s32[21]{0:T(128)S(1)} %collective-permute-done.1.refs_1_, s32[6]{0:T(128)S(1)} %stack.58.refs_2_, bf16[2,128,512]{2,1,0:T(8,128)(2,1)S(1)} %collective-permute-done.7.refs_3_, ...), custom_call_target="tpu_custom_call", output_to_operand_aliasing={{0}: (7, {})} | custom-call | flops 1000000 | bytes 512 | tf_op jit(solution)/shard_map/left_mix/pallas_call | solution.py:205
  40.8 0.0 collective-permute-done.10.refs_5_
  40.8 3.1 %right_mix.4 = (f32[2,128,512]{2,1,0:T(8,128)S(1)}, bf16[1,2,128,512]{3,2,1,0:T(8,128)(2,1)S(1)}) custom-call(s32[21]{0:T(128)S(1)} %pad_add_fusion.refs_0_, s32[21]{0:T(128)S(1)} %collective-permute-done.1.refs_1_, s32[6]{0:T(128)S(1)} %stack.57.refs_2_, bf16[20,512,512]{2,1,0:T(8,128)(2,1)} %get-tuple-element.49.refs_3_, bf16[10,512,512]{2,1,0:T(8,128)(2,1)} %refs_4_.7, ...), custom_call_target="tpu_custom_call" | custom-call | flops 3000000000 | bytes 3670016 | tf_op jit(solution)/shard_map/right_mix/pallas_call | solution.py:228
  43.9 3.2 %collective-permute-start.11 = (bf16[2,128,512]{2,1,0:T(8,128)(2,1)S(1)}, bf16[2,128,512]{2,1,0:T(8,128)(2,1)S(1)}, u32[]{:S(2)}, u32[]{:S(2)}) collective-permute-start(bf16[2,128,512]{2,1,0:T(8,128)(2,1)S(1)} %bitcast.32), channel_id=1, source_target_pairs={{0,2},{1,3},{2,0},{3,1},{4,6},{5,7},{6,4},{7,5},{8,10},{9,11},{10,... | collective-permute-start | bytes 786440 | tf_op jit(solution)/shard_map/ppermute | solution.py:158
  47.1 3.1 %right_mix.6 = (f32[2,128,512]{2,1,0:T(8,128)S(1)}, bf16[1,2,128,512]{3,2,1,0:T(8,128)(2,1)S(1)}) custom-call(s32[21]{0:T(128)S(1)} %pad_add_fusion.refs_0_, s32[21]{0:T(128)S(1)} %collective-permute-done.1.refs_1_, s32[6]{0:T(128)S(1)} %stack.57.refs_2_, bf16[20,512,512]{2,1,0:T(8,128)(2,1)} %get-tuple-element.49.refs_3_, bf16[10,512,512]{2,1,0:T(8,128)(2,1)} %refs_4_.7, ...), custom_call_target="tpu_custom_call" | custom-call | flops 3000000000 | bytes 3670016 | tf_op jit(solution)/shard_map/right_mix/pallas_call | solution.py:228
  50.1 0.1 collective-permute-start.13
  50.2 2.5 %collective-permute-done.11 = bf16[2,128,512]{2,1,0:T(8,128)(2,1)S(1)} collective-permute-done((bf16[2,128,512]{2,1,0:T(8,128)(2,1)S(1)}, bf16[2,128,512]{2,1,0:T(8,128)(2,1)S(1)}, u32[]{:S(2)}, u32[]{:S(2)}) %collective-permute-start.11) | collective-permute-done | bytes 262176 | tf_op jit(solution)/shard_map/ppermute | solution.py:158
  52.7 0.1 add_convert_fusion.2
  52.8 0.1 collective-permute-start.14
  52.9 4.8 %right_mix.7 = (f32[2,128,512]{2,1,0:T(8,128)S(1)}, bf16[1,2,128,512]{3,2,1,0:T(8,128)(2,1)S(1)}) custom-call(s32[21]{0:T(128)S(1)} %pad_add_fusion.refs_0_, s32[21]{0:T(128)S(1)} %collective-permute-done.1.refs_1_, s32[6]{0:T(128)S(1)} %stack.57.refs_2_, bf16[20,512,512]{2,1,0:T(8,128)(2,1)} %get-tuple-element.49.refs_3_, bf16[10,512,512]{2,1,0:T(8,128)(2,1)} %refs_4_.7, ...), custom_call_target="tpu_custom_call" | custom-call | flops 3000000000 | bytes 3670016 | tf_op jit(solution)/shard_map/right_mix/pallas_call | solution.py:228
  57.6 2.0 %collective-permute-start.16 = (bf16[2,128,512]{2,1,0:T(8,128)(2,1)S(1)}, bf16[2,128,512]{2,1,0:T(8,128)(2,1)S(1)}, u32[]{:S(2)}, u32[]{:S(2)}) collective-permute-start(bf16[2,128,512]{2,1,0:T(8,128)(2,1)S(1)} %bitcast.31), channel_id=1, source_target_pairs={{0,2},{1,3},{2,0},{3,1},{4,6},{5,7},{6,4},{7,5},{8,10},{9,11},{10,... | collective-permute-start | bytes 786440 | tf_op jit(solution)/shard_map/ppermute | solution.py:158
  59.6 3.1 %right_mix.5 = (f32[2,128,512]{2,1,0:T(8,128)S(1)}, bf16[1,2,128,512]{3,2,1,0:T(8,128)(2,1)S(1)}) custom-call(s32[21]{0:T(128)S(1)} %pad_add_fusion.refs_0_, s32[21]{0:T(128)S(1)} %collective-permute-done.1.refs_1_, s32[6]{0:T(128)S(1)} %stack.57.refs_2_, bf16[20,512,512]{2,1,0:T(8,128)(2,1)} %get-tuple-element.49.refs_3_, bf16[10,512,512]{2,1,0:T(8,128)(2,1)} %refs_4_.7, ...), custom_call_target="tpu_custom_call" | custom-call | flops 3000000000 | bytes 3670016 | tf_op jit(solution)/shard_map/right_mix/pallas_call | solution.py:228
  62.7 1.0 %collective-permute-start.12 = (bf16[2,128,512]{2,1,0:T(8,128)(2,1)S(1)}, bf16[2,128,512]{2,1,0:T(8,128)(2,1)S(1)}, u32[]{:S(2)}, u32[]{:S(2)}) collective-permute-start(bf16[2,128,512]{2,1,0:T(8,128)(2,1)S(1)} %bitcast.29), channel_id=1, source_target_pairs={{0,2},{1,3},{2,0},{3,1},{4,6},{5,7},{6,4},{7,5},{8,10},{9,11},{10,... | collective-permute-start | bytes 786440 | tf_op jit(solution)/shard_map/ppermute | solution.py:158
  63.7 0.0 collective-permute-done.13
  63.7 0.0 collective-permute-done.14
  63.7 0.1 add_convert_fusion.1
  63.8 7.3 %collective-permute-start.15 = (bf16[2,128,512]{2,1,0:T(8,128)(2,1)S(1)}, bf16[2,128,512]{2,1,0:T(8,128)(2,1)S(1)}, u32[]{:S(2)}, u32[]{:S(2)}) collective-permute-start(bf16[2,128,512]{2,1,0:T(8,128)(2,1)S(1)} %add_convert_fusion.1), channel_id=1, source_target_pairs={{0,12},{1,13},{2,14},{3,15},{4,8},{5,9},{6,10},{7,11},{8,4},{9,5},... | collective-permute-start | bytes 786440 | tf_op jit(solution)/shard_map/ppermute | solution.py:158
  71.1 0.0 collective-permute-done.16
  71.1 0.1 add_convert_fusion
  71.2 1.6 %collective-permute-start.17 = (bf16[2,128,512]{2,1,0:T(8,128)(2,1)S(1)}, bf16[2,128,512]{2,1,0:T(8,128)(2,1)S(1)}, u32[]{:S(2)}, u32[]{:S(2)}) collective-permute-start(bf16[2,128,512]{2,1,0:T(8,128)(2,1)S(1)} %add_convert_fusion), channel_id=1, source_target_pairs={{0,4},{1,5},{2,6},{3,7},{4,0},{5,1},{6,2},{7,3},{8,12},{9,13},{10,... | collective-permute-start | bytes 786440 | tf_op jit(solution)/shard_map/ppermute | solution.py:158
  72.8 0.0 collective-permute-done.12
  72.8 6.5 %collective-permute-done.15 = bf16[2,128,512]{2,1,0:T(8,128)(2,1)S(1)} collective-permute-done((bf16[2,128,512]{2,1,0:T(8,128)(2,1)S(1)}, bf16[2,128,512]{2,1,0:T(8,128)(2,1)S(1)}, u32[]{:S(2)}, u32[]{:S(2)}) %collective-permute-start.15) | collective-permute-done | bytes 262176 | tf_op jit(solution)/shard_map/ppermute | solution.py:158
  79.3 0.9 collective-permute-done.17
  80.2 0.1 convert_add_fusion
  80.4 5.5 %collective-permute-start.18 = (f32[128,512]{1,0:T(8,128)S(1)}, f32[128,512]{1,0:T(8,128)S(1)}, u32[]{:S(2)}, u32[]{:S(2)}) collective-permute-start(f32[128,512]{1,0:T(8,128)S(1)} %slice_bitcast_fusion), channel_id=1, source_target_pairs={{0,1},{1,0},{2,3},{3,2},{4,5},{5,4},{6,7},{7,6},{8,9},{9,8},{10,11... | collective-permute-start | bytes 786440 | tf_op jit(solution)/shard_map/ppermute | solution.py:158
  85.8 1.2 %collective-permute-done.18 = f32[128,512]{1,0:T(8,128)S(1)} collective-permute-done((f32[128,512]{1,0:T(8,128)S(1)}, f32[128,512]{1,0:T(8,128)S(1)}, u32[]{:S(2)}, u32[]{:S(2)}) %collective-permute-start.18) | collective-permute-done | bytes 262176 | tf_op jit(solution)/shard_map/ppermute | solution.py:158
  87.1 0.8 pad_maximum_fusion
  (3 shorter events, 0.1 us)
Async XLA Ops:
  1.0 3.3 %collective-permute-start = (bf16[128,512]{1,0:T(8,128)(2,1)S(1)}, bf16[128,512]{1,0:T(8,128)(2,1)S(1)}, u32[]{:S(2)}, u32[]{:S(2)}) collective-permute-start(bf16[128,512]{1,0:T(8,128)(2,1)S(1)} %get-tuple-element.64), channel_id=1, source_target_pairs={{0,1},{1,0},{2,3},{3,2},{4,5},{5,4},{6,7},{7,6},{8,9},{9,8},{10,11... | collective-permute-start | bytes 393224 | tf_op jit(solution)/shard_map/ppermute | solution.py:158
  3.1 1.1 %collective-permute-start.1 = (s32[21]{0:T(128)S(1)}, s32[21]{0:T(128)S(1)}, u32[]{:S(2)}, u32[]{:S(2)}) collective-permute-start(s32[21]{0:T(128)S(1)} %pad_add_fusion.refs_0_), channel_id=1, source_target_pairs={{0,1},{1,0},{2,3},{3,2},{4,5},{5,4},{6,7},{7,6},{8,9},{9,8},{10,11... | collective-permute-start | bytes 260 | tf_op jit(solution)/shard_map/ppermute | solution.py:158
  4.3 9.2 %collective-permute-start.6 = (bf16[10,512,512]{2,1,0:T(8,128)(2,1)}, bf16[10,512,512]{2,1,0:T(8,128)(2,1)}, u32[]{:S(2)}, u32[]{:S(2)}) collective-permute-start(bf16[10,512,512]{2,1,0:T(8,128)(2,1)} %refs_5_.7), channel_id=1, source_target_pairs={{0,1},{1,0},{2,3},{3,2},{4,5},{5,4},{6,7},{7,6},{8,9},{9,8},{10,11... | collective-permute-start | bytes 15728648 | tf_op jit(solution)/shard_map/ppermute | solution.py:158
  4.5 7.7 %collective-permute-start.4 = (bf16[2,128,512]{2,1,0:T(8,128)(2,1)S(1)}, bf16[2,128,512]{2,1,0:T(8,128)(2,1)S(1)}, u32[]{:S(2)}, u32[]{:S(2)}) collective-permute-start(bf16[2,128,512]{2,1,0:T(8,128)(2,1)S(1)} %pad_maximum_fusion.1.refs_3_), channel_id=1, source_target_pairs={{0,2},{1,3},{2,0},{3,1},{4,6},{5,7},{6,4},{7,5},{8,10},{9,11},{10,... | collective-permute-start | bytes 786440 | tf_op jit(solution)/shard_map/ppermute | solution.py:158
  5.8 7.3 %collective-permute-start.3 = (bf16[2,128,512]{2,1,0:T(8,128)(2,1)S(1)}, bf16[2,128,512]{2,1,0:T(8,128)(2,1)S(1)}, u32[]{:S(2)}, u32[]{:S(2)}) collective-permute-start(bf16[2,128,512]{2,1,0:T(8,128)(2,1)S(1)} %pad_maximum_fusion.1.refs_3_), channel_id=1, source_target_pairs={{0,4},{1,5},{2,6},{3,7},{4,0},{5,1},{6,2},{7,3},{8,12},{9,13},{10,... | collective-permute-start | bytes 786440 | tf_op jit(solution)/shard_map/ppermute | solution.py:158
  5.9 12.1 %collective-permute-start.2 = (bf16[2,128,512]{2,1,0:T(8,128)(2,1)S(1)}, bf16[2,128,512]{2,1,0:T(8,128)(2,1)S(1)}, u32[]{:S(2)}, u32[]{:S(2)}) collective-permute-start(bf16[2,128,512]{2,1,0:T(8,128)(2,1)S(1)} %pad_maximum_fusion.1.refs_3_), channel_id=1, source_target_pairs={{0,12},{1,13},{2,14},{3,15},{4,8},{5,9},{6,10},{7,11},{8,4},{9,5},... | collective-permute-start | bytes 786440 | tf_op jit(solution)/shard_map/ppermute | solution.py:158
  13.0 5.5 %collective-permute-start.5 = (bf16[2,128,512]{2,1,0:T(8,128)(2,1)S(1)}, bf16[2,128,512]{2,1,0:T(8,128)(2,1)S(1)}, u32[]{:S(2)}, u32[]{:S(2)}) collective-permute-start(bf16[2,128,512]{2,1,0:T(8,128)(2,1)S(1)} %collective-permute-done.3.refs_3_), channel_id=1, source_target_pairs={{0,2},{1,3},{2,0},{3,1},{4,6},{5,7},{6,4},{7,5},{8,10},{9,11},{10,... | collective-permute-start | bytes 786440 | tf_op jit(solution)/shard_map/ppermute | solution.py:158
  13.5 2.5 %copy-start = (bf16[10,512,512]{2,1,0:T(8,128)(2,1)S(1)}, bf16[10,512,512]{2,1,0:T(8,128)(2,1)}, u32[]{:S(2)}) copy-start(bf16[10,512,512]{2,1,0:T(8,128)(2,1)} %refs_5_.7) | copy-start | bytes 15728644
  18.6 22.2 %collective-permute-start.10 = (bf16[10,512,512]{2,1,0:T(8,128)(2,1)}, bf16[10,512,512]{2,1,0:T(8,128)(2,1)}, u32[]{:S(2)}, u32[]{:S(2)}) collective-permute-start(bf16[10,512,512]{2,1,0:T(8,128)(2,1)} %refs_4_.7), channel_id=1, source_target_pairs={{0,1},{1,0},{2,3},{3,2},{4,5},{5,4},{6,7},{7,6},{8,9},{9,8},{10,11... | collective-permute-start | bytes 15728648 | tf_op jit(solution)/shard_map/ppermute | solution.py:158
  21.9 7.9 %collective-permute-start.7 = (bf16[2,128,512]{2,1,0:T(8,128)(2,1)S(1)}, bf16[2,128,512]{2,1,0:T(8,128)(2,1)S(1)}, u32[]{:S(2)}, u32[]{:S(2)}) collective-permute-start(bf16[2,128,512]{2,1,0:T(8,128)(2,1)S(1)} %collective-permute-done.2.refs_3_), channel_id=1, source_target_pairs={{0,4},{1,5},{2,6},{3,7},{4,0},{5,1},{6,2},{7,3},{8,12},{9,13},{10,... | collective-permute-start | bytes 786440 | tf_op jit(solution)/shard_map/ppermute | solution.py:158
  22.4 8.6 %collective-permute-start.9 = (bf16[2,128,512]{2,1,0:T(8,128)(2,1)S(1)}, bf16[2,128,512]{2,1,0:T(8,128)(2,1)S(1)}, u32[]{:S(2)}, u32[]{:S(2)}) collective-permute-start(bf16[2,128,512]{2,1,0:T(8,128)(2,1)S(1)} %collective-permute-done.2.refs_3_), channel_id=1, source_target_pairs={{0,2},{1,3},{2,0},{3,1},{4,6},{5,7},{6,4},{7,5},{8,10},{9,11},{10,... | collective-permute-start | bytes 786440 | tf_op jit(solution)/shard_map/ppermute | solution.py:158
  29.9 7.7 %collective-permute-start.8 = (bf16[2,128,512]{2,1,0:T(8,128)(2,1)S(1)}, bf16[2,128,512]{2,1,0:T(8,128)(2,1)S(1)}, u32[]{:S(2)}, u32[]{:S(2)}) collective-permute-start(bf16[2,128,512]{2,1,0:T(8,128)(2,1)S(1)} %collective-permute-done.7.refs_3_), channel_id=1, source_target_pairs={{0,2},{1,3},{2,0},{3,1},{4,6},{5,7},{6,4},{7,5},{8,10},{9,11},{10,... | collective-permute-start | bytes 786440 | tf_op jit(solution)/shard_map/ppermute | solution.py:158
  31.1 2.5 %copy-start.1 = (bf16[10,512,512]{2,1,0:T(8,128)(2,1)S(1)}, bf16[10,512,512]{2,1,0:T(8,128)(2,1)}, u32[]{:S(2)}) copy-start(bf16[10,512,512]{2,1,0:T(8,128)(2,1)} %refs_5_.7) | copy-start | bytes 15728644
  43.9 8.8 %collective-permute-start.11 = (bf16[2,128,512]{2,1,0:T(8,128)(2,1)S(1)}, bf16[2,128,512]{2,1,0:T(8,128)(2,1)S(1)}, u32[]{:S(2)}, u32[]{:S(2)}) collective-permute-start(bf16[2,128,512]{2,1,0:T(8,128)(2,1)S(1)} %bitcast.32), channel_id=1, source_target_pairs={{0,2},{1,3},{2,0},{3,1},{4,6},{5,7},{6,4},{7,5},{8,10},{9,11},{10,... | collective-permute-start | bytes 786440 | tf_op jit(solution)/shard_map/ppermute | solution.py:158
  50.1 13.6 %collective-permute-start.13 = (bf16[2,128,512]{2,1,0:T(8,128)(2,1)S(1)}, bf16[2,128,512]{2,1,0:T(8,128)(2,1)S(1)}, u32[]{:S(2)}, u32[]{:S(2)}) collective-permute-start(bf16[2,128,512]{2,1,0:T(8,128)(2,1)S(1)} %bitcast.30), channel_id=1, source_target_pairs={{0,2},{1,3},{2,0},{3,1},{4,6},{5,7},{6,4},{7,5},{8,10},{9,11},{10,... | collective-permute-start | bytes 786440 | tf_op jit(solution)/shard_map/ppermute | solution.py:158
  52.8 10.9 %collective-permute-start.14 = (bf16[2,128,512]{2,1,0:T(8,128)(2,1)S(1)}, bf16[2,128,512]{2,1,0:T(8,128)(2,1)S(1)}, u32[]{:S(2)}, u32[]{:S(2)}) collective-permute-start(bf16[2,128,512]{2,1,0:T(8,128)(2,1)S(1)} %add_convert_fusion.2), channel_id=1, source_target_pairs={{0,4},{1,5},{2,6},{3,7},{4,0},{5,1},{6,2},{7,3},{8,12},{9,13},{10,... | collective-permute-start | bytes 786440 | tf_op jit(solution)/shard_map/ppermute | solution.py:158
  57.6 13.5 %collective-permute-start.16 = (bf16[2,128,512]{2,1,0:T(8,128)(2,1)S(1)}, bf16[2,128,512]{2,1,0:T(8,128)(2,1)S(1)}, u32[]{:S(2)}, u32[]{:S(2)}) collective-permute-start(bf16[2,128,512]{2,1,0:T(8,128)(2,1)S(1)} %bitcast.31), channel_id=1, source_target_pairs={{0,2},{1,3},{2,0},{3,1},{4,6},{5,7},{6,4},{7,5},{8,10},{9,11},{10,... | collective-permute-start | bytes 786440 | tf_op jit(solution)/shard_map/ppermute | solution.py:158
  62.7 10.1 %collective-permute-start.12 = (bf16[2,128,512]{2,1,0:T(8,128)(2,1)S(1)}, bf16[2,128,512]{2,1,0:T(8,128)(2,1)S(1)}, u32[]{:S(2)}, u32[]{:S(2)}) collective-permute-start(bf16[2,128,512]{2,1,0:T(8,128)(2,1)S(1)} %bitcast.29), channel_id=1, source_target_pairs={{0,2},{1,3},{2,0},{3,1},{4,6},{5,7},{6,4},{7,5},{8,10},{9,11},{10,... | collective-permute-start | bytes 786440 | tf_op jit(solution)/shard_map/ppermute | solution.py:158
  63.8 15.5 %collective-permute-start.15 = (bf16[2,128,512]{2,1,0:T(8,128)(2,1)S(1)}, bf16[2,128,512]{2,1,0:T(8,128)(2,1)S(1)}, u32[]{:S(2)}, u32[]{:S(2)}) collective-permute-start(bf16[2,128,512]{2,1,0:T(8,128)(2,1)S(1)} %add_convert_fusion.1), channel_id=1, source_target_pairs={{0,12},{1,13},{2,14},{3,15},{4,8},{5,9},{6,10},{7,11},{8,4},{9,5},... | collective-permute-start | bytes 786440 | tf_op jit(solution)/shard_map/ppermute | solution.py:158
  71.2 9.0 %collective-permute-start.17 = (bf16[2,128,512]{2,1,0:T(8,128)(2,1)S(1)}, bf16[2,128,512]{2,1,0:T(8,128)(2,1)S(1)}, u32[]{:S(2)}, u32[]{:S(2)}) collective-permute-start(bf16[2,128,512]{2,1,0:T(8,128)(2,1)S(1)} %add_convert_fusion), channel_id=1, source_target_pairs={{0,4},{1,5},{2,6},{3,7},{4,0},{5,1},{6,2},{7,3},{8,12},{9,13},{10,... | collective-permute-start | bytes 786440 | tf_op jit(solution)/shard_map/ppermute | solution.py:158
  80.4 6.7 %collective-permute-start.18 = (f32[128,512]{1,0:T(8,128)S(1)}, f32[128,512]{1,0:T(8,128)S(1)}, u32[]{:S(2)}, u32[]{:S(2)}) collective-permute-start(f32[128,512]{1,0:T(8,128)S(1)} %slice_bitcast_fusion), channel_id=1, source_target_pairs={{0,1},{1,0},{2,3},{3,2},{4,5},{5,4},{6,7},{7,6},{8,9},{9,8},{10,11... | collective-permute-start | bytes 786440 | tf_op jit(solution)/shard_map/ppermute | solution.py:158

commit v3 on v2

--- a/solution.py
+++ b/solution.py
@@ -9,7 +9,7 @@
 
 F32, BF16 = jnp.float32, jnp.bfloat16
 CORES = 2
-VMEM = 48 * 1024 * 1024
+VMEM = 16 * 1024 * 1024
 ANY = pl.BlockSpec(memory_space=pl.ANY)
 SMEM = pl.BlockSpec(memory_space=pltpu.SMEM)
 WHOLE = pl.BlockSpec(memory_space=pltpu.VMEM)
@@ -176,8 +176,11 @@
     own_block = jnp.stack([mine, from_sib])
     mirror_block = move(own_block, mirror)
     beside_block, own_bands = lax.optimization_barrier((move(own_block, beside), bands_of(own_block)))
-    beside_bands = bands_of(beside_block)
-    blocks = [(own_block, own_bands), None, None, None]
+    far_block = move(mirror_block, beside)
+    mirror_block, beside_bands, right_sib = lax.optimization_barrier((mirror_block, bands_of(beside_block), right))
+    right_sib = move(right_sib, flip=True)
+    mirror_bands = bands_of(mirror_block)
+    blocks = [(own_block, own_bands), (beside_block, beside_bands), None, None]
     partner = plane ^ 1
     where_src = jnp.stack([plane, partner, 3 - plane, 3 - partner, band, core]).astype(jnp.int32)
     where_dst = jnp.stack([3 - partner, 3 - plane, partner, plane, band, core]).astype(jnp.int32)
@@ -189,16 +192,8 @@
     mixed = None
     for phase in range(sectors):
         if phase == 1:
-            mirror_block, right_sib, beside_bands, token = lax.optimization_barrier(
-                (mirror_block, right, beside_bands, token)
-            )
-            right_sib = move(right_sib, flip=True)
-            blocks[1] = (beside_block, beside_bands)
-            blocks[2] = (mirror_block, bands_of(mirror_block))
-            far_block = move(mirror_block, beside)
-        if phase == 2:
-            far_block, token = lax.optimization_barrier((far_block, token))
-            blocks[3] = (far_block, bands_of(far_block))
+            far_block, mirror_bands, token = lax.optimization_barrier((far_block, mirror_bands, token))
+            blocks[2:] = [(mirror_block, mirror_bands), (far_block, bands_of(far_block))]
         operands = [own_meta, sib_meta, where_src, *blocks[phase], left, left_sib]
         if mixed is not None:
             operands += [mixed, token]

time: 88.4 us -> 104 us (1.18); the launches traced: 87.9 us -> 105 us
  local copies, waits for them, and re-layouts: 6.15 us -> 22.2 us
  waiting for transfers between devices: 20.4 us -> 28.1 us
  Pallas kernels: 27 us -> 23.2 us
  starting transfers between devices: 31.5 us -> 28.2 us
    unnamed x4 -> x16, local copies, waits for them, and re-layouts: 4.98 us -> 21 us
    ppermute x19, waiting for transfers between devices: 20.4 us -> 28.1 us  [move(): return lax.ppermute(value, 'term', pairs)]
    ppermute x19, starting transfers between devices: 31.5 us -> 28.2 us  [move(): return lax.ppermute(value, 'term', pairs)]
    pallas_call x4, Pallas kernels: 14 us -> 10.9 us  [right_mix(): pl.pallas_call(functools.partial(right_kernel, phase), out_shape=(jax.Sha...]
  transfers between devices with their start and end apart: 19 -> 19, of which waited for: 9 -> 8; matrix products, arithmetic and copies ran while one was open for 1% -> 1% of each run, Pallas kernels for 27% -> 20%
where the time goes in v3:
time: 104 us; the launch traced here: 105 us
  starting transfers between devices  28.2 us (27%)
  waiting for transfers between devices  28.1 us (27%)
  Pallas kernels  23.2 us (22%)
  local copies, waits for them, and re-layouts  22.2 us (21%)
  other arithmetic  2.02 us (2%)
    ppermute x19, starting transfers between devices, move(): return lax.ppermute(value, 'term', pairs)  28.2 us
    ppermute x19, waiting for transfers between devices, move(): return lax.ppermute(value, 'term', pairs)  28.1 us
    unnamed x16, local copies, waits for them, and re-layouts  21 us
    pallas_call x4, Pallas kernels, local(): pl.pallas_call(functools.partial(left_kernel, phase), out_shape=(jax.Shap...  12.4 us
    pallas_call x4, Pallas kernels, right_mix(): pl.pallas_call(functools.partial(right_kernel, phase), out_shape=(jax.Sha...  10.9 us
  transfers between devices with their start and end apart: 19, of which 8 were waited for; matrix products, arithmetic and copies ran while one was open for 1% of the time, Pallas kernels for 20%

profile of v3, /device:TPU:13, one launch (start us, length us, event | category | flops | bytes accessed | tf_op | source)
XLA Modules:
  0.0 104.6 jit_solution(8220780453567162746)
XLA Ops:
  0.0 1.0 dynamic-slice_bitcast_fusion
  1.0 0.7 collective-permute-start
  2.4 0.7 pad_add_fusion.refs_0_
  3.1 0.0 collective-permute-start.1
  3.1 1.1 %collective-permute-done.1.refs_1_ = s32[21]{0:T(128)S(1)} collective-permute-done((s32[21]{0:T(128)S(1)}, s32[21]{0:T(128)S(1)}, u32[]{:S(2)}, u32[]{:S(2)}) %collective-permute-start.1) | collective-permute-done | bytes 116 | tf_op jit(solution)/shard_map/ppermute | solution.py:158
  4.3 0.0 collective-permute-done
  4.3 1.3 %collective-permute-start.5 = (bf16[2,128,512]{2,1,0:T(8,128)(2,1)S(1)}, bf16[2,128,512]{2,1,0:T(8,128)(2,1)S(1)}, u32[]{:S(2)}, u32[]{:S(2)}) collective-permute-start(bf16[2,128,512]{2,1,0:T(8,128)(2,1)S(1)} %pad_maximum_fusion.1.refs_3_), channel_id=1, source_target_pairs={{0,2},{1,3},{2,0},{3,1},{4,6},{5,7},{6,4},{7,5},{8,10},{9,11},{10,... | collective-permute-start | bytes 786440 | tf_op jit(solution)/shard_map/ppermute | solution.py:158
  5.6 0.2 collective-permute-start.4
  5.7 0.8 collective-permute-start.8
  6.5 2.4 %collective-permute-start.2 = (bf16[2,128,512]{2,1,0:T(8,128)(2,1)S(1)}, bf16[2,128,512]{2,1,0:T(8,128)(2,1)S(1)}, u32[]{:S(2)}, u32[]{:S(2)}) collective-permute-start(bf16[2,128,512]{2,1,0:T(8,128)(2,1)S(1)} %pad_maximum_fusion.1.refs_3_), channel_id=1, source_target_pairs={{0,12},{1,13},{2,14},{3,15},{4,8},{5,9},{6,10},{7,11},{8,4},{9,5},... | collective-permute-start | bytes 786440 | tf_op jit(solution)/shard_map/ppermute | solution.py:158
  8.9 3.1 %collective-permute-done.5 = bf16[2,128,512]{2,1,0:T(8,128)(2,1)S(1)} collective-permute-done((bf16[2,128,512]{2,1,0:T(8,128)(2,1)S(1)}, bf16[2,128,512]{2,1,0:T(8,128)(2,1)S(1)}, u32[]{:S(2)}, u32[]{:S(2)}) %collective-permute-start.5) | collective-permute-done | bytes 262176 | tf_op jit(solution)/shard_map/ppermute | solution.py:158
  12.1 0.9 collective-permute-done.4.refs_3_
  13.0 0.3 collective-permute-start.6
  13.3 7.9 %collective-permute-done.2.refs_3_ = bf16[2,128,512]{2,1,0:T(8,128)(2,1)S(1)} collective-permute-done((bf16[2,128,512]{2,1,0:T(8,128)(2,1)S(1)}, bf16[2,128,512]{2,1,0:T(8,128)(2,1)S(1)}, u32[]{:S(2)}, u32[]{:S(2)}) %collective-permute-start.2) | collective-permute-done | bytes 262176 | tf_op jit(solution)/shard_map/ppermute | solution.py:158
  21.2 0.0 collective-permute-done.6
  21.2 0.6 collective-permute-start.10
  21.8 0.4 collective-permute-start.3
  22.2 0.3 collective-permute-start.7
  22.5 0.1 stack.58.refs_2_
  22.5 0.0 collective-permute-done.8.refs_6_
  22.6 2.5 %copy-done.4 = bf16[10,512,512]{2,1,0:T(8,128)(2,1)S(1)} copy-done((bf16[10,512,512]{2,1,0:T(8,128)(2,1)S(1)}, bf16[10,512,512]{2,1,0:T(8,128)(2,1)}, u32[]{:S(2)}) %copy-start.4) | copy-done | bytes 5242904
  25.0 2.9 %left_mix.4 = (bf16[20,512,512]{2,1,0:T(8,128)(2,1)S(1)}, f32[8,128]{1,0:T(8,128)S(1)}) custom-call(s32[21]{0:T(128)S(1)} %pad_add_fusion.refs_0_, s32[21]{0:T(128)S(1)} %collective-permute-done.1.refs_1_, s32[6]{0:T(128)S(1)} %stack.58.refs_2_, bf16[2,128,512]{2,1,0:T(8,128)(2,1)S(1)} %pad_maximum_fusion.1.refs_3_, bf16[1,2,128,512]{3,2,1,0:T(8,128)(2,1)S(1)} %bitcast.30, ...), custom_call_target="tpu_custom_call" | custom-call | flops 1000000 | bytes 512 | tf_op jit(solution)/shard_map/left_mix/pallas_call | solution.py:200
  28.0 0.0 copy-start
  28.0 4.0 %copy-done = bf16[20,512,512]{2,1,0:T(8,128)(2,1)} copy-done((bf16[20,512,512]{2,1,0:T(8,128)(2,1)}, bf16[20,512,512]{2,1,0:T(8,128)(2,1)S(1)}, u32[]{:S(2)}) %copy-start) | copy-done | bytes 10485784
  32.0 0.0 collective-permute-done.3.refs_3_
  32.0 0.0 collective-permute-done.7
  32.0 2.1 %collective-permute-start.9 = (bf16[2,128,512]{2,1,0:T(8,128)(2,1)S(1)}, bf16[2,128,512]{2,1,0:T(8,128)(2,1)S(1)}, u32[]{:S(2)}, u32[]{:S(2)}) collective-permute-start(bf16[2,128,512]{2,1,0:T(8,128)(2,1)S(1)} %collective-permute-done.3.refs_3_), channel_id=1, source_target_pairs={{0,2},{1,3},{2,0},{3,1},{4,6},{5,7},{6,4},{7,5},{8,10},{9,11},{10,... | collective-permute-start | bytes 786440 | tf_op jit(solution)/shard_map/ppermute | solution.py:158
  34.1 0.1 stack.57.refs_2_
  34.2 4.0 %copy-done.1 = bf16[20,512,512]{2,1,0:T(8,128)(2,1)S(1)} copy-done((bf16[20,512,512]{2,1,0:T(8,128)(2,1)S(1)}, bf16[20,512,512]{2,1,0:T(8,128)(2,1)}, u32[]{:S(2)}) %copy-start.1) | copy-done | bytes 10485784
  38.2 2.5 %copy-done.5 = bf16[10,512,512]{2,1,0:T(8,128)(2,1)S(1)} copy-done((bf16[10,512,512]{2,1,0:T(8,128)(2,1)S(1)}, bf16[10,512,512]{2,1,0:T(8,128)(2,1)}, u32[]{:S(2)}) %copy-start.5) | copy-done | bytes 5242904
  40.6 3.0 %left_mix.5 = (bf16[20,512,512]{2,1,0:T(8,128)(2,1)S(1)}, f32[8,128]{1,0:T(8,128)S(1)}) custom-call(s32[21]{0:T(128)S(1)} %pad_add_fusion.refs_0_, s32[21]{0:T(128)S(1)} %collective-permute-done.1.refs_1_, s32[6]{0:T(128)S(1)} %stack.58.refs_2_, bf16[2,128,512]{2,1,0:T(8,128)(2,1)S(1)} %collective-permute-done.4.refs_3_, ...), custom_call_target="tpu_custom_call", output_to_operand_aliasing={{0}: (7, {})} | custom-call | flops 1000000 | bytes 512 | tf_op jit(solution)/shard_map/left_mix/pallas_call | solution.py:200
  43.7 0.0 slice-start
  43.7 3.4 %left_mix.6 = (bf16[20,512,512]{2,1,0:T(8,128)(2,1)S(1)}, f32[8,128]{1,0:T(8,128)S(1)}) custom-call(s32[21]{0:T(128)S(1)} %pad_add_fusion.refs_0_, s32[21]{0:T(128)S(1)} %collective-permute-done.1.refs_1_, s32[6]{0:T(128)S(1)} %stack.58.refs_2_, bf16[2,128,512]{2,1,0:T(8,128)(2,1)S(1)} %collective-permute-done.2.refs_3_, ...), custom_call_target="tpu_custom_call", output_to_operand_aliasing={{0}: (7, {})} | custom-call | flops 1000000 | bytes 512 | tf_op jit(solution)/shard_map/left_mix/pallas_call | solution.py:200
  47.1 0.0 collective-permute-done.9
  47.1 0.0 slice-start.1
  47.2 3.0 %left_mix.7 = (bf16[20,512,512]{2,1,0:T(8,128)(2,1)S(1)}, f32[8,128]{1,0:T(8,128)}) custom-call(s32[21]{0:T(128)S(1)} %pad_add_fusion.refs_0_, s32[21]{0:T(128)S(1)} %collective-permute-done.1.refs_1_, s32[6]{0:T(128)S(1)} %stack.58.refs_2_, bf16[2,128,512]{2,1,0:T(8,128)(2,1)S(1)} %collective-permute-done.3.refs_3_, ...), custom_call_target="tpu_custom_call", output_to_operand_aliasing={{0}: (7, {})} | custom-call | flops 1000000 | bytes 512 | tf_op jit(solution)/shard_map/left_mix/pallas_call | solution.py:200
  50.1 4.0 %copy-done.2 = bf16[20,512,512]{2,1,0:T(8,128)(2,1)} copy-done((bf16[20,512,512]{2,1,0:T(8,128)(2,1)}, bf16[20,512,512]{2,1,0:T(8,128)(2,1)S(1)}, u32[]{:S(2)}) %copy-start.2) | copy-done | bytes 10485784
  54.2 0.0 collective-permute-done.10.refs_5_
  54.2 4.0 %copy-done.3 = bf16[20,512,512]{2,1,0:T(8,128)(2,1)S(1)} copy-done((bf16[20,512,512]{2,1,0:T(8,128)(2,1)S(1)}, bf16[20,512,512]{2,1,0:T(8,128)(2,1)}, u32[]{:S(2)}) %copy-start.3) | copy-done | bytes 10485784
  58.2 2.3 %right_mix.4 = (f32[2,128,512]{2,1,0:T(8,128)S(1)}, bf16[1,2,128,512]{3,2,1,0:T(8,128)(2,1)S(1)}) custom-call(s32[21]{0:T(128)S(1)} %pad_add_fusion.refs_0_, s32[21]{0:T(128)S(1)} %collective-permute-done.1.refs_1_, s32[6]{0:T(128)S(1)} %stack.57.refs_2_, bf16[20,512,512]{2,1,0:T(8,128)(2,1)S(1)} %copy-done.3, bf16[10,512,512]{2,1,0:T(8,128)(2,1)S(1)} %bitcast.26, ...), custom_call_target="tpu_custom_call" | custom-call | flops 3000000000 | bytes 3670016 | tf_op jit(solution)/shard_map/right_mix/pallas_call | solution.py:223
  60.5 2.8 %collective-permute-start.11 = (bf16[2,128,512]{2,1,0:T(8,128)(2,1)S(1)}, bf16[2,128,512]{2,1,0:T(8,128)(2,1)S(1)}, u32[]{:S(2)}, u32[]{:S(2)}) collective-permute-start(bf16[2,128,512]{2,1,0:T(8,128)(2,1)S(1)} %bitcast.34), channel_id=1, source_target_pairs={{0,2},{1,3},{2,0},{3,1},{4,6},{5,7},{6,4},{7,5},{8,10},{9,11},{10,... | collective-permute-start | bytes 786440 | tf_op jit(solution)/shard_map/ppermute | solution.py:158
  63.3 3.5 %right_mix.6 = (f32[2,128,512]{2,1,0:T(8,128)S(1)}, bf16[1,2,128,512]{3,2,1,0:T(8,128)(2,1)S(1)}) custom-call(s32[21]{0:T(128)S(1)} %pad_add_fusion.refs_0_, s32[21]{0:T(128)S(1)} %collective-permute-done.1.refs_1_, s32[6]{0:T(128)S(1)} %stack.57.refs_2_, bf16[20,512,512]{2,1,0:T(8,128)(2,1)S(1)} %copy-done.3, bf16[10,512,512]{2,1,0:T(8,128)(2,1)S(1)} %bitcast.26, ...), custom_call_target="tpu_custom_call" | custom-call | flops 3000000000 | bytes 3670016 | tf_op jit(solution)/shard_map/right_mix/pallas_call | solution.py:223
  66.8 0.1 collective-permute-start.13
  66.9 1.8 %collective-permute-done.11 = bf16[2,128,512]{2,1,0:T(8,128)(2,1)S(1)} collective-permute-done((bf16[2,128,512]{2,1,0:T(8,128)(2,1)S(1)}, bf16[2,128,512]{2,1,0:T(8,128)(2,1)S(1)}, u32[]{:S(2)}, u32[]{:S(2)}) %collective-permute-start.11) | collective-permute-done | bytes 262176 | tf_op jit(solution)/shard_map/ppermute | solution.py:158
  68.8 0.1 add_convert_fusion.2
  68.8 0.1 collective-permute-start.14
  68.9 3.2 %right_mix.7 = (f32[2,128,512]{2,1,0:T(8,128)S(1)}, bf16[1,2,128,512]{3,2,1,0:T(8,128)(2,1)S(1)}) custom-call(s32[21]{0:T(128)S(1)} %pad_add_fusion.refs_0_, s32[21]{0:T(128)S(1)} %collective-permute-done.1.refs_1_, s32[6]{0:T(128)S(1)} %stack.57.refs_2_, bf16[20,512,512]{2,1,0:T(8,128)(2,1)S(1)} %copy-done.3, bf16[10,512,512]{2,1,0:T(8,128)(2,1)S(1)} %bitcast.26, ...), custom_call_target="tpu_custom_call" | custom-call | flops 3000000000 | bytes 3670016 | tf_op jit(solution)/shard_map/right_mix/pallas_call | solution.py:223
  72.1 1.8 %collective-permute-start.16 = (bf16[2,128,512]{2,1,0:T(8,128)(2,1)S(1)}, bf16[2,128,512]{2,1,0:T(8,128)(2,1)S(1)}, u32[]{:S(2)}, u32[]{:S(2)}) collective-permute-start(bf16[2,128,512]{2,1,0:T(8,128)(2,1)S(1)} %bitcast.33), channel_id=1, source_target_pairs={{0,2},{1,3},{2,0},{3,1},{4,6},{5,7},{6,4},{7,5},{8,10},{9,11},{10,... | collective-permute-start | bytes 786440 | tf_op jit(solution)/shard_map/ppermute | solution.py:158
  73.9 1.8 %right_mix.5 = (f32[2,128,512]{2,1,0:T(8,128)S(1)}, bf16[1,2,128,512]{3,2,1,0:T(8,128)(2,1)S(1)}) custom-call(s32[21]{0:T(128)S(1)} %pad_add_fusion.refs_0_, s32[21]{0:T(128)S(1)} %collective-permute-done.1.refs_1_, s32[6]{0:T(128)S(1)} %stack.57.refs_2_, bf16[20,512,512]{2,1,0:T(8,128)(2,1)S(1)} %copy-done.3, bf16[10,512,512]{2,1,0:T(8,128)(2,1)S(1)} %bitcast.26, ...), custom_call_target="tpu_custom_call" | custom-call | flops 3000000000 | bytes 3670016 | tf_op jit(solution)/shard_map/right_mix/pallas_call | solution.py:223
  75.7 2.6 %collective-permute-start.12 = (bf16[2,128,512]{2,1,0:T(8,128)(2,1)S(1)}, bf16[2,128,512]{2,1,0:T(8,128)(2,1)S(1)}, u32[]{:S(2)}, u32[]{:S(2)}) collective-permute-start(bf16[2,128,512]{2,1,0:T(8,128)(2,1)S(1)} %bitcast.31), channel_id=1, source_target_pairs={{0,2},{1,3},{2,0},{3,1},{4,6},{5,7},{6,4},{7,5},{8,10},{9,11},{10,... | collective-permute-start | bytes 786440 | tf_op jit(solution)/shard_map/ppermute | solution.py:158
  78.3 0.0 collective-permute-done.13
  78.3 0.0 collective-permute-done.14
  78.3 0.1 add_convert_fusion.1
  78.4 9.8 %collective-permute-start.15 = (bf16[2,128,512]{2,1,0:T(8,128)(2,1)S(1)}, bf16[2,128,512]{2,1,0:T(8,128)(2,1)S(1)}, u32[]{:S(2)}, u32[]{:S(2)}) collective-permute-start(bf16[2,128,512]{2,1,0:T(8,128)(2,1)S(1)} %add_convert_fusion.1), channel_id=1, source_target_pairs={{0,12},{1,13},{2,14},{3,15},{4,8},{5,9},{6,10},{7,11},{8,4},{9,5},... | collective-permute-start | bytes 786440 | tf_op jit(solution)/shard_map/ppermute | solution.py:158
  88.2 0.0 collective-permute-done.16
  88.2 0.1 add_convert_fusion
  88.3 1.7 %collective-permute-start.17 = (bf16[2,128,512]{2,1,0:T(8,128)(2,1)S(1)}, bf16[2,128,512]{2,1,0:T(8,128)(2,1)S(1)}, u32[]{:S(2)}, u32[]{:S(2)}) collective-permute-start(bf16[2,128,512]{2,1,0:T(8,128)(2,1)S(1)} %add_convert_fusion), channel_id=1, source_target_pairs={{0,4},{1,5},{2,6},{3,7},{4,0},{5,1},{6,2},{7,3},{8,12},{9,13},{10,... | collective-permute-start | bytes 786440 | tf_op jit(solution)/shard_map/ppermute | solution.py:158
  89.9 0.0 collective-permute-done.12
  89.9 10.7 %collective-permute-done.15 = bf16[2,128,512]{2,1,0:T(8,128)(2,1)S(1)} collective-permute-done((bf16[2,128,512]{2,1,0:T(8,128)(2,1)S(1)}, bf16[2,128,512]{2,1,0:T(8,128)(2,1)S(1)}, u32[]{:S(2)}, u32[]{:S(2)}) %collective-permute-start.15) | collective-permute-done | bytes 262176 | tf_op jit(solution)/shard_map/ppermute | solution.py:158
  100.6 1.4 %collective-permute-done.17 = bf16[2,128,512]{2,1,0:T(8,128)(2,1)S(1)} collective-permute-done((bf16[2,128,512]{2,1,0:T(8,128)(2,1)S(1)}, bf16[2,128,512]{2,1,0:T(8,128)(2,1)S(1)}, u32[]{:S(2)}, u32[]{:S(2)}) %collective-permute-start.17) | collective-permute-done | bytes 262176 | tf_op jit(solution)/shard_map/ppermute | solution.py:158
  102.0 0.1 convert_add_fusion
  102.1 0.5 collective-permute-start.18
  102.6 1.2 %collective-permute-done.18 = f32[128,512]{1,0:T(8,128)S(1)} collective-permute-done((f32[128,512]{1,0:T(8,128)S(1)}, f32[128,512]{1,0:T(8,128)S(1)}, u32[]{:S(2)}, u32[]{:S(2)}) %collective-permute-start.18) | collective-permute-done | bytes 262176 | tf_op jit(solution)/shard_map/ppermute | solution.py:158
  103.8 0.8 pad_maximum_fusion
  (11 shorter events, 0.1 us)
Async XLA Ops:
  1.0 3.3 %collective-permute-start = (bf16[128,512]{1,0:T(8,128)(2,1)S(1)}, bf16[128,512]{1,0:T(8,128)(2,1)S(1)}, u32[]{:S(2)}, u32[]{:S(2)}) collective-permute-start(bf16[128,512]{1,0:T(8,128)(2,1)S(1)} %get-tuple-element.64), channel_id=1, source_target_pairs={{0,1},{1,0},{2,3},{3,2},{4,5},{5,4},{6,7},{7,6},{8,9},{9,8},{10,11... | collective-permute-start | bytes 393224 | tf_op jit(solution)/shard_map/ppermute | solution.py:158
  3.1 1.1 %collective-permute-start.1 = (s32[21]{0:T(128)S(1)}, s32[21]{0:T(128)S(1)}, u32[]{:S(2)}, u32[]{:S(2)}) collective-permute-start(s32[21]{0:T(128)S(1)} %pad_add_fusion.refs_0_), channel_id=1, source_target_pairs={{0,1},{1,0},{2,3},{3,2},{4,5},{5,4},{6,7},{7,6},{8,9},{9,8},{10,11... | collective-permute-start | bytes 260 | tf_op jit(solution)/shard_map/ppermute | solution.py:158
  4.3 7.8 %collective-permute-start.5 = (bf16[2,128,512]{2,1,0:T(8,128)(2,1)S(1)}, bf16[2,128,512]{2,1,0:T(8,128)(2,1)S(1)}, u32[]{:S(2)}, u32[]{:S(2)}) collective-permute-start(bf16[2,128,512]{2,1,0:T(8,128)(2,1)S(1)} %pad_maximum_fusion.1.refs_3_), channel_id=1, source_target_pairs={{0,2},{1,3},{2,0},{3,1},{4,6},{5,7},{6,4},{7,5},{8,10},{9,11},{10,... | collective-permute-start | bytes 786440 | tf_op jit(solution)/shard_map/ppermute | solution.py:158
  5.6 7.4 %collective-permute-start.4 = (bf16[2,128,512]{2,1,0:T(8,128)(2,1)S(1)}, bf16[2,128,512]{2,1,0:T(8,128)(2,1)S(1)}, u32[]{:S(2)}, u32[]{:S(2)}) collective-permute-start(bf16[2,128,512]{2,1,0:T(8,128)(2,1)S(1)} %pad_maximum_fusion.1.refs_3_), channel_id=1, source_target_pairs={{0,4},{1,5},{2,6},{3,7},{4,0},{5,1},{6,2},{7,3},{8,12},{9,13},{10,... | collective-permute-start | bytes 786440 | tf_op jit(solution)/shard_map/ppermute | solution.py:158
  5.7 16.8 %collective-permute-start.8 = (bf16[10,512,512]{2,1,0:T(8,128)(2,1)}, bf16[10,512,512]{2,1,0:T(8,128)(2,1)}, u32[]{:S(2)}, u32[]{:S(2)}) collective-permute-start(bf16[10,512,512]{2,1,0:T(8,128)(2,1)} %refs_5_.7), channel_id=1, source_target_pairs={{0,1},{1,0},{2,3},{3,2},{4,5},{5,4},{6,7},{7,6},{8,9},{9,8},{10,11... | collective-permute-start | bytes 15728648 | tf_op jit(solution)/shard_map/ppermute | solution.py:158
  6.5 14.7 %collective-permute-start.2 = (bf16[2,128,512]{2,1,0:T(8,128)(2,1)S(1)}, bf16[2,128,512]{2,1,0:T(8,128)(2,1)S(1)}, u32[]{:S(2)}, u32[]{:S(2)}) collective-permute-start(bf16[2,128,512]{2,1,0:T(8,128)(2,1)S(1)} %pad_maximum_fusion.1.refs_3_), channel_id=1, source_target_pairs={{0,12},{1,13},{2,14},{3,15},{4,8},{5,9},{6,10},{7,11},{8,4},{9,5},... | collective-permute-start | bytes 786440 | tf_op jit(solution)/shard_map/ppermute | solution.py:158
  13.0 8.3 %collective-permute-start.6 = (bf16[2,128,512]{2,1,0:T(8,128)(2,1)S(1)}, bf16[2,128,512]{2,1,0:T(8,128)(2,1)S(1)}, u32[]{:S(2)}, u32[]{:S(2)}) collective-permute-start(bf16[2,128,512]{2,1,0:T(8,128)(2,1)S(1)} %collective-permute-done.4.refs_3_), channel_id=1, source_target_pairs={{0,2},{1,3},{2,0},{3,1},{4,6},{5,7},{6,4},{7,5},{8,10},{9,11},{10,... | collective-permute-start | bytes 786440 | tf_op jit(solution)/shard_map/ppermute | solution.py:158
  21.2 32.9 %collective-permute-start.10 = (bf16[10,512,512]{2,1,0:T(8,128)(2,1)}, bf16[10,512,512]{2,1,0:T(8,128)(2,1)}, u32[]{:S(2)}, u32[]{:S(2)}) collective-permute-start(bf16[10,512,512]{2,1,0:T(8,128)(2,1)} %refs_4_.7), channel_id=1, source_target_pairs={{0,1},{1,0},{2,3},{3,2},{4,5},{5,4},{6,7},{7,6},{8,9},{9,8},{10,11... | collective-permute-start | bytes 15728648 | tf_op jit(solution)/shard_map/ppermute | solution.py:158
  21.8 10.2 %collective-permute-start.3 = (bf16[2,128,512]{2,1,0:T(8,128)(2,1)S(1)}, bf16[2,128,512]{2,1,0:T(8,128)(2,1)S(1)}, u32[]{:S(2)}, u32[]{:S(2)}) collective-permute-start(bf16[2,128,512]{2,1,0:T(8,128)(2,1)S(1)} %collective-permute-done.2.refs_3_), channel_id=1, source_target_pairs={{0,4},{1,5},{2,6},{3,7},{4,0},{5,1},{6,2},{7,3},{8,12},{9,13},{10,... | collective-permute-start | bytes 786440 | tf_op jit(solution)/shard_map/ppermute | solution.py:158
  22.2 9.8 %collective-permute-start.7 = (bf16[2,128,512]{2,1,0:T(8,128)(2,1)S(1)}, bf16[2,128,512]{2,1,0:T(8,128)(2,1)S(1)}, u32[]{:S(2)}, u32[]{:S(2)}) collective-permute-start(bf16[2,128,512]{2,1,0:T(8,128)(2,1)S(1)} %collective-permute-done.2.refs_3_), channel_id=1, source_target_pairs={{0,2},{1,3},{2,0},{3,1},{4,6},{5,7},{6,4},{7,5},{8,10},{9,11},{10,... | collective-permute-start | bytes 786440 | tf_op jit(solution)/shard_map/ppermute | solution.py:158
  22.6 2.5 %copy-start.4 = (bf16[10,512,512]{2,1,0:T(8,128)(2,1)S(1)}, bf16[10,512,512]{2,1,0:T(8,128)(2,1)}, u32[]{:S(2)}) copy-start(bf16[10,512,512]{2,1,0:T(8,128)(2,1)} %refs_5_.7) | copy-start | bytes 15728644
  28.0 4.0 %copy-start = (bf16[20,512,512]{2,1,0:T(8,128)(2,1)}, bf16[20,512,512]{2,1,0:T(8,128)(2,1)S(1)}, u32[]{:S(2)}) copy-start(bf16[20,512,512]{2,1,0:T(8,128)(2,1)S(1)} %get-tuple-element.43.refs_7_) | copy-start | bytes 31457284
  32.0 15.1 %collective-permute-start.9 = (bf16[2,128,512]{2,1,0:T(8,128)(2,1)S(1)}, bf16[2,128,512]{2,1,0:T(8,128)(2,1)S(1)}, u32[]{:S(2)}, u32[]{:S(2)}) collective-permute-start(bf16[2,128,512]{2,1,0:T(8,128)(2,1)S(1)} %collective-permute-done.3.refs_3_), channel_id=1, source_target_pairs={{0,2},{1,3},{2,0},{3,1},{4,6},{5,7},{6,4},{7,5},{8,10},{9,11},{10,... | collective-permute-start | bytes 786440 | tf_op jit(solution)/shard_map/ppermute | solution.py:158
  34.2 4.0 %copy-start.1 = (bf16[20,512,512]{2,1,0:T(8,128)(2,1)S(1)}, bf16[20,512,512]{2,1,0:T(8,128)(2,1)}, u32[]{:S(2)}) copy-start(bf16[20,512,512]{2,1,0:T(8,128)(2,1)} %copy-done) | copy-start | bytes 31457284
  38.2 2.5 %copy-start.5 = (bf16[10,512,512]{2,1,0:T(8,128)(2,1)S(1)}, bf16[10,512,512]{2,1,0:T(8,128)(2,1)}, u32[]{:S(2)}) copy-start(bf16[10,512,512]{2,1,0:T(8,128)(2,1)} %refs_5_.7) | copy-start | bytes 15728644
  43.7 10.5 %slice-start = ((s8[5242880]{0:T(1024)(128)(4,1)}), s8[4194304]{0:T(1024)(128)(4,1)S(1)}, s32[]{:S(2)}) async-start(s8[5242880]{0:T(1024)(128)(4,1)} %bitcast.25), calls=%async_computation | async-start | bytes 8388608
  47.1 7.0 %slice-start.1 = ((s8[5242880]{0:T(1024)(128)(4,1)}), s8[1048576]{0:T(1024)(128)(4,1)S(1)}, s32[]{:S(2)}) async-start(s8[5242880]{0:T(1024)(128)(4,1)} %bitcast.25), calls=%async_computation.1 | async-start | bytes 2097152
  50.1 4.0 %copy-start.2 = (bf16[20,512,512]{2,1,0:T(8,128)(2,1)}, bf16[20,512,512]{2,1,0:T(8,128)(2,1)S(1)}, u32[]{:S(2)}) copy-start(bf16[20,512,512]{2,1,0:T(8,128)(2,1)S(1)} %get-tuple-element.49.refs_3_) | copy-start | bytes 31457284
  54.2 4.0 %copy-start.3 = (bf16[20,512,512]{2,1,0:T(8,128)(2,1)S(1)}, bf16[20,512,512]{2,1,0:T(8,128)(2,1)}, u32[]{:S(2)}) copy-start(bf16[20,512,512]{2,1,0:T(8,128)(2,1)} %copy-done.2) | copy-start | bytes 31457284
  60.5 8.3 %collective-permute-start.11 = (bf16[2,128,512]{2,1,0:T(8,128)(2,1)S(1)}, bf16[2,128,512]{2,1,0:T(8,128)(2,1)S(1)}, u32[]{:S(2)}, u32[]{:S(2)}) collective-permute-start(bf16[2,128,512]{2,1,0:T(8,128)(2,1)S(1)} %bitcast.34), channel_id=1, source_target_pairs={{0,2},{1,3},{2,0},{3,1},{4,6},{5,7},{6,4},{7,5},{8,10},{9,11},{10,... | collective-permute-start | bytes 786440 | tf_op jit(solution)/shard_map/ppermute | solution.py:158
  66.8 11.4 %collective-permute-start.13 = (bf16[2,128,512]{2,1,0:T(8,128)(2,1)S(1)}, bf16[2,128,512]{2,1,0:T(8,128)(2,1)S(1)}, u32[]{:S(2)}, u32[]{:S(2)}) collective-permute-start(bf16[2,128,512]{2,1,0:T(8,128)(2,1)S(1)} %bitcast.32), channel_id=1, source_target_pairs={{0,2},{1,3},{2,0},{3,1},{4,6},{5,7},{6,4},{7,5},{8,10},{9,11},{10,... | collective-permute-start | bytes 786440 | tf_op jit(solution)/shard_map/ppermute | solution.py:158
  68.8 9.4 %collective-permute-start.14 = (bf16[2,128,512]{2,1,0:T(8,128)(2,1)S(1)}, bf16[2,128,512]{2,1,0:T(8,128)(2,1)S(1)}, u32[]{:S(2)}, u32[]{:S(2)}) collective-permute-start(bf16[2,128,512]{2,1,0:T(8,128)(2,1)S(1)} %add_convert_fusion.2), channel_id=1, source_target_pairs={{0,4},{1,5},{2,6},{3,7},{4,0},{5,1},{6,2},{7,3},{8,12},{9,13},{10,... | collective-permute-start | bytes 786440 | tf_op jit(solution)/shard_map/ppermute | solution.py:158
  72.1 16.1 %collective-permute-start.16 = (bf16[2,128,512]{2,1,0:T(8,128)(2,1)S(1)}, bf16[2,128,512]{2,1,0:T(8,128)(2,1)S(1)}, u32[]{:S(2)}, u32[]{:S(2)}) collective-permute-start(bf16[2,128,512]{2,1,0:T(8,128)(2,1)S(1)} %bitcast.33), channel_id=1, source_target_pairs={{0,2},{1,3},{2,0},{3,1},{4,6},{5,7},{6,4},{7,5},{8,10},{9,11},{10,... | collective-permute-start | bytes 786440 | tf_op jit(solution)/shard_map/ppermute | solution.py:158
  75.7 14.2 %collective-permute-start.12 = (bf16[2,128,512]{2,1,0:T(8,128)(2,1)S(1)}, bf16[2,128,512]{2,1,0:T(8,128)(2,1)S(1)}, u32[]{:S(2)}, u32[]{:S(2)}) collective-permute-start(bf16[2,128,512]{2,1,0:T(8,128)(2,1)S(1)} %bitcast.31), channel_id=1, source_target_pairs={{0,2},{1,3},{2,0},{3,1},{4,6},{5,7},{6,4},{7,5},{8,10},{9,11},{10,... | collective-permute-start | bytes 786440 | tf_op jit(solution)/shard_map/ppermute | solution.py:158
  78.4 22.2 %collective-permute-start.15 = (bf16[2,128,512]{2,1,0:T(8,128)(2,1)S(1)}, bf16[2,128,512]{2,1,0:T(8,128)(2,1)S(1)}, u32[]{:S(2)}, u32[]{:S(2)}) collective-permute-start(bf16[2,128,512]{2,1,0:T(8,128)(2,1)S(1)} %add_convert_fusion.1), channel_id=1, source_target_pairs={{0,12},{1,13},{2,14},{3,15},{4,8},{5,9},{6,10},{7,11},{8,4},{9,5},... | collective-permute-start | bytes 786440 | tf_op jit(solution)/shard_map/ppermute | solution.py:158
  88.3 13.7 %collective-permute-start.17 = (bf16[2,128,512]{2,1,0:T(8,128)(2,1)S(1)}, bf16[2,128,512]{2,1,0:T(8,128)(2,1)S(1)}, u32[]{:S(2)}, u32[]{:S(2)}) collective-permute-start(bf16[2,128,512]{2,1,0:T(8,128)(2,1)S(1)} %add_convert_fusion), channel_id=1, source_target_pairs={{0,4},{1,5},{2,6},{3,7},{4,0},{5,1},{6,2},{7,3},{8,12},{9,13},{10,... | collective-permute-start | bytes 786440 | tf_op jit(solution)/shard_map/ppermute | solution.py:158
  102.1 1.6 %collective-permute-start.18 = (f32[128,512]{1,0:T(8,128)S(1)}, f32[128,512]{1,0:T(8,128)S(1)}, u32[]{:S(2)}, u32[]{:S(2)}) collective-permute-start(f32[128,512]{1,0:T(8,128)S(1)} %slice_bitcast_fusion), channel_id=1, source_target_pairs={{0,1},{1,0},{2,3},{3,2},{4,5},{5,4},{6,7},{7,6},{8,9},{9,8},{10,11... | collective-permute-start | bytes 786440 | tf_op jit(solution)/shard_map/ppermute | solution.py:158

commit v4 on v3

--- a/solution.py
+++ b/solution.py
@@ -65,8 +65,7 @@
 
 def left_kernel(phase, *refs):
     (own, sib, where, here, others, left, left_sib), refs = refs[:7], refs[7:]
-    mixed, token, found, source, lbuf, obuf, lsem, osem = refs[-8:]
-    token[...] = jnp.zeros_like(token)
+    mixed, found, source, lbuf, obuf, lsem, osem = refs[-7:]
     slots, depth, outs = left.shape[0], lbuf.shape[0], obuf.shape[0]
     half = here.shape[1]
     bands = others.shape[0] + 1
@@ -186,25 +185,21 @@
     where_dst = jnp.stack([3 - partner, 3 - plane, partner, plane, band, core]).astype(jnp.int32)
 
     params = pltpu.CompilerParams(vmem_limit_bytes=VMEM)
-    left_cost = pl.CostEstimate(flops=10**6, bytes_accessed=width, transcendentals=0)
     cost = pl.CostEstimate(flops=3 * 10**9, bytes_accessed=7 * width * width * 2, transcendentals=0)
     depth = 8
     mixed = None
     for phase in range(sectors):
         if phase == 1:
-            far_block, mirror_bands, token = lax.optimization_barrier((far_block, mirror_bands, token))
+            far_block, mirror_bands, mixed = lax.optimization_barrier((far_block, mirror_bands, mixed))
             blocks[2:] = [(mirror_block, mirror_bands), (far_block, bands_of(far_block))]
         operands = [own_meta, sib_meta, where_src, *blocks[phase], left, left_sib]
         if mixed is not None:
-            operands += [mixed, token]
-        mixed, token = pl.pallas_call(
+            operands.append(mixed)
+        mixed = pl.pallas_call(
             functools.partial(left_kernel, phase),
-            out_shape=(
-                jax.ShapeDtypeStruct((CORES * slots, width, width), BF16),
-                jax.ShapeDtypeStruct((8, 128), F32),
-            ),
+            out_shape=jax.ShapeDtypeStruct((CORES * slots, width, width), BF16),
             in_specs=[SMEM] * 3 + [WHOLE] * 2 + [ANY] * (len(operands) - 5),
-            out_specs=(ANY, WHOLE),
+            out_specs=ANY,
             scratch_shapes=[
                 pltpu.SMEM((CORES * slots + 1,), jnp.int32),
                 pltpu.VMEM((width, width), BF16),
@@ -215,7 +210,7 @@
             ],
             input_output_aliases={} if mixed is None else {7: 0},
             compiler_params=params,
-            cost_estimate=left_cost,
+            cost_estimate=cost,
             name="left_mix",
         )(*operands)
 

time: 104 us -> 85 us (0.82); the launches traced: 105 us -> 84.3 us
  local copies, waits for them, and re-layouts: 22.2 us -> 3.67 us
  Pallas kernels: 23.2 us -> 18.1 us
  waiting for transfers between devices: 28.1 us -> 31.2 us
    unnamed x16 -> x6, local copies, waits for them, and re-layouts: 21 us -> 2.5 us
    pallas_call x4, Pallas kernels: 12.4 us -> 8.71 us  [local(): pl.pallas_call(functools.partial(left_kernel, phase), out_shape=jax.Shape...]
    ppermute x19, waiting for transfers between devices: 28.1 us -> 31.2 us  [move(): return lax.ppermute(value, 'term', pairs)]
    pallas_call x4, Pallas kernels: 10.9 us -> 9.39 us  [right_mix(): pl.pallas_call(functools.partial(right_kernel, phase), out_shape=(jax.Sha...]
  transfers between devices with their start and end apart: 19 -> 19, of which waited for: 8 -> 11; matrix products, arithmetic and copies ran while one was open for 1% -> 1% of each run, Pallas kernels for 20% -> 19%
where the time goes in v4:
time: 85 us; the launch traced here: 84.3 us
  waiting for transfers between devices  31.2 us (37%)
  starting transfers between devices  28.5 us (34%)
  Pallas kernels  18.1 us (21%)
  local copies, waits for them, and re-layouts  3.67 us (4%)
  other arithmetic  2.02 us (2%)
  between operations  0.85 us (1%)
    ppermute x19, waiting for transfers between devices, move(): return lax.ppermute(value, 'term', pairs)  31.2 us
    ppermute x19, starting transfers between devices, move(): return lax.ppermute(value, 'term', pairs)  28.5 us
    pallas_call x4, Pallas kernels, right_mix(): pl.pallas_call(functools.partial(right_kernel, phase), out_shape=(jax.Sha...  9.39 us
    pallas_call x4, Pallas kernels, local(): pl.pallas_call(functools.partial(left_kernel, phase), out_shape=jax.Shape...  8.71 us
    unnamed x6, local copies, waits for them, and re-layouts  2.5 us
  transfers between devices with their start and end apart: 19, of which 11 were waited for; matrix products, arithmetic and copies ran while one was open for 1% of the time, Pallas kernels for 19%

profile of v4, /device:TPU:13, one launch (start us, length us, event | category | flops | bytes accessed | tf_op | source)
XLA Modules:
  0.0 84.3 jit_solution(1183189741017384678)
XLA Ops:
  0.0 1.0 %dynamic-slice_bitcast_fusion = (bf16[1,128,512]{2,1,0:T(8,128)(2,1)S(1)}, bf16[128,512]{1,0:T(8,128)(2,1)S(1)}) fusion(bf16[128,1024]{1,0:T(8,128)(2,1)} %param.6, s32[]{:T(128)S(6)} %select_n.42, s32[]{:T(128)S(6)} %select_n.38), kind=kLoop, calls=%fused_computation.10 | loop fusion | bytes 524296 | tf_op jit(solution)/shard_map/stack | solution.py:175
  1.0 0.7 collective-permute-start
  2.4 0.7 pad_add_fusion.refs_0_
  3.1 0.0 collective-permute-start.1
  3.1 1.1 %collective-permute-done.1.refs_1_ = s32[21]{0:T(128)S(1)} collective-permute-done((s32[21]{0:T(128)S(1)}, s32[21]{0:T(128)S(1)}, u32[]{:S(2)}, u32[]{:S(2)}) %collective-permute-start.1) | collective-permute-done | bytes 116 | tf_op jit(solution)/shard_map/ppermute | solution.py:157
  4.3 0.0 collective-permute-done
  4.3 0.2 collective-permute-start.8
  4.5 1.3 %collective-permute-start.5 = (bf16[2,128,512]{2,1,0:T(8,128)(2,1)S(1)}, bf16[2,128,512]{2,1,0:T(8,128)(2,1)S(1)}, u32[]{:S(2)}, u32[]{:S(2)}) collective-permute-start(bf16[2,128,512]{2,1,0:T(8,128)(2,1)S(1)} %pad_maximum_fusion.1.refs_3_), channel_id=1, source_target_pairs={{0,2},{1,3},{2,0},{3,1},{4,6},{5,7},{6,4},{7,5},{8,10},{9,11},{10,... | collective-permute-start | bytes 786440 | tf_op jit(solution)/shard_map/ppermute | solution.py:157
  5.8 0.2 collective-permute-start.4
  5.9 2.4 %collective-permute-start.2 = (bf16[2,128,512]{2,1,0:T(8,128)(2,1)S(1)}, bf16[2,128,512]{2,1,0:T(8,128)(2,1)S(1)}, u32[]{:S(2)}, u32[]{:S(2)}) collective-permute-start(bf16[2,128,512]{2,1,0:T(8,128)(2,1)S(1)} %pad_maximum_fusion.1.refs_3_), channel_id=1, source_target_pairs={{0,12},{1,13},{2,14},{3,15},{4,8},{5,9},{6,10},{7,11},{8,4},{9,5},... | collective-permute-start | bytes 786440 | tf_op jit(solution)/shard_map/ppermute | solution.py:157
  8.4 3.8 %collective-permute-done.5 = bf16[2,128,512]{2,1,0:T(8,128)(2,1)S(1)} collective-permute-done((bf16[2,128,512]{2,1,0:T(8,128)(2,1)S(1)}, bf16[2,128,512]{2,1,0:T(8,128)(2,1)S(1)}, u32[]{:S(2)}, u32[]{:S(2)}) %collective-permute-start.5) | collective-permute-done | bytes 262176 | tf_op jit(solution)/shard_map/ppermute | solution.py:157
  12.2 0.9 %collective-permute-done.4.refs_3_ = bf16[2,128,512]{2,1,0:T(8,128)(2,1)S(1)} collective-permute-done((bf16[2,128,512]{2,1,0:T(8,128)(2,1)S(1)}, bf16[2,128,512]{2,1,0:T(8,128)(2,1)S(1)}, u32[]{:S(2)}, u32[]{:S(2)}) %collective-permute-start.4) | collective-permute-done | bytes 262176 | tf_op jit(solution)/shard_map/ppermute | solution.py:157
  13.0 0.3 collective-permute-start.6
  13.4 0.9 %collective-permute-done.2.refs_3_ = bf16[2,128,512]{2,1,0:T(8,128)(2,1)S(1)} collective-permute-done((bf16[2,128,512]{2,1,0:T(8,128)(2,1)S(1)}, bf16[2,128,512]{2,1,0:T(8,128)(2,1)S(1)}, u32[]{:S(2)}, u32[]{:S(2)}) %collective-permute-start.2) | collective-permute-done | bytes 262176 | tf_op jit(solution)/shard_map/ppermute | solution.py:157
  14.3 4.3 %collective-permute-done.6 = bf16[2,128,512]{2,1,0:T(8,128)(2,1)S(1)} collective-permute-done((bf16[2,128,512]{2,1,0:T(8,128)(2,1)S(1)}, bf16[2,128,512]{2,1,0:T(8,128)(2,1)S(1)}, u32[]{:S(2)}, u32[]{:S(2)}) %collective-permute-start.6) | collective-permute-done | bytes 262176 | tf_op jit(solution)/shard_map/ppermute | solution.py:157
  18.6 3.4 %collective-permute-start.10 = (bf16[10,512,512]{2,1,0:T(8,128)(2,1)}, bf16[10,512,512]{2,1,0:T(8,128)(2,1)}, u32[]{:S(2)}, u32[]{:S(2)}) collective-permute-start(bf16[10,512,512]{2,1,0:T(8,128)(2,1)} %refs_4_.7), channel_id=1, source_target_pairs={{0,1},{1,0},{2,3},{3,2},{4,5},{5,4},{6,7},{7,6},{8,9},{9,8},{10,11... | collective-permute-start | bytes 15728648 | tf_op jit(solution)/shard_map/ppermute | solution.py:157
  21.9 0.1 stack.58.refs_2_
  22.0 0.1 stack.57.refs_2_
  22.1 0.5 collective-permute-start.3
  22.6 0.3 collective-permute-start.7
  22.8 0.0 collective-permute-done.8.refs_6_
  22.8 0.0 copy-start
  22.8 2.5 %copy-done = bf16[10,512,512]{2,1,0:T(8,128)(2,1)S(1)} copy-done((bf16[10,512,512]{2,1,0:T(8,128)(2,1)S(1)}, bf16[10,512,512]{2,1,0:T(8,128)(2,1)}, u32[]{:S(2)}) %copy-start) | copy-done | bytes 5242904
  25.3 1.3 %left_mix.4.refs_7_ = bf16[20,512,512]{2,1,0:T(8,128)(2,1)S(1)} custom-call(s32[21]{0:T(128)S(1)} %pad_add_fusion.refs_0_, s32[21]{0:T(128)S(1)} %collective-permute-done.1.refs_1_, s32[6]{0:T(128)S(1)} %stack.58.refs_2_, bf16[2,128,512]{2,1,0:T(8,128)(2,1)S(1)} %pad_maximum_fusion.1.refs_3_, bf16[1,2,128,512]{3,2,1,0:T(8,128)(2,1)S(1)} %bitcast.27, ...), custom_call_target="tpu_custom_call" | custom-call | flops 3000000000 | bytes 3670016 | tf_op jit(solution)/shard_map/left_mix/pallas_call | solution.py:198
  26.7 3.4 %collective-permute-done.3.refs_3_ = bf16[2,128,512]{2,1,0:T(8,128)(2,1)S(1)} collective-permute-done((bf16[2,128,512]{2,1,0:T(8,128)(2,1)S(1)}, bf16[2,128,512]{2,1,0:T(8,128)(2,1)S(1)}, u32[]{:S(2)}, u32[]{:S(2)}) %collective-permute-start.3) | collective-permute-done | bytes 262176 | tf_op jit(solution)/shard_map/ppermute | solution.py:157
  30.0 0.2 collective-permute-done.7
  30.2 0.3 collective-permute-start.9
  30.5 0.8 left_mix.5.refs_7_
  31.3 0.0 slice-start
  31.3 3.2 %left_mix.6.refs_7_ = bf16[20,512,512]{2,1,0:T(8,128)(2,1)S(1)} custom-call(s32[21]{0:T(128)S(1)} %pad_add_fusion.refs_0_, s32[21]{0:T(128)S(1)} %collective-permute-done.1.refs_1_, s32[6]{0:T(128)S(1)} %stack.58.refs_2_, bf16[2,128,512]{2,1,0:T(8,128)(2,1)S(1)} %collective-permute-done.2.refs_3_, ...), custom_call_target="tpu_custom_call", output_to_operand_aliasing={{}: (7, {})} | custom-call | flops 3000000000 | bytes 3670016 | tf_op jit(solution)/shard_map/left_mix/pallas_call | solution.py:198
  34.5 0.0 slice-start.1
  34.5 2.4 %collective-permute-done.9 = bf16[2,128,512]{2,1,0:T(8,128)(2,1)S(1)} collective-permute-done((bf16[2,128,512]{2,1,0:T(8,128)(2,1)S(1)}, bf16[2,128,512]{2,1,0:T(8,128)(2,1)S(1)}, u32[]{:S(2)}, u32[]{:S(2)}) %collective-permute-start.9) | collective-permute-done | bytes 262176 | tf_op jit(solution)/shard_map/ppermute | solution.py:157
  36.9 3.4 %left_mix.7.refs_3_ = bf16[20,512,512]{2,1,0:T(8,128)(2,1)S(1)} custom-call(s32[21]{0:T(128)S(1)} %pad_add_fusion.refs_0_, s32[21]{0:T(128)S(1)} %collective-permute-done.1.refs_1_, s32[6]{0:T(128)S(1)} %stack.58.refs_2_, bf16[2,128,512]{2,1,0:T(8,128)(2,1)S(1)} %collective-permute-done.3.refs_3_, ...), custom_call_target="tpu_custom_call", output_to_operand_aliasing={{}: (7, {})} | custom-call | flops 3000000000 | bytes 3670016 | tf_op jit(solution)/shard_map/left_mix/pallas_call | solution.py:198
  40.3 0.0 collective-permute-done.10.refs_5_
  40.3 0.0 slice-done
  40.3 0.0 slice-done.1
  40.4 2.4 %right_mix.4 = (f32[2,128,512]{2,1,0:T(8,128)S(1)}, bf16[1,2,128,512]{3,2,1,0:T(8,128)(2,1)S(1)}) custom-call(s32[21]{0:T(128)S(1)} %pad_add_fusion.refs_0_, s32[21]{0:T(128)S(1)} %collective-permute-done.1.refs_1_, s32[6]{0:T(128)S(1)} %stack.57.refs_2_, bf16[20,512,512]{2,1,0:T(8,128)(2,1)S(1)} %left_mix.7.refs_3_, bf16[10,512,512]{2,1,0:T(8,128)(2,1)S(1)} %bitcast.26, ...), custom_call_target="tpu_custom_call" | custom-call | flops 3000000000 | bytes 3670016 | tf_op jit(solution)/shard_map/right_mix/pallas_call | solution.py:218
  42.7 2.4 %collective-permute-start.11 = (bf16[2,128,512]{2,1,0:T(8,128)(2,1)S(1)}, bf16[2,128,512]{2,1,0:T(8,128)(2,1)S(1)}, u32[]{:S(2)}, u32[]{:S(2)}) collective-permute-start(bf16[2,128,512]{2,1,0:T(8,128)(2,1)S(1)} %bitcast.34), channel_id=1, source_target_pairs={{0,2},{1,3},{2,0},{3,1},{4,6},{5,7},{6,4},{7,5},{8,10},{9,11},{10,... | collective-permute-start | bytes 786440 | tf_op jit(solution)/shard_map/ppermute | solution.py:157
  45.1 3.2 %right_mix.6 = (f32[2,128,512]{2,1,0:T(8,128)S(1)}, bf16[1,2,128,512]{3,2,1,0:T(8,128)(2,1)S(1)}) custom-call(s32[21]{0:T(128)S(1)} %pad_add_fusion.refs_0_, s32[21]{0:T(128)S(1)} %collective-permute-done.1.refs_1_, s32[6]{0:T(128)S(1)} %stack.57.refs_2_, bf16[20,512,512]{2,1,0:T(8,128)(2,1)S(1)} %left_mix.7.refs_3_, bf16[10,512,512]{2,1,0:T(8,128)(2,1)S(1)} %bitcast.26, ...), custom_call_target="tpu_custom_call" | custom-call | flops 3000000000 | bytes 3670016 | tf_op jit(solution)/shard_map/right_mix/pallas_call | solution.py:218
  48.4 0.1 collective-permute-start.13
  48.4 3.5 %collective-permute-done.11 = bf16[2,128,512]{2,1,0:T(8,128)(2,1)S(1)} collective-permute-done((bf16[2,128,512]{2,1,0:T(8,128)(2,1)S(1)}, bf16[2,128,512]{2,1,0:T(8,128)(2,1)S(1)}, u32[]{:S(2)}, u32[]{:S(2)}) %collective-permute-start.11) | collective-permute-done | bytes 262176 | tf_op jit(solution)/shard_map/ppermute | solution.py:157
  51.9 0.1 add_convert_fusion.2
  52.0 0.1 collective-permute-start.14
  52.1 2.4 %right_mix.7 = (f32[2,128,512]{2,1,0:T(8,128)S(1)}, bf16[1,2,128,512]{3,2,1,0:T(8,128)(2,1)S(1)}) custom-call(s32[21]{0:T(128)S(1)} %pad_add_fusion.refs_0_, s32[21]{0:T(128)S(1)} %collective-permute-done.1.refs_1_, s32[6]{0:T(128)S(1)} %stack.57.refs_2_, bf16[20,512,512]{2,1,0:T(8,128)(2,1)S(1)} %left_mix.7.refs_3_, bf16[10,512,512]{2,1,0:T(8,128)(2,1)S(1)} %bitcast.26, ...), custom_call_target="tpu_custom_call" | custom-call | flops 3000000000 | bytes 3670016 | tf_op jit(solution)/shard_map/right_mix/pallas_call | solution.py:218
  54.4 2.6 %collective-permute-start.16 = (bf16[2,128,512]{2,1,0:T(8,128)(2,1)S(1)}, bf16[2,128,512]{2,1,0:T(8,128)(2,1)S(1)}, u32[]{:S(2)}, u32[]{:S(2)}) collective-permute-start(bf16[2,128,512]{2,1,0:T(8,128)(2,1)S(1)} %bitcast.33), channel_id=1, source_target_pairs={{0,2},{1,3},{2,0},{3,1},{4,6},{5,7},{6,4},{7,5},{8,10},{9,11},{10,... | collective-permute-start | bytes 786440 | tf_op jit(solution)/shard_map/ppermute | solution.py:157
  57.0 1.4 %right_mix.5 = (f32[2,128,512]{2,1,0:T(8,128)S(1)}, bf16[1,2,128,512]{3,2,1,0:T(8,128)(2,1)S(1)}) custom-call(s32[21]{0:T(128)S(1)} %pad_add_fusion.refs_0_, s32[21]{0:T(128)S(1)} %collective-permute-done.1.refs_1_, s32[6]{0:T(128)S(1)} %stack.57.refs_2_, bf16[20,512,512]{2,1,0:T(8,128)(2,1)S(1)} %left_mix.7.refs_3_, bf16[10,512,512]{2,1,0:T(8,128)(2,1)S(1)} %bitcast.26, ...), custom_call_target="tpu_custom_call" | custom-call | flops 3000000000 | bytes 3670016 | tf_op jit(solution)/shard_map/right_mix/pallas_call | solution.py:218
  58.4 2.0 %collective-permute-start.12 = (bf16[2,128,512]{2,1,0:T(8,128)(2,1)S(1)}, bf16[2,128,512]{2,1,0:T(8,128)(2,1)S(1)}, u32[]{:S(2)}, u32[]{:S(2)}) collective-permute-start(bf16[2,128,512]{2,1,0:T(8,128)(2,1)S(1)} %bitcast.31), channel_id=1, source_target_pairs={{0,2},{1,3},{2,0},{3,1},{4,6},{5,7},{6,4},{7,5},{8,10},{9,11},{10,... | collective-permute-start | bytes 786440 | tf_op jit(solution)/shard_map/ppermute | solution.py:157
  60.4 0.0 collective-permute-done.13
  60.4 0.0 collective-permute-done.14
  60.4 0.1 add_convert_fusion.1
  60.5 8.7 %collective-permute-start.15 = (bf16[2,128,512]{2,1,0:T(8,128)(2,1)S(1)}, bf16[2,128,512]{2,1,0:T(8,128)(2,1)S(1)}, u32[]{:S(2)}, u32[]{:S(2)}) collective-permute-start(bf16[2,128,512]{2,1,0:T(8,128)(2,1)S(1)} %add_convert_fusion.1), channel_id=1, source_target_pairs={{0,12},{1,13},{2,14},{3,15},{4,8},{5,9},{6,10},{7,11},{8,4},{9,5},... | collective-permute-start | bytes 786440 | tf_op jit(solution)/shard_map/ppermute | solution.py:157
  69.2 0.0 collective-permute-done.16
  69.2 0.1 add_convert_fusion
  69.3 0.1 collective-permute-start.17
  69.4 0.0 collective-permute-done.12
  69.4 9.6 %collective-permute-done.15 = bf16[2,128,512]{2,1,0:T(8,128)(2,1)S(1)} collective-permute-done((bf16[2,128,512]{2,1,0:T(8,128)(2,1)S(1)}, bf16[2,128,512]{2,1,0:T(8,128)(2,1)S(1)}, u32[]{:S(2)}, u32[]{:S(2)}) %collective-permute-start.15) | collective-permute-done | bytes 262176 | tf_op jit(solution)/shard_map/ppermute | solution.py:157
  79.0 0.0 collective-permute-done.17
  79.0 0.1 convert_add_fusion
  79.2 3.1 %collective-permute-start.18 = (f32[128,512]{1,0:T(8,128)S(1)}, f32[128,512]{1,0:T(8,128)S(1)}, u32[]{:S(2)}, u32[]{:S(2)}) collective-permute-start(f32[128,512]{1,0:T(8,128)S(1)} %slice_bitcast_fusion), channel_id=1, source_target_pairs={{0,1},{1,0},{2,3},{3,2},{4,5},{5,4},{6,7},{7,6},{8,9},{9,8},{10,11... | collective-permute-start | bytes 786440 | tf_op jit(solution)/shard_map/ppermute | solution.py:157
  82.3 1.2 %collective-permute-done.18 = f32[128,512]{1,0:T(8,128)S(1)} collective-permute-done((f32[128,512]{1,0:T(8,128)S(1)}, f32[128,512]{1,0:T(8,128)S(1)}, u32[]{:S(2)}, u32[]{:S(2)}) %collective-permute-start.18) | collective-permute-done | bytes 262176 | tf_op jit(solution)/shard_map/ppermute | solution.py:157
  83.5 0.8 pad_maximum_fusion
  (4 shorter events, 0.1 us)
Async XLA Ops:
  1.0 3.3 %collective-permute-start = (bf16[128,512]{1,0:T(8,128)(2,1)S(1)}, bf16[128,512]{1,0:T(8,128)(2,1)S(1)}, u32[]{:S(2)}, u32[]{:S(2)}) collective-permute-start(bf16[128,512]{1,0:T(8,128)(2,1)S(1)} %get-tuple-element.50), channel_id=1, source_target_pairs={{0,1},{1,0},{2,3},{3,2},{4,5},{5,4},{6,7},{7,6},{8,9},{9,8},{10,11... | collective-permute-start | bytes 393224 | tf_op jit(solution)/shard_map/ppermute | solution.py:157
  3.1 1.1 %collective-permute-start.1 = (s32[21]{0:T(128)S(1)}, s32[21]{0:T(128)S(1)}, u32[]{:S(2)}, u32[]{:S(2)}) collective-permute-start(s32[21]{0:T(128)S(1)} %pad_add_fusion.refs_0_), channel_id=1, source_target_pairs={{0,1},{1,0},{2,3},{3,2},{4,5},{5,4},{6,7},{7,6},{8,9},{9,8},{10,11... | collective-permute-start | bytes 260 | tf_op jit(solution)/shard_map/ppermute | solution.py:157
  4.3 18.6 %collective-permute-start.8 = (bf16[10,512,512]{2,1,0:T(8,128)(2,1)}, bf16[10,512,512]{2,1,0:T(8,128)(2,1)}, u32[]{:S(2)}, u32[]{:S(2)}) collective-permute-start(bf16[10,512,512]{2,1,0:T(8,128)(2,1)} %refs_5_.7), channel_id=1, source_target_pairs={{0,1},{1,0},{2,3},{3,2},{4,5},{5,4},{6,7},{7,6},{8,9},{9,8},{10,11... | collective-permute-start | bytes 15728648 | tf_op jit(solution)/shard_map/ppermute | solution.py:157
  4.5 7.7 %collective-permute-start.5 = (bf16[2,128,512]{2,1,0:T(8,128)(2,1)S(1)}, bf16[2,128,512]{2,1,0:T(8,128)(2,1)S(1)}, u32[]{:S(2)}, u32[]{:S(2)}) collective-permute-start(bf16[2,128,512]{2,1,0:T(8,128)(2,1)S(1)} %pad_maximum_fusion.1.refs_3_), channel_id=1, source_target_pairs={{0,2},{1,3},{2,0},{3,1},{4,6},{5,7},{6,4},{7,5},{8,10},{9,11},{10,... | collective-permute-start | bytes 786440 | tf_op jit(solution)/shard_map/ppermute | solution.py:157
  5.8 7.3 %collective-permute-start.4 = (bf16[2,128,512]{2,1,0:T(8,128)(2,1)S(1)}, bf16[2,128,512]{2,1,0:T(8,128)(2,1)S(1)}, u32[]{:S(2)}, u32[]{:S(2)}) collective-permute-start(bf16[2,128,512]{2,1,0:T(8,128)(2,1)S(1)} %pad_maximum_fusion.1.refs_3_), channel_id=1, source_target_pairs={{0,4},{1,5},{2,6},{3,7},{4,0},{5,1},{6,2},{7,3},{8,12},{9,13},{10,... | collective-permute-start | bytes 786440 | tf_op jit(solution)/shard_map/ppermute | solution.py:157
  5.9 8.3 %collective-permute-start.2 = (bf16[2,128,512]{2,1,0:T(8,128)(2,1)S(1)}, bf16[2,128,512]{2,1,0:T(8,128)(2,1)S(1)}, u32[]{:S(2)}, u32[]{:S(2)}) collective-permute-start(bf16[2,128,512]{2,1,0:T(8,128)(2,1)S(1)} %pad_maximum_fusion.1.refs_3_), channel_id=1, source_target_pairs={{0,12},{1,13},{2,14},{3,15},{4,8},{5,9},{6,10},{7,11},{8,4},{9,5},... | collective-permute-start | bytes 786440 | tf_op jit(solution)/shard_map/ppermute | solution.py:157
  13.0 5.5 %collective-permute-start.6 = (bf16[2,128,512]{2,1,0:T(8,128)(2,1)S(1)}, bf16[2,128,512]{2,1,0:T(8,128)(2,1)S(1)}, u32[]{:S(2)}, u32[]{:S(2)}) collective-permute-start(bf16[2,128,512]{2,1,0:T(8,128)(2,1)S(1)} %collective-permute-done.4.refs_3_), channel_id=1, source_target_pairs={{0,2},{1,3},{2,0},{3,1},{4,6},{5,7},{6,4},{7,5},{8,10},{9,11},{10,... | collective-permute-start | bytes 786440 | tf_op jit(solution)/shard_map/ppermute | solution.py:157
  18.6 21.8 %collective-permute-start.10 = (bf16[10,512,512]{2,1,0:T(8,128)(2,1)}, bf16[10,512,512]{2,1,0:T(8,128)(2,1)}, u32[]{:S(2)}, u32[]{:S(2)}) collective-permute-start(bf16[10,512,512]{2,1,0:T(8,128)(2,1)} %refs_4_.7), channel_id=1, source_target_pairs={{0,1},{1,0},{2,3},{3,2},{4,5},{5,4},{6,7},{7,6},{8,9},{9,8},{10,11... | collective-permute-start | bytes 15728648 | tf_op jit(solution)/shard_map/ppermute | solution.py:157
  22.1 7.9 %collective-permute-start.3 = (bf16[2,128,512]{2,1,0:T(8,128)(2,1)S(1)}, bf16[2,128,512]{2,1,0:T(8,128)(2,1)S(1)}, u32[]{:S(2)}, u32[]{:S(2)}) collective-permute-start(bf16[2,128,512]{2,1,0:T(8,128)(2,1)S(1)} %collective-permute-done.2.refs_3_), channel_id=1, source_target_pairs={{0,4},{1,5},{2,6},{3,7},{4,0},{5,1},{6,2},{7,3},{8,12},{9,13},{10,... | collective-permute-start | bytes 786440 | tf_op jit(solution)/shard_map/ppermute | solution.py:157
  22.6 7.6 %collective-permute-start.7 = (bf16[2,128,512]{2,1,0:T(8,128)(2,1)S(1)}, bf16[2,128,512]{2,1,0:T(8,128)(2,1)S(1)}, u32[]{:S(2)}, u32[]{:S(2)}) collective-permute-start(bf16[2,128,512]{2,1,0:T(8,128)(2,1)S(1)} %collective-permute-done.2.refs_3_), channel_id=1, source_target_pairs={{0,2},{1,3},{2,0},{3,1},{4,6},{5,7},{6,4},{7,5},{8,10},{9,11},{10,... | collective-permute-start | bytes 786440 | tf_op jit(solution)/shard_map/ppermute | solution.py:157
  22.8 2.5 %copy-start = (bf16[10,512,512]{2,1,0:T(8,128)(2,1)S(1)}, bf16[10,512,512]{2,1,0:T(8,128)(2,1)}, u32[]{:S(2)}) copy-start(bf16[10,512,512]{2,1,0:T(8,128)(2,1)} %refs_5_.7) | copy-start | bytes 15728644
  30.2 6.7 %collective-permute-start.9 = (bf16[2,128,512]{2,1,0:T(8,128)(2,1)S(1)}, bf16[2,128,512]{2,1,0:T(8,128)(2,1)S(1)}, u32[]{:S(2)}, u32[]{:S(2)}) collective-permute-start(bf16[2,128,512]{2,1,0:T(8,128)(2,1)S(1)} %collective-permute-done.3.refs_3_), channel_id=1, source_target_pairs={{0,2},{1,3},{2,0},{3,1},{4,6},{5,7},{6,4},{7,5},{8,10},{9,11},{10,... | collective-permute-start | bytes 786440 | tf_op jit(solution)/shard_map/ppermute | solution.py:157
  31.3 9.1 %slice-start = ((s8[5242880]{0:T(1024)(128)(4,1)}), s8[4194304]{0:T(1024)(128)(4,1)S(1)}, s32[]{:S(2)}) async-start(s8[5242880]{0:T(1024)(128)(4,1)} %bitcast.25), calls=%async_computation | async-start | bytes 8388608
  34.5 5.9 %slice-start.1 = ((s8[5242880]{0:T(1024)(128)(4,1)}), s8[1048576]{0:T(1024)(128)(4,1)S(1)}, s32[]{:S(2)}) async-start(s8[5242880]{0:T(1024)(128)(4,1)} %bitcast.25), calls=%async_computation.1 | async-start | bytes 2097152
  42.7 9.2 %collective-permute-start.11 = (bf16[2,128,512]{2,1,0:T(8,128)(2,1)S(1)}, bf16[2,128,512]{2,1,0:T(8,128)(2,1)S(1)}, u32[]{:S(2)}, u32[]{:S(2)}) collective-permute-start(bf16[2,128,512]{2,1,0:T(8,128)(2,1)S(1)} %bitcast.34), channel_id=1, source_target_pairs={{0,2},{1,3},{2,0},{3,1},{4,6},{5,7},{6,4},{7,5},{8,10},{9,11},{10,... | collective-permute-start | bytes 786440 | tf_op jit(solution)/shard_map/ppermute | solution.py:157
  48.4 12.0 %collective-permute-start.13 = (bf16[2,128,512]{2,1,0:T(8,128)(2,1)S(1)}, bf16[2,128,512]{2,1,0:T(8,128)(2,1)S(1)}, u32[]{:S(2)}, u32[]{:S(2)}) collective-permute-start(bf16[2,128,512]{2,1,0:T(8,128)(2,1)S(1)} %bitcast.32), channel_id=1, source_target_pairs={{0,2},{1,3},{2,0},{3,1},{4,6},{5,7},{6,4},{7,5},{8,10},{9,11},{10,... | collective-permute-start | bytes 786440 | tf_op jit(solution)/shard_map/ppermute | solution.py:157
  52.0 8.4 %collective-permute-start.14 = (bf16[2,128,512]{2,1,0:T(8,128)(2,1)S(1)}, bf16[2,128,512]{2,1,0:T(8,128)(2,1)S(1)}, u32[]{:S(2)}, u32[]{:S(2)}) collective-permute-start(bf16[2,128,512]{2,1,0:T(8,128)(2,1)S(1)} %add_convert_fusion.2), channel_id=1, source_target_pairs={{0,4},{1,5},{2,6},{3,7},{4,0},{5,1},{6,2},{7,3},{8,12},{9,13},{10,... | collective-permute-start | bytes 786440 | tf_op jit(solution)/shard_map/ppermute | solution.py:157
  54.4 14.8 %collective-permute-start.16 = (bf16[2,128,512]{2,1,0:T(8,128)(2,1)S(1)}, bf16[2,128,512]{2,1,0:T(8,128)(2,1)S(1)}, u32[]{:S(2)}, u32[]{:S(2)}) collective-permute-start(bf16[2,128,512]{2,1,0:T(8,128)(2,1)S(1)} %bitcast.33), channel_id=1, source_target_pairs={{0,2},{1,3},{2,0},{3,1},{4,6},{5,7},{6,4},{7,5},{8,10},{9,11},{10,... | collective-permute-start | bytes 786440 | tf_op jit(solution)/shard_map/ppermute | solution.py:157
  58.4 11.0 %collective-permute-start.12 = (bf16[2,128,512]{2,1,0:T(8,128)(2,1)S(1)}, bf16[2,128,512]{2,1,0:T(8,128)(2,1)S(1)}, u32[]{:S(2)}, u32[]{:S(2)}) collective-permute-start(bf16[2,128,512]{2,1,0:T(8,128)(2,1)S(1)} %bitcast.31), channel_id=1, source_target_pairs={{0,2},{1,3},{2,0},{3,1},{4,6},{5,7},{6,4},{7,5},{8,10},{9,11},{10,... | collective-permute-start | bytes 786440 | tf_op jit(solution)/shard_map/ppermute | solution.py:157
  60.5 18.5 %collective-permute-start.15 = (bf16[2,128,512]{2,1,0:T(8,128)(2,1)S(1)}, bf16[2,128,512]{2,1,0:T(8,128)(2,1)S(1)}, u32[]{:S(2)}, u32[]{:S(2)}) collective-permute-start(bf16[2,128,512]{2,1,0:T(8,128)(2,1)S(1)} %add_convert_fusion.1), channel_id=1, source_target_pairs={{0,12},{1,13},{2,14},{3,15},{4,8},{5,9},{6,10},{7,11},{8,4},{9,5},... | collective-permute-start | bytes 786440 | tf_op jit(solution)/shard_map/ppermute | solution.py:157
  69.3 9.7 %collective-permute-start.17 = (bf16[2,128,512]{2,1,0:T(8,128)(2,1)S(1)}, bf16[2,128,512]{2,1,0:T(8,128)(2,1)S(1)}, u32[]{:S(2)}, u32[]{:S(2)}) collective-permute-start(bf16[2,128,512]{2,1,0:T(8,128)(2,1)S(1)} %add_convert_fusion), channel_id=1, source_target_pairs={{0,4},{1,5},{2,6},{3,7},{4,0},{5,1},{6,2},{7,3},{8,12},{9,13},{10,... | collective-permute-start | bytes 786440 | tf_op jit(solution)/shard_map/ppermute | solution.py:157
  79.2 4.3 %collective-permute-start.18 = (f32[128,512]{1,0:T(8,128)S(1)}, f32[128,512]{1,0:T(8,128)S(1)}, u32[]{:S(2)}, u32[]{:S(2)}) collective-permute-start(f32[128,512]{1,0:T(8,128)S(1)} %slice_bitcast_fusion), channel_id=1, source_target_pairs={{0,1},{1,0},{2,3},{3,2},{4,5},{5,4},{6,7},{7,6},{8,9},{9,8},{10,11... | collective-permute-start | bytes 786440 | tf_op jit(solution)/shard_map/ppermute | solution.py:157

commit v5 on v4

--- a/solution.py
+++ b/solution.py
@@ -170,13 +170,15 @@
     mine = lax.dynamic_slice_in_dim(wavefunction, core * width, width, 1)
     theirs = lax.dynamic_slice_in_dim(wavefunction, (1 - core) * width, width, 1)
     from_sib = move(theirs, flip=True)
-    left_sib, from_sib, sib_meta = lax.optimization_barrier((left, from_sib, sib_meta))
+    left_sib, from_sib = lax.optimization_barrier((left, from_sib))
     left_sib = move(left_sib, flip=True)
     own_block = jnp.stack([mine, from_sib])
     mirror_block = move(own_block, mirror)
     beside_block, own_bands = lax.optimization_barrier((move(own_block, beside), bands_of(own_block)))
     far_block = move(mirror_block, beside)
-    mirror_block, beside_bands, right_sib = lax.optimization_barrier((mirror_block, bands_of(beside_block), right))
+    mirror_block, beside_bands, right_sib, sib_meta = lax.optimization_barrier(
+        (mirror_block, bands_of(beside_block), right, sib_meta)
+    )
     right_sib = move(right_sib, flip=True)
     mirror_bands = bands_of(mirror_block)
     blocks = [(own_block, own_bands), (beside_block, beside_bands), None, None]
@@ -185,6 +187,7 @@
     where_dst = jnp.stack([3 - partner, 3 - plane, partner, plane, band, core]).astype(jnp.int32)
 
     params = pltpu.CompilerParams(vmem_limit_bytes=VMEM)
+    last_cost = pl.CostEstimate(flops=60 * 10**9, bytes_accessed=7 * width * width * 2, transcendentals=0)
     cost = pl.CostEstimate(flops=3 * 10**9, bytes_accessed=7 * width * width * 2, transcendentals=0)
     depth = 8
     mixed = None
@@ -210,7 +213,7 @@
             ],
             input_output_aliases={} if mixed is None else {7: 0},
             compiler_params=params,
-            cost_estimate=cost,
+            cost_estimate=last_cost if phase == sectors - 1 else cost,
             name="left_mix",
         )(*operands)
 

time: 85 us -> 81.6 us (0.960)
  waiting for transfers between devices: 31.2 us -> 20.8 us
  starting transfers between devices: 28.5 us -> 31.9 us
  Pallas kernels: 18.1 us -> 21.4 us
    ppermute x19, waiting for transfers between devices: 31.2 us -> 20.8 us  [move(): return lax.ppermute(value, 'term', pairs)]
    pallas_call x4, Pallas kernels: 8.71 us -> 13.1 us  [local(): pl.pallas_call(functools.partial(left_kernel, phase), out_shape=jax.Shape...]
    ppermute x19, starting transfers between devices: 28.5 us -> 31.9 us  [move(): return lax.ppermute(value, 'term', pairs)]
    pallas_call x4, Pallas kernels: 9.39 us -> 8.26 us  [right_mix(): pl.pallas_call(functools.partial(right_kernel, phase), out_shape=(jax.Sha...]
    unnamed x6 -> x10, local copies, waits for them, and re-layouts: 2.5 us -> 2.51 us
  transfers between devices with their start and end apart: 19 -> 19, of which waited for: 11 -> 8; matrix products, arithmetic and copies ran while one was open for 1% -> 1% of each run, Pallas kernels for 19% -> 24%
where the time goes in v5:
time: 81.6 us; the launch traced here: 80.8 us
  starting transfers between devices  31.9 us (39%)
  Pallas kernels  21.4 us (26%)
  waiting for transfers between devices  20.8 us (25%)
  local copies, waits for them, and re-layouts  3.68 us (5%)
  other arithmetic  2.07 us (3%)
  between operations  0.88 us (1%)
    ppermute x19, starting transfers between devices, move(): return lax.ppermute(value, 'term', pairs)  31.9 us
    ppermute x19, waiting for transfers between devices, move(): return lax.ppermute(value, 'term', pairs)  20.8 us
    pallas_call x4, Pallas kernels, local(): pl.pallas_call(functools.partial(left_kernel, phase), out_shape=jax.Shape...  13.1 us
    pallas_call x4, Pallas kernels, right_mix(): pl.pallas_call(functools.partial(right_kernel, phase), out_shape=(jax.Sha...  8.26 us
    unnamed x10, local copies, waits for them, and re-layouts  2.51 us
  transfers between devices with their start and end apart: 19, of which 8 were waited for; matrix products, arithmetic and copies ran while one was open for 1% of the time, Pallas kernels for 24%

profile of v5, /device:TPU:13, one launch (start us, length us, event | category | flops | bytes accessed | tf_op | source)
XLA Modules:
  0.0 80.8 jit_solution(13781682576191720393)
XLA Ops:
  0.0 1.0 %dynamic-slice_bitcast_fusion = (bf16[1,128,512]{2,1,0:T(8,128)(2,1)S(1)}, bf16[128,512]{1,0:T(8,128)(2,1)S(1)}) fusion(bf16[128,1024]{1,0:T(8,128)(2,1)} %param.6, s32[]{:T(128)S(6)} %select_n.38, s32[]{:T(128)S(6)} %select_n.39), kind=kLoop, calls=%fused_computation.10 | loop fusion | bytes 524296 | tf_op jit(solution)/shard_map/stack | solution.py:175
  1.0 0.7 collective-permute-start
  1.7 1.0 %collective-permute-done = bf16[128,512]{1,0:T(8,128)(2,1)S(1)} collective-permute-done((bf16[128,512]{1,0:T(8,128)(2,1)S(1)}, bf16[128,512]{1,0:T(8,128)(2,1)S(1)}, u32[]{:S(2)}, u32[]{:S(2)}) %collective-permute-start) | collective-permute-done | bytes 131104 | tf_op jit(solution)/shard_map/ppermute | solution.py:157
  2.7 0.4 collective-permute-start.8
  3.1 1.3 %collective-permute-start.3 = (bf16[2,128,512]{2,1,0:T(8,128)(2,1)S(1)}, bf16[2,128,512]{2,1,0:T(8,128)(2,1)S(1)}, u32[]{:S(2)}, u32[]{:S(2)}) collective-permute-start(bf16[2,128,512]{2,1,0:T(8,128)(2,1)S(1)} %pad_maximum_fusion.1.refs_3_), channel_id=1, source_target_pairs={{0,2},{1,3},{2,0},{3,1},{4,6},{5,7},{6,4},{7,5},{8,10},{9,11},{10,... | collective-permute-start | bytes 786440 | tf_op jit(solution)/shard_map/ppermute | solution.py:157
  4.4 0.2 collective-permute-start.2
  4.6 2.4 %collective-permute-start.1 = (bf16[2,128,512]{2,1,0:T(8,128)(2,1)S(1)}, bf16[2,128,512]{2,1,0:T(8,128)(2,1)S(1)}, u32[]{:S(2)}, u32[]{:S(2)}) collective-permute-start(bf16[2,128,512]{2,1,0:T(8,128)(2,1)S(1)} %pad_maximum_fusion.1.refs_3_), channel_id=1, source_target_pairs={{0,12},{1,13},{2,14},{3,15},{4,8},{5,9},{6,10},{7,11},{8,4},{9,5},... | collective-permute-start | bytes 786440 | tf_op jit(solution)/shard_map/ppermute | solution.py:157
  7.0 4.0 %collective-permute-done.3 = bf16[2,128,512]{2,1,0:T(8,128)(2,1)S(1)} collective-permute-done((bf16[2,128,512]{2,1,0:T(8,128)(2,1)S(1)}, bf16[2,128,512]{2,1,0:T(8,128)(2,1)S(1)}, u32[]{:S(2)}, u32[]{:S(2)}) %collective-permute-start.3) | collective-permute-done | bytes 262176 | tf_op jit(solution)/shard_map/ppermute | solution.py:157
  10.9 0.9 %collective-permute-done.2.refs_3_ = bf16[2,128,512]{2,1,0:T(8,128)(2,1)S(1)} collective-permute-done((bf16[2,128,512]{2,1,0:T(8,128)(2,1)S(1)}, bf16[2,128,512]{2,1,0:T(8,128)(2,1)S(1)}, u32[]{:S(2)}, u32[]{:S(2)}) %collective-permute-start.2) | collective-permute-done | bytes 262176 | tf_op jit(solution)/shard_map/ppermute | solution.py:157
  11.8 0.3 collective-permute-start.4
  12.8 0.7 pad_add_fusion.refs_0_
  13.5 2.4 %collective-permute-start.5 = (s32[21]{0:T(128)S(1)}, s32[21]{0:T(128)S(1)}, u32[]{:S(2)}, u32[]{:S(2)}) collective-permute-start(s32[21]{0:T(128)S(1)} %pad_add_fusion.refs_0_), channel_id=1, source_target_pairs={{0,1},{1,0},{2,3},{3,2},{4,5},{5,4},{6,7},{7,6},{8,9},{9,8},{10,11... | collective-permute-start | bytes 260 | tf_op jit(solution)/shard_map/ppermute | solution.py:157
  15.9 0.1 stack.63.refs_2_
  16.0 0.1 stack.62.refs_2_
  16.1 0.0 collective-permute-done.1.refs_3_
  16.1 3.6 %collective-permute-start.6 = (bf16[2,128,512]{2,1,0:T(8,128)(2,1)S(1)}, bf16[2,128,512]{2,1,0:T(8,128)(2,1)S(1)}, u32[]{:S(2)}, u32[]{:S(2)}) collective-permute-start(bf16[2,128,512]{2,1,0:T(8,128)(2,1)S(1)} %collective-permute-done.1.refs_3_), channel_id=1, source_target_pairs={{0,4},{1,5},{2,6},{3,7},{4,0},{5,1},{6,2},{7,3},{8,12},{9,13},{10,... | collective-permute-start | bytes 786440 | tf_op jit(solution)/shard_map/ppermute | solution.py:157
  19.7 0.0 collective-permute-done.5.refs_1_
  19.7 0.0 collective-permute-done.4
  19.7 0.3 collective-permute-start.7
  19.9 1.9 %collective-permute-start.10 = (bf16[10,512,512]{2,1,0:T(8,128)(2,1)}, bf16[10,512,512]{2,1,0:T(8,128)(2,1)S(1)}, u32[]{:S(2)}, u32[]{:S(2)}) collective-permute-start(bf16[10,512,512]{2,1,0:T(8,128)(2,1)} %refs_4_.7), channel_id=1, source_target_pairs={{0,1},{1,0},{2,3},{3,2},{4,5},{5,4},{6,7},{7,6},{8,9},{9,8},{10,11... | collective-permute-start | bytes 15728648 | tf_op jit(solution)/shard_map/ppermute | solution.py:157
  21.8 0.0 collective-permute-done.8.refs_6_
  21.9 2.5 %copy-done = bf16[10,512,512]{2,1,0:T(8,128)(2,1)S(1)} copy-done((bf16[10,512,512]{2,1,0:T(8,128)(2,1)S(1)}, bf16[10,512,512]{2,1,0:T(8,128)(2,1)}, u32[]{:S(2)}) %copy-start) | copy-done | bytes 5242904
  24.3 2.3 %left_mix.4.refs_7_ = bf16[20,512,512]{2,1,0:T(8,128)(2,1)S(1)} custom-call(s32[21]{0:T(128)S(1)} %pad_add_fusion.refs_0_, s32[21]{0:T(128)S(1)} %collective-permute-done.5.refs_1_, s32[6]{0:T(128)S(1)} %stack.63.refs_2_, bf16[2,128,512]{2,1,0:T(8,128)(2,1)S(1)} %pad_maximum_fusion.1.refs_3_, bf16[1,2,128,512]{3,2,1,0:T(8,128)(2,1)S(1)} %bitcast.29, ...), custom_call_target="tpu_custom_call" | custom-call | flops 3000000000 | bytes 3670016 | tf_op jit(solution)/shard_map/left_mix/pallas_call | solution.py:201
  26.6 0.0 collective-permute-done.6.refs_3_
  26.6 0.0 collective-permute-done.7
  26.7 0.0 slice-start.2
  26.7 0.0 slice-start.3
  26.7 0.3 collective-permute-start.9
  27.0 3.4 %left_mix.5.refs_7_ = bf16[20,512,512]{2,1,0:T(8,128)(2,1)S(1)} custom-call(s32[21]{0:T(128)S(1)} %pad_add_fusion.refs_0_, s32[21]{0:T(128)S(1)} %collective-permute-done.5.refs_1_, s32[6]{0:T(128)S(1)} %stack.63.refs_2_, bf16[2,128,512]{2,1,0:T(8,128)(2,1)S(1)} %collective-permute-done.2.refs_3_, ...), custom_call_target="tpu_custom_call", output_to_operand_aliasing={{}: (7, {})} | custom-call | flops 3000000000 | bytes 3670016 | tf_op jit(solution)/shard_map/left_mix/pallas_call | solution.py:201
  30.4 0.0 slice-done.2
  30.4 0.0 slice-done.3
  30.4 0.0 slice-start
  30.5 3.2 %left_mix.6.refs_7_ = bf16[20,512,512]{2,1,0:T(8,128)(2,1)S(1)} custom-call(s32[21]{0:T(128)S(1)} %pad_add_fusion.refs_0_, s32[21]{0:T(128)S(1)} %collective-permute-done.5.refs_1_, s32[6]{0:T(128)S(1)} %stack.63.refs_2_, bf16[2,128,512]{2,1,0:T(8,128)(2,1)S(1)} %collective-permute-done.1.refs_3_, ...), custom_call_target="tpu_custom_call", output_to_operand_aliasing={{}: (7, {})} | custom-call | flops 3000000000 | bytes 3670016 | tf_op jit(solution)/shard_map/left_mix/pallas_call | solution.py:201
  33.6 0.0 collective-permute-done.9
  33.6 0.0 slice-start.1
  33.6 4.3 %left_mix.7.refs_3_ = bf16[20,512,512]{2,1,0:T(8,128)(2,1)S(1)} custom-call(s32[21]{0:T(128)S(1)} %pad_add_fusion.refs_0_, s32[21]{0:T(128)S(1)} %collective-permute-done.5.refs_1_, s32[6]{0:T(128)S(1)} %stack.63.refs_2_, bf16[2,128,512]{2,1,0:T(8,128)(2,1)S(1)} %collective-permute-done.6.refs_3_, ...), custom_call_target="tpu_custom_call", output_to_operand_aliasing={{}: (7, {})} | custom-call | flops 60000002048 | bytes 3670016 | tf_op jit(solution)/shard_map/left_mix/pallas_call | solution.py:201
  37.9 0.0 collective-permute-done.10.refs_5_
  37.9 0.0 slice-done
  38.0 0.0 slice-done.1
  38.0 2.3 %right_mix.4 = (f32[2,128,512]{2,1,0:T(8,128)S(1)}, bf16[1,2,128,512]{3,2,1,0:T(8,128)(2,1)S(1)}) custom-call(s32[21]{0:T(128)S(1)} %pad_add_fusion.refs_0_, s32[21]{0:T(128)S(1)} %collective-permute-done.5.refs_1_, s32[6]{0:T(128)S(1)} %stack.62.refs_2_, bf16[20,512,512]{2,1,0:T(8,128)(2,1)S(1)} %left_mix.7.refs_3_, bf16[10,512,512]{2,1,0:T(8,128)(2,1)S(1)} %bitcast.26, ...), custom_call_target="tpu_custom_call" | custom-call | flops 3000000000 | bytes 3670016 | tf_op jit(solution)/shard_map/right_mix/pallas_call | solution.py:221
  40.3 0.8 %collective-permute-start.11 = (bf16[2,128,512]{2,1,0:T(8,128)(2,1)S(1)}, bf16[2,128,512]{2,1,0:T(8,128)(2,1)S(1)}, u32[]{:S(2)}, u32[]{:S(2)}) collective-permute-start(bf16[2,128,512]{2,1,0:T(8,128)(2,1)S(1)} %bitcast.36), channel_id=1, source_target_pairs={{0,2},{1,3},{2,0},{3,1},{4,6},{5,7},{6,4},{7,5},{8,10},{9,11},{10,... | collective-permute-start | bytes 786440 | tf_op jit(solution)/shard_map/ppermute | solution.py:157
  41.2 2.3 %right_mix.6 = (f32[2,128,512]{2,1,0:T(8,128)S(1)}, bf16[1,2,128,512]{3,2,1,0:T(8,128)(2,1)S(1)}) custom-call(s32[21]{0:T(128)S(1)} %pad_add_fusion.refs_0_, s32[21]{0:T(128)S(1)} %collective-permute-done.5.refs_1_, s32[6]{0:T(128)S(1)} %stack.62.refs_2_, bf16[20,512,512]{2,1,0:T(8,128)(2,1)S(1)} %left_mix.7.refs_3_, bf16[10,512,512]{2,1,0:T(8,128)(2,1)S(1)} %bitcast.26, ...), custom_call_target="tpu_custom_call" | custom-call | flops 3000000000 | bytes 3670016 | tf_op jit(solution)/shard_map/right_mix/pallas_call | solution.py:221
  43.5 0.2 collective-permute-start.13
  43.7 3.5 %collective-permute-done.11 = bf16[2,128,512]{2,1,0:T(8,128)(2,1)S(1)} collective-permute-done((bf16[2,128,512]{2,1,0:T(8,128)(2,1)S(1)}, bf16[2,128,512]{2,1,0:T(8,128)(2,1)S(1)}, u32[]{:S(2)}, u32[]{:S(2)}) %collective-permute-start.11) | collective-permute-done | bytes 262176 | tf_op jit(solution)/shard_map/ppermute | solution.py:157
  47.3 0.1 add_convert_fusion.2
  47.3 4.4 %collective-permute-start.14 = (bf16[2,128,512]{2,1,0:T(8,128)(2,1)S(1)}, bf16[2,128,512]{2,1,0:T(8,128)(2,1)S(1)}, u32[]{:S(2)}, u32[]{:S(2)}) collective-permute-start(bf16[2,128,512]{2,1,0:T(8,128)(2,1)S(1)} %add_convert_fusion.2), channel_id=1, source_target_pairs={{0,4},{1,5},{2,6},{3,7},{4,0},{5,1},{6,2},{7,3},{8,12},{9,13},{10,... | collective-permute-start | bytes 786440 | tf_op jit(solution)/shard_map/ppermute | solution.py:157
  51.8 1.8 %right_mix.7 = (f32[2,128,512]{2,1,0:T(8,128)S(1)}, bf16[1,2,128,512]{3,2,1,0:T(8,128)(2,1)S(1)}) custom-call(s32[21]{0:T(128)S(1)} %pad_add_fusion.refs_0_, s32[21]{0:T(128)S(1)} %collective-permute-done.5.refs_1_, s32[6]{0:T(128)S(1)} %stack.62.refs_2_, bf16[20,512,512]{2,1,0:T(8,128)(2,1)S(1)} %left_mix.7.refs_3_, bf16[10,512,512]{2,1,0:T(8,128)(2,1)S(1)} %bitcast.26, ...), custom_call_target="tpu_custom_call" | custom-call | flops 3000000000 | bytes 3670016 | tf_op jit(solution)/shard_map/right_mix/pallas_call | solution.py:221
  53.6 4.0 %collective-permute-start.16 = (bf16[2,128,512]{2,1,0:T(8,128)(2,1)S(1)}, bf16[2,128,512]{2,1,0:T(8,128)(2,1)S(1)}, u32[]{:S(2)}, u32[]{:S(2)}) collective-permute-start(bf16[2,128,512]{2,1,0:T(8,128)(2,1)S(1)} %bitcast.34), channel_id=1, source_target_pairs={{0,2},{1,3},{2,0},{3,1},{4,6},{5,7},{6,4},{7,5},{8,10},{9,11},{10,... | collective-permute-start | bytes 786440 | tf_op jit(solution)/shard_map/ppermute | solution.py:157
  57.6 1.8 %right_mix.5 = (f32[2,128,512]{2,1,0:T(8,128)S(1)}, bf16[1,2,128,512]{3,2,1,0:T(8,128)(2,1)S(1)}) custom-call(s32[21]{0:T(128)S(1)} %pad_add_fusion.refs_0_, s32[21]{0:T(128)S(1)} %collective-permute-done.5.refs_1_, s32[6]{0:T(128)S(1)} %stack.62.refs_2_, bf16[20,512,512]{2,1,0:T(8,128)(2,1)S(1)} %left_mix.7.refs_3_, bf16[10,512,512]{2,1,0:T(8,128)(2,1)S(1)} %bitcast.26, ...), custom_call_target="tpu_custom_call" | custom-call | flops 3000000000 | bytes 3670016 | tf_op jit(solution)/shard_map/right_mix/pallas_call | solution.py:221
  59.3 0.6 collective-permute-start.12
  60.0 0.0 collective-permute-done.13
  60.0 0.0 collective-permute-done.14
  60.0 0.1 add_convert_fusion.1
  60.1 3.4 %collective-permute-start.15 = (bf16[2,128,512]{2,1,0:T(8,128)(2,1)S(1)}, bf16[2,128,512]{2,1,0:T(8,128)(2,1)S(1)}, u32[]{:S(2)}, u32[]{:S(2)}) collective-permute-start(bf16[2,128,512]{2,1,0:T(8,128)(2,1)S(1)} %add_convert_fusion.1), channel_id=1, source_target_pairs={{0,12},{1,13},{2,14},{3,15},{4,8},{5,9},{6,10},{7,11},{8,4},{9,5},... | collective-permute-start | bytes 786440 | tf_op jit(solution)/shard_map/ppermute | solution.py:157
  63.5 0.0 collective-permute-done.16
  63.5 0.1 add_convert_fusion
  63.6 2.1 %collective-permute-start.17 = (bf16[2,128,512]{2,1,0:T(8,128)(2,1)S(1)}, bf16[2,128,512]{2,1,0:T(8,128)(2,1)S(1)}, u32[]{:S(2)}, u32[]{:S(2)}) collective-permute-start(bf16[2,128,512]{2,1,0:T(8,128)(2,1)S(1)} %add_convert_fusion), channel_id=1, source_target_pairs={{0,4},{1,5},{2,6},{3,7},{4,0},{5,1},{6,2},{7,3},{8,12},{9,13},{10,... | collective-permute-start | bytes 786440 | tf_op jit(solution)/shard_map/ppermute | solution.py:157
  65.7 2.1 %collective-permute-done.12 = bf16[2,128,512]{2,1,0:T(8,128)(2,1)S(1)} collective-permute-done((bf16[2,128,512]{2,1,0:T(8,128)(2,1)S(1)}, bf16[2,128,512]{2,1,0:T(8,128)(2,1)S(1)}, u32[]{:S(2)}, u32[]{:S(2)}) %collective-permute-start.12) | collective-permute-done | bytes 262176 | tf_op jit(solution)/shard_map/ppermute | solution.py:157
  67.8 7.2 %collective-permute-done.15 = bf16[2,128,512]{2,1,0:T(8,128)(2,1)S(1)} collective-permute-done((bf16[2,128,512]{2,1,0:T(8,128)(2,1)S(1)}, bf16[2,128,512]{2,1,0:T(8,128)(2,1)S(1)}, u32[]{:S(2)}, u32[]{:S(2)}) %collective-permute-start.15) | collective-permute-done | bytes 262176 | tf_op jit(solution)/shard_map/ppermute | solution.py:157
  75.0 1.0 %collective-permute-done.17 = bf16[2,128,512]{2,1,0:T(8,128)(2,1)S(1)} collective-permute-done((bf16[2,128,512]{2,1,0:T(8,128)(2,1)S(1)}, bf16[2,128,512]{2,1,0:T(8,128)(2,1)S(1)}, u32[]{:S(2)}, u32[]{:S(2)}) %collective-permute-start.17) | collective-permute-done | bytes 262176 | tf_op jit(solution)/shard_map/ppermute | solution.py:157
  76.0 0.2 convert_add_fusion
  76.2 2.6 %collective-permute-start.18 = (f32[128,512]{1,0:T(8,128)S(1)}, f32[128,512]{1,0:T(8,128)S(1)}, u32[]{:S(2)}, u32[]{:S(2)}) collective-permute-start(f32[128,512]{1,0:T(8,128)S(1)} %slice_bitcast_fusion), channel_id=1, source_target_pairs={{0,1},{1,0},{2,3},{3,2},{4,5},{5,4},{6,7},{7,6},{8,9},{9,8},{10,11... | collective-permute-start | bytes 786440 | tf_op jit(solution)/shard_map/ppermute | solution.py:157
  78.8 1.2 %collective-permute-done.18 = f32[128,512]{1,0:T(8,128)S(1)} collective-permute-done((f32[128,512]{1,0:T(8,128)S(1)}, f32[128,512]{1,0:T(8,128)S(1)}, u32[]{:S(2)}, u32[]{:S(2)}) %collective-permute-start.18) | collective-permute-done | bytes 262176 | tf_op jit(solution)/shard_map/ppermute | solution.py:157
  80.0 0.8 %pad_maximum_fusion = f32[128,1024]{1,0:T(8,128)} fusion(f32[128,512]{1,0:T(8,128)S(1)} %get-tuple-element.48, f32[128,512]{1,0:T(8,128)S(1)} %get-tuple-element.47), kind=kLoop, calls=%fused_computation | loop fusion | flops 131072 | bytes 1048576 | tf_op jit(solution)/shard_map/concatenate | solution.py:253
  (6 shorter events, 0.1 us)
Async XLA Ops:
  1.0 1.7 %collective-permute-start = (bf16[128,512]{1,0:T(8,128)(2,1)S(1)}, bf16[128,512]{1,0:T(8,128)(2,1)S(1)}, u32[]{:S(2)}, u32[]{:S(2)}) collective-permute-start(bf16[128,512]{1,0:T(8,128)(2,1)S(1)} %get-tuple-element.50), channel_id=1, source_target_pairs={{0,1},{1,0},{2,3},{3,2},{4,5},{5,4},{6,7},{7,6},{8,9},{9,8},{10,11... | collective-permute-start | bytes 393224 | tf_op jit(solution)/shard_map/ppermute | solution.py:157
  2.7 19.1 %collective-permute-start.8 = (bf16[10,512,512]{2,1,0:T(8,128)(2,1)}, bf16[10,512,512]{2,1,0:T(8,128)(2,1)}, u32[]{:S(2)}, u32[]{:S(2)}) collective-permute-start(bf16[10,512,512]{2,1,0:T(8,128)(2,1)} %refs_5_.7), channel_id=1, source_target_pairs={{0,1},{1,0},{2,3},{3,2},{4,5},{5,4},{6,7},{7,6},{8,9},{9,8},{10,11... | collective-permute-start | bytes 15728648 | tf_op jit(solution)/shard_map/ppermute | solution.py:157
  3.1 7.8 %collective-permute-start.3 = (bf16[2,128,512]{2,1,0:T(8,128)(2,1)S(1)}, bf16[2,128,512]{2,1,0:T(8,128)(2,1)S(1)}, u32[]{:S(2)}, u32[]{:S(2)}) collective-permute-start(bf16[2,128,512]{2,1,0:T(8,128)(2,1)S(1)} %pad_maximum_fusion.1.refs_3_), channel_id=1, source_target_pairs={{0,2},{1,3},{2,0},{3,1},{4,6},{5,7},{6,4},{7,5},{8,10},{9,11},{10,... | collective-permute-start | bytes 786440 | tf_op jit(solution)/shard_map/ppermute | solution.py:157
  4.4 7.4 %collective-permute-start.2 = (bf16[2,128,512]{2,1,0:T(8,128)(2,1)S(1)}, bf16[2,128,512]{2,1,0:T(8,128)(2,1)S(1)}, u32[]{:S(2)}, u32[]{:S(2)}) collective-permute-start(bf16[2,128,512]{2,1,0:T(8,128)(2,1)S(1)} %pad_maximum_fusion.1.refs_3_), channel_id=1, source_target_pairs={{0,4},{1,5},{2,6},{3,7},{4,0},{5,1},{6,2},{7,3},{8,12},{9,13},{10,... | collective-permute-start | bytes 786440 | tf_op jit(solution)/shard_map/ppermute | solution.py:157
  4.6 11.5 %collective-permute-start.1 = (bf16[2,128,512]{2,1,0:T(8,128)(2,1)S(1)}, bf16[2,128,512]{2,1,0:T(8,128)(2,1)S(1)}, u32[]{:S(2)}, u32[]{:S(2)}) collective-permute-start(bf16[2,128,512]{2,1,0:T(8,128)(2,1)S(1)} %pad_maximum_fusion.1.refs_3_), channel_id=1, source_target_pairs={{0,12},{1,13},{2,14},{3,15},{4,8},{5,9},{6,10},{7,11},{8,4},{9,5},... | collective-permute-start | bytes 786440 | tf_op jit(solution)/shard_map/ppermute | solution.py:157
  11.8 7.9 %collective-permute-start.4 = (bf16[2,128,512]{2,1,0:T(8,128)(2,1)S(1)}, bf16[2,128,512]{2,1,0:T(8,128)(2,1)S(1)}, u32[]{:S(2)}, u32[]{:S(2)}) collective-permute-start(bf16[2,128,512]{2,1,0:T(8,128)(2,1)S(1)} %collective-permute-done.2.refs_3_), channel_id=1, source_target_pairs={{0,2},{1,3},{2,0},{3,1},{4,6},{5,7},{6,4},{7,5},{8,10},{9,11},{10,... | collective-permute-start | bytes 786440 | tf_op jit(solution)/shard_map/ppermute | solution.py:157
  13.5 6.1 %collective-permute-start.5 = (s32[21]{0:T(128)S(1)}, s32[21]{0:T(128)S(1)}, u32[]{:S(2)}, u32[]{:S(2)}) collective-permute-start(s32[21]{0:T(128)S(1)} %pad_add_fusion.refs_0_), channel_id=1, source_target_pairs={{0,1},{1,0},{2,3},{3,2},{4,5},{5,4},{6,7},{7,6},{8,9},{9,8},{10,11... | collective-permute-start | bytes 260 | tf_op jit(solution)/shard_map/ppermute | solution.py:157
  16.1 10.5 %collective-permute-start.6 = (bf16[2,128,512]{2,1,0:T(8,128)(2,1)S(1)}, bf16[2,128,512]{2,1,0:T(8,128)(2,1)S(1)}, u32[]{:S(2)}, u32[]{:S(2)}) collective-permute-start(bf16[2,128,512]{2,1,0:T(8,128)(2,1)S(1)} %collective-permute-done.1.refs_3_), channel_id=1, source_target_pairs={{0,4},{1,5},{2,6},{3,7},{4,0},{5,1},{6,2},{7,3},{8,12},{9,13},{10,... | collective-permute-start | bytes 786440 | tf_op jit(solution)/shard_map/ppermute | solution.py:157
  19.7 7.0 %collective-permute-start.7 = (bf16[2,128,512]{2,1,0:T(8,128)(2,1)S(1)}, bf16[2,128,512]{2,1,0:T(8,128)(2,1)S(1)}, u32[]{:S(2)}, u32[]{:S(2)}) collective-permute-start(bf16[2,128,512]{2,1,0:T(8,128)(2,1)S(1)} %collective-permute-done.1.refs_3_), channel_id=1, source_target_pairs={{0,2},{1,3},{2,0},{3,1},{4,6},{5,7},{6,4},{7,5},{8,10},{9,11},{10,... | collective-permute-start | bytes 786440 | tf_op jit(solution)/shard_map/ppermute | solution.py:157
  19.9 18.0 %collective-permute-start.10 = (bf16[10,512,512]{2,1,0:T(8,128)(2,1)}, bf16[10,512,512]{2,1,0:T(8,128)(2,1)S(1)}, u32[]{:S(2)}, u32[]{:S(2)}) collective-permute-start(bf16[10,512,512]{2,1,0:T(8,128)(2,1)} %refs_4_.7), channel_id=1, source_target_pairs={{0,1},{1,0},{2,3},{3,2},{4,5},{5,4},{6,7},{7,6},{8,9},{9,8},{10,11... | collective-permute-start | bytes 15728648 | tf_op jit(solution)/shard_map/ppermute | solution.py:157
  21.9 2.5 %copy-start = (bf16[10,512,512]{2,1,0:T(8,128)(2,1)S(1)}, bf16[10,512,512]{2,1,0:T(8,128)(2,1)}, u32[]{:S(2)}) copy-start(bf16[10,512,512]{2,1,0:T(8,128)(2,1)} %refs_5_.7) | copy-start | bytes 15728644
  26.7 3.8 %slice-start.2 = ((s8[5242880]{0:T(1024)(128)(4,1)}), s8[4194304]{0:T(1024)(128)(4,1)S(1)}, s32[]{:S(2)}) async-start(s8[5242880]{0:T(1024)(128)(4,1)} %bitcast.27), calls=%async_computation.2 | async-start | bytes 8388608
  26.7 3.8 %slice-start.3 = ((s8[5242880]{0:T(1024)(128)(4,1)}), s8[1048576]{0:T(1024)(128)(4,1)S(1)}, s32[]{:S(2)}) async-start(s8[5242880]{0:T(1024)(128)(4,1)} %bitcast.27), calls=%async_computation.3 | async-start | bytes 2097152
  26.7 6.9 %collective-permute-start.9 = (bf16[2,128,512]{2,1,0:T(8,128)(2,1)S(1)}, bf16[2,128,512]{2,1,0:T(8,128)(2,1)S(1)}, u32[]{:S(2)}, u32[]{:S(2)}) collective-permute-start(bf16[2,128,512]{2,1,0:T(8,128)(2,1)S(1)} %collective-permute-done.6.refs_3_), channel_id=1, source_target_pairs={{0,2},{1,3},{2,0},{3,1},{4,6},{5,7},{6,4},{7,5},{8,10},{9,11},{10,... | collective-permute-start | bytes 786440 | tf_op jit(solution)/shard_map/ppermute | solution.py:157
  30.4 7.5 %slice-start = ((s8[5242880]{0:T(1024)(128)(4,1)}), s8[4194304]{0:T(1024)(128)(4,1)S(1)}, s32[]{:S(2)}) async-start(s8[5242880]{0:T(1024)(128)(4,1)} %bitcast.25), calls=%async_computation | async-start | bytes 8388608
  33.6 4.3 %slice-start.1 = ((s8[5242880]{0:T(1024)(128)(4,1)}), s8[1048576]{0:T(1024)(128)(4,1)S(1)}, s32[]{:S(2)}) async-start(s8[5242880]{0:T(1024)(128)(4,1)} %bitcast.25), calls=%async_computation.1 | async-start | bytes 2097152
  40.3 6.9 %collective-permute-start.11 = (bf16[2,128,512]{2,1,0:T(8,128)(2,1)S(1)}, bf16[2,128,512]{2,1,0:T(8,128)(2,1)S(1)}, u32[]{:S(2)}, u32[]{:S(2)}) collective-permute-start(bf16[2,128,512]{2,1,0:T(8,128)(2,1)S(1)} %bitcast.36), channel_id=1, source_target_pairs={{0,2},{1,3},{2,0},{3,1},{4,6},{5,7},{6,4},{7,5},{8,10},{9,11},{10,... | collective-permute-start | bytes 786440 | tf_op jit(solution)/shard_map/ppermute | solution.py:157
  43.5 16.5 %collective-permute-start.13 = (bf16[2,128,512]{2,1,0:T(8,128)(2,1)S(1)}, bf16[2,128,512]{2,1,0:T(8,128)(2,1)S(1)}, u32[]{:S(2)}, u32[]{:S(2)}) collective-permute-start(bf16[2,128,512]{2,1,0:T(8,128)(2,1)S(1)} %bitcast.33), channel_id=1, source_target_pairs={{0,2},{1,3},{2,0},{3,1},{4,6},{5,7},{6,4},{7,5},{8,10},{9,11},{10,... | collective-permute-start | bytes 786440 | tf_op jit(solution)/shard_map/ppermute | solution.py:157
  47.3 12.6 %collective-permute-start.14 = (bf16[2,128,512]{2,1,0:T(8,128)(2,1)S(1)}, bf16[2,128,512]{2,1,0:T(8,128)(2,1)S(1)}, u32[]{:S(2)}, u32[]{:S(2)}) collective-permute-start(bf16[2,128,512]{2,1,0:T(8,128)(2,1)S(1)} %add_convert_fusion.2), channel_id=1, source_target_pairs={{0,4},{1,5},{2,6},{3,7},{4,0},{5,1},{6,2},{7,3},{8,12},{9,13},{10,... | collective-permute-start | bytes 786440 | tf_op jit(solution)/shard_map/ppermute | solution.py:157
  53.6 10.0 %collective-permute-start.16 = (bf16[2,128,512]{2,1,0:T(8,128)(2,1)S(1)}, bf16[2,128,512]{2,1,0:T(8,128)(2,1)S(1)}, u32[]{:S(2)}, u32[]{:S(2)}) collective-permute-start(bf16[2,128,512]{2,1,0:T(8,128)(2,1)S(1)} %bitcast.34), channel_id=1, source_target_pairs={{0,2},{1,3},{2,0},{3,1},{4,6},{5,7},{6,4},{7,5},{8,10},{9,11},{10,... | collective-permute-start | bytes 786440 | tf_op jit(solution)/shard_map/ppermute | solution.py:157
  59.3 8.5 %collective-permute-start.12 = (bf16[2,128,512]{2,1,0:T(8,128)(2,1)S(1)}, bf16[2,128,512]{2,1,0:T(8,128)(2,1)S(1)}, u32[]{:S(2)}, u32[]{:S(2)}) collective-permute-start(bf16[2,128,512]{2,1,0:T(8,128)(2,1)S(1)} %bitcast.32), channel_id=1, source_target_pairs={{0,2},{1,3},{2,0},{3,1},{4,6},{5,7},{6,4},{7,5},{8,10},{9,11},{10,... | collective-permute-start | bytes 786440 | tf_op jit(solution)/shard_map/ppermute | solution.py:157
  60.1 14.9 %collective-permute-start.15 = (bf16[2,128,512]{2,1,0:T(8,128)(2,1)S(1)}, bf16[2,128,512]{2,1,0:T(8,128)(2,1)S(1)}, u32[]{:S(2)}, u32[]{:S(2)}) collective-permute-start(bf16[2,128,512]{2,1,0:T(8,128)(2,1)S(1)} %add_convert_fusion.1), channel_id=1, source_target_pairs={{0,12},{1,13},{2,14},{3,15},{4,8},{5,9},{6,10},{7,11},{8,4},{9,5},... | collective-permute-start | bytes 786440 | tf_op jit(solution)/shard_map/ppermute | solution.py:157
  63.6 12.4 %collective-permute-start.17 = (bf16[2,128,512]{2,1,0:T(8,128)(2,1)S(1)}, bf16[2,128,512]{2,1,0:T(8,128)(2,1)S(1)}, u32[]{:S(2)}, u32[]{:S(2)}) collective-permute-start(bf16[2,128,512]{2,1,0:T(8,128)(2,1)S(1)} %add_convert_fusion), channel_id=1, source_target_pairs={{0,4},{1,5},{2,6},{3,7},{4,0},{5,1},{6,2},{7,3},{8,12},{9,13},{10,... | collective-permute-start | bytes 786440 | tf_op jit(solution)/shard_map/ppermute | solution.py:157
  76.2 3.7 %collective-permute-start.18 = (f32[128,512]{1,0:T(8,128)S(1)}, f32[128,512]{1,0:T(8,128)S(1)}, u32[]{:S(2)}, u32[]{:S(2)}) collective-permute-start(f32[128,512]{1,0:T(8,128)S(1)} %slice_bitcast_fusion), channel_id=1, source_target_pairs={{0,1},{1,0},{2,3},{3,2},{4,5},{5,4},{6,7},{7,6},{8,9},{9,8},{10,11... | collective-permute-start | bytes 786440 | tf_op jit(solution)/shard_map/ppermute | solution.py:157
